TPU v7x, 32 devices: a whole 2x2x4 slice. The times are simulated.
32 devices in a mesh: slab: 2 (over y), gy: 4 (over z), gx: 4 (over x, core).
Axes of the slice: x: 2, y: 2, z: 4, core: 2. Of those that a mesh axis runs over, the one named last changes fastest.
Arguments:
- volume: float32 [8, 256, 1024], P(None, ('slab', 'gy'), 'gx'), parts along dimension 1, may hold values from -8 to 8
- tissue_mask: int32 [2, 32, 128], P(None, ('slab', 'gy'), 'gx'), parts along dimension 1, may hold values from 0 to 1
- smoothing: float32 [1], replicated, may hold values from 0.7 to 1.4
Outputs:
- filtered: float32 [8, 256, 1024], P(None, ('slab', 'gy'), 'gx'), parts along dimension 1
There are 2 independent parts, one for each index of `slab`. A program takes and returns all parts, laid end to end along the dimension named above; an argument that names none is the same for every part. Nothing has to cross between parts.
All inputs are finite; a program needn't handle non-finite values.
Results may differ from a plain program's by a relative error of at most 0.00002.
Values sent between devices are 32-bit elements; how exact they have to be, the bound alone decides.
No kernel may reach another device: no remote copies, remote signals or barrier semaphores. Data moves between devices by JAX's collectives and lax.ppermute only.
A program may use at most 64 MiB of HBM per device.

v0:
```python
import jax
import jax.numpy as jnp
from jax import lax
from jax.sharding import PartitionSpec as P

OFFSETS = [(a, b, c) for a in (-4, 0, 4) for b in (-8, 0, 8) for c in (-8, 0, 8)]


def extended(block, sides, width):
    for axis, dim in sides:
        count = lax.axis_size(axis)
        forward = [(i, i + 1) for i in range(count - 1)]
        backward = [(target, source) for source, target in forward]
        low = lax.ppermute(
            lax.slice_in_dim(block, block.shape[dim] - width, None, axis=dim), axis, forward
        )
        high = lax.ppermute(lax.slice_in_dim(block, 0, width, axis=dim), axis, backward)
        block = jnp.concatenate([low, block, high], axis=dim)
    return block


def expand_mask(tissue_mask):
    blocks_z, blocks_y, blocks_x = tissue_mask.shape
    spread = jnp.broadcast_to(
        tissue_mask[:, None, :, None, :, None], (blocks_z, 4, blocks_y, 8, blocks_x, 8)
    )
    return spread.reshape(blocks_z * 4, blocks_y * 8, blocks_x * 8).astype(jnp.float32)


def noise_terms(values, tissue):
    residual = values[1:-1] - 0.5 * (values[:-2] + values[2:])
    inner = tissue[1:-1]
    summed = jnp.sum(inner * residual * residual) * (2.0 / 3.0)
    return (summed, jnp.sum(inner))


def box_sum(squared, depth, rows, cols):
    first = squared[0:depth] + squared[1 : depth + 1] + squared[2 : depth + 2]
    second = first[:, 0:rows] + first[:, 1 : rows + 1] + first[:, 2 : rows + 2]
    return second[:, :, 0:cols] + second[:, :, 1 : cols + 1] + second[:, :, 2 : cols + 2]


def smooth_once(padded_vals, padded_tiss, values, tissue, inverse_width):
    depth, rows, cols = values.shape
    centre = padded_vals[4 : depth + 6, 8 : rows + 10, 8 : cols + 10]
    numerator = jnp.zeros(values.shape, jnp.float32)
    denominator = jnp.zeros(values.shape, jnp.float32)
    for offset in OFFSETS:
        shift_z, shift_y, shift_x = offset
        moved = padded_vals[
            4 + shift_z : depth + 6 + shift_z,
            8 + shift_y : rows + 10 + shift_y,
            8 + shift_x : cols + 10 + shift_x,
        ]
        differ = centre - moved
        distance = box_sum(differ * differ, depth, rows, cols)
        other_tiss = padded_tiss[
            5 + shift_z : 5 + shift_z + depth,
            9 + shift_y : 9 + shift_y + rows,
            9 + shift_x : 9 + shift_x + cols,
        ]
        other_vals = padded_vals[
            5 + shift_z : 5 + shift_z + depth,
            9 + shift_y : 9 + shift_y + rows,
            9 + shift_x : 9 + shift_x + cols,
        ]
        weight_field = jnp.exp(-distance * inverse_width) * other_tiss
        numerator = numerator + weight_field * other_vals
        denominator = denominator + weight_field
    return tissue * numerator / (denominator + 1.0 - tissue) + (1.0 - tissue) * values


def widen_values(values):
    widened = extended(values, (("gy", 1), ("gx", 2)), 9)
    return jnp.pad(widened, ((5, 5), (0, 0), (0, 0)))


def on_device(volume, tissue_mask, smoothing):
    tissue = expand_mask(tissue_mask)
    local_sum, local_count = noise_terms(volume, tissue)
    summed, tissue_count = lax.psum((local_sum, local_count), ("gy", "gx"))
    variance = summed / jnp.maximum(tissue_count, 1.0) + 1e-05
    inverse_width = 1.0 / (54.0 * smoothing[0] * smoothing[0] * variance)
    stacked = jnp.stack([volume, tissue])
    widened = extended(stacked, (("gy", 2), ("gx", 3)), 9)
    widened = jnp.pad(widened, ((0, 0), (5, 5), (0, 0), (0, 0)))
    padded_tiss = widened[1]
    values = smooth_once(widened[0], padded_tiss, volume, tissue, inverse_width)
    padded_vals = widen_values(values)
    values = smooth_once(padded_vals, padded_tiss, values, tissue, inverse_width)
    return values


def solution(mesh):
    placed = (P(None, ("slab", "gy"), "gx"), P(None, ("slab", "gy"), "gx"), P())
    return jax.shard_map(
        on_device,
        mesh=mesh,
        in_specs=placed,
        out_specs=P(None, ("slab", "gy"), "gx"),
        check_vma=False,
    )
```

profile of v0, /device:TPU:0, one launch (start us, length us, event | category | flops | bytes accessed | tf_op | source)
XLA Modules:
  0.0 173.5 jit_solution(4089723964887068323)
XLA Ops:
  0.7 2.6 %broadcast_in_dim.2 = f32[2,4,4,8,32,8]{5,4,3,2,1,0:T(8,128)} broadcast(f32[2,4,32]{2,1,0:T(4,128)S(1)} %convert_element_type.22), dimensions={0,2,4} | broadcast | bytes 263168 | tf_op jit(solution)/shard_map/broadcast_in_dim | solution.py:24
  3.2 4.1 %convert_element_type.24 = f32[1,8,32,256]{3,2,1,0:T(8,128)S(1)} reshape(f32[2,4,4,8,32,8]{5,4,3,2,1,0:T(8,128)} %broadcast_in_dim.2) | data formatting | bytes 524288 | tf_op jit(solution)/shard_map/convert_element_type | solution.py:27
  7.4 4.9 %collective-permute-start = (f32[2,8,9,256]{3,2,1,0:T(8,128)S(1)}, f32[2,8,9,256]{3,2,1,0:T(8,128)S(1)}, u32[]{:S(2)}, u32[]{:S(2)}) collective-permute-start(f32[2,8,9,256]{3,2,1,0:T(8,128)S(1)} %get-tuple-element.69), channel_id=1, source_target_pairs={{0,4},{4,8},{8,12},{1,5},{5,9},{9,13},{2,6},{6,10},{10,14},{3,7},{... | collective-permute-start | bytes 442376 | tf_op jit(solution)/shard_map/ppermute | solution.py:14
  12.3 1.3 collective-permute-start.1
  13.6 4.0 %convert_element_type.23 = f32[8,32,256]{2,1,0:T(8,128)S(1)} reshape(f32[2,4,4,8,32,8]{5,4,3,2,1,0:T(8,128)} %broadcast_in_dim.2) | data formatting | bytes 524288 | tf_op jit(solution)/shard_map/convert_element_type | solution.py:27
  17.9 4.1 %collective-permute-done.1 = f32[2,8,9,256]{3,2,1,0:T(8,128)S(1)} collective-permute-done((f32[2,8,9,256]{3,2,1,0:T(8,128)S(1)}, f32[2,8,9,256]{3,2,1,0:T(8,128)S(1)}, u32[]{:S(2)}, u32[]{:S(2)}) %collective-permute-start.1) | collective-permute-done | bytes 147488 | tf_op jit(solution)/shard_map/ppermute | solution.py:17
  22.3 1.3 collective-permute-start.2
  23.6 1.3 collective-permute-start.3
  26.2 34.1 %all-reduce.2 = (f32[]{:T(128)}, f32[]{:T(128)}) all-reduce(f32[]{:T(128)S(6)} %mul.743, f32[]{:T(128)} %get-tuple-element.5), channel_id=1, replica_groups=mesh['slab'=2,'gy'=4,'gx'=4] {'gy','gx'}, use_global_device_ids=true, to_apply=%region_1.0 | all-reduce | flops 2 | bytes 16 | tf_op jit(solution)/shard_map/psum | solution.py:81
  62.4 1.4 select_maximum_fusion
  64.0 1.0 fusion.51
  65.1 1.2 fusion.53
  66.3 1.2 fusion.52
  68.4 0.8 slice_add_fusion.210
  69.3 0.8 slice_add_fusion.182
  70.2 0.9 slice_add_fusion.184
  71.9 0.9 slice_add_fusion.206
  72.9 0.8 slice_add_fusion.162
  74.6 0.8 slice_add_fusion.214
  75.5 0.8 slice_add_fusion.178
  78.1 0.8 slice_add_fusion.200
  79.1 0.8 slice_add_fusion.164
  79.9 0.9 slice_add_fusion.170
  80.9 0.9 slice_add_fusion.202
  81.7 0.9 slice_add_fusion.204
  82.7 0.8 slice_add_fusion.196
  83.5 0.9 slice_add_fusion.212
  84.5 0.8 slice_add_fusion.166
  85.3 0.8 slice_add_fusion.168
  86.3 0.9 slice_add_fusion.174
  88.0 0.8 slice_add_fusion.188
  90.6 0.8 slice_add_fusion.194
  91.5 18.5 %fusion.197 = f32[8,32,256]{2,1,0:T(8,128)} fusion(f32[8,32,256]{2,1,0:T(8,128)} %copy-done.2, f32[18,50,274]{2,1,0:T(8,128)S(1)} %get-tuple-element.10, f32[8,32,256]{2,1,0:T(8,128)S(1)} %copy-done, f32[8,32,258]{2,1,0:T(8,128)} %slice_add_fusion.162, f32[8,32,258]{2,1,0:T(8,128)} %slice_add_fusion.164, f32[8,32,258]{2,1,0:T(8,128)} %slice_add_fusion.166, ...), kind=kLoop, calls=%fused_computation.570 | loop fusion | flops 14483456 | bytes 36175876 | tf_op jit(solution)/shard_map/add | solution.py:70
  109.9 1.0 fusion.334
  111.0 1.3 collective-permute-start.4
  112.3 1.3 collective-permute-start.5
  113.6 1.2 collective-permute-done.4
  114.8 4.4 %collective-permute-done.5 = f32[8,9,256]{2,1,0:T(8,128)S(1)} collective-permute-done((f32[8,9,256]{2,1,0:T(8,128)S(1)}, f32[8,9,256]{2,1,0:T(8,128)S(1)}, u32[]{:S(2)}, u32[]{:S(2)}) %collective-permute-start.5) | collective-permute-done | bytes 73760 | tf_op jit(solution)/shard_map/ppermute | solution.py:17
  119.1 1.0 pad_maximum_fusion.2
  120.3 1.3 collective-permute-start.6
  121.6 1.6 collective-permute-start.7
  123.2 1.8 %collective-permute-done.7 = f32[8,50,9]{2,1,0:T(8,128)S(1)} collective-permute-done((f32[8,50,9]{2,1,0:T(8,128)S(1)}, f32[8,50,9]{2,1,0:T(8,128)S(1)}, u32[]{:S(2)}, u32[]{:S(2)}) %collective-permute-start.7) | collective-permute-done | bytes 14432 | tf_op jit(solution)/shard_map/ppermute | solution.py:17
  125.4 1.0 fusion.27
  126.4 1.2 fusion.26
  127.6 1.2 subtract_multiply_fusion
  130.6 0.8 slice_add_fusion.114
  131.5 0.9 slice_add_fusion.154
  132.4 0.8 slice_add_fusion.122
  133.2 0.8 slice_add_fusion.156
  134.1 0.8 slice_add_fusion.108
  135.0 0.8 slice_add_fusion.124
  136.8 0.9 slice_add_fusion.144
  138.5 0.9 slice_add_fusion.146
  140.3 0.8 slice_add_fusion.148
  142.1 0.8 slice_add_fusion.150
  144.7 0.9 slice_add_fusion.126
  145.6 0.8 slice_add_fusion.128
  146.5 0.8 slice_add_fusion.130
  147.4 0.8 slice_add_fusion.132
  148.3 0.8 slice_add_fusion.136
  150.9 0.9 slice_add_fusion.142
  151.8 0.9 slice_add_fusion.116
  152.7 1.4 maximum_maximum_fusion
  154.1 19.3 %fusion.58 = f32[8,32,256]{2,1,0:T(8,128)} fusion(f32[8,32,256]{2,1,0:T(8,128)} %copy-done.2, f32[18,50,274]{2,1,0:T(8,128)S(1)} %select_maximum_fusion.5, f32[8,50,265]{2,1,0:T(8,128)} %get-tuple-element.68, f32[8,9,256]{2,1,0:T(8,128)} %copy-done.3, f32[8,32,256]{2,1,0:T(8,128)S(1)} %copy-done.1, f32[8,50,265]{2,1,0:T(8,128)} %get-tuple-element.67, ...), kind=kLoop, calls=%fused_computation.351 | loop fusion | flops 14614528 | bytes 35536900 | tf_op jit(solution)/shard_map/add | solution.py:70
  (79 shorter events, 19.9 us)
Async XLA Ops:
  3.2 4.1 %copy-start = (f32[8,32,256]{2,1,0:T(8,128)S(1)}, f32[8,32,256]{2,1,0:T(8,128)}, u32[]{:S(2)}) copy-start(f32[8,32,256]{2,1,0:T(8,128)} %param.3) | copy-start | bytes 786436
  7.4 10.5 %collective-permute-start = (f32[2,8,9,256]{3,2,1,0:T(8,128)S(1)}, f32[2,8,9,256]{3,2,1,0:T(8,128)S(1)}, u32[]{:S(2)}, u32[]{:S(2)}) collective-permute-start(f32[2,8,9,256]{3,2,1,0:T(8,128)S(1)} %get-tuple-element.69), channel_id=1, source_target_pairs={{0,4},{4,8},{8,12},{1,5},{5,9},{9,13},{2,6},{6,10},{10,14},{3,7},{... | collective-permute-start | bytes 442376 | tf_op jit(solution)/shard_map/ppermute | solution.py:14
  12.3 9.7 %collective-permute-start.1 = (f32[2,8,9,256]{3,2,1,0:T(8,128)S(1)}, f32[2,8,9,256]{3,2,1,0:T(8,128)S(1)}, u32[]{:S(2)}, u32[]{:S(2)}) collective-permute-start(f32[2,8,9,256]{3,2,1,0:T(8,128)S(1)} %get-tuple-element.70), channel_id=1, source_target_pairs={{4,0},{8,4},{12,8},{5,1},{9,5},{13,9},{6,2},{10,6},{14,10},{7,3},{... | collective-permute-start | bytes 442376 | tf_op jit(solution)/shard_map/ppermute | solution.py:17
  17.7 7.3 %copy-start.2 = (f32[8,32,256]{2,1,0:T(8,128)}, f32[8,32,256]{2,1,0:T(8,128)S(1)}, u32[]{:S(2)}) copy-start(f32[8,32,256]{2,1,0:T(8,128)S(1)} %convert_element_type.23) | copy-start | bytes 786436
  22.3 40.1 %collective-permute-start.2 = (f32[2,8,50,9]{3,2,1,0:T(8,128)S(1)}, f32[2,8,50,9]{3,2,1,0:T(8,128)S(1)}, u32[]{:S(2)}, u32[]{:S(2)}) collective-permute-start(f32[2,8,50,9]{3,2,1,0:T(8,128)S(1)} %get-tuple-element.65), channel_id=1, source_target_pairs={{0,1},{1,2},{2,3},{4,5},{5,6},{6,7},{8,9},{9,10},{10,11},{12,13},{... | collective-permute-start | bytes 86408 | tf_op jit(solution)/shard_map/ppermute | solution.py:14
  23.6 38.7 %collective-permute-start.3 = (f32[2,8,50,9]{3,2,1,0:T(8,128)S(1)}, f32[2,8,50,9]{3,2,1,0:T(8,128)S(1)}, u32[]{:S(2)}, u32[]{:S(2)}) collective-permute-start(f32[2,8,50,9]{3,2,1,0:T(8,128)S(1)} %get-tuple-element.66), channel_id=1, source_target_pairs={{1,0},{2,1},{3,2},{5,4},{6,5},{7,6},{9,8},{10,9},{11,10},{13,12},{... | collective-permute-start | bytes 86408 | tf_op jit(solution)/shard_map/ppermute | solution.py:17
  109.9 15.1 %copy-start.1 = (f32[8,32,256]{2,1,0:T(8,128)S(1)}, f32[8,32,256]{2,1,0:T(8,128)}, u32[]{:S(2)}) copy-start(f32[8,32,256]{2,1,0:T(8,128)} %fusion.197) | copy-start | bytes 786436
  111.0 3.8 %collective-permute-start.4 = (f32[8,9,256]{2,1,0:T(8,128)S(1)}, f32[8,9,256]{2,1,0:T(8,128)S(1)}, u32[]{:S(2)}, u32[]{:S(2)}) collective-permute-start(f32[8,9,256]{2,1,0:T(8,128)S(1)} %get-tuple-element.73), channel_id=1, source_target_pairs={{0,4},{4,8},{8,12},{1,5},{5,9},{9,13},{2,6},{6,10},{10,14},{3,7},{... | collective-permute-start | bytes 221192 | tf_op jit(solution)/shard_map/ppermute | solution.py:14
  112.3 6.9 %collective-permute-start.5 = (f32[8,9,256]{2,1,0:T(8,128)S(1)}, f32[8,9,256]{2,1,0:T(8,128)S(1)}, u32[]{:S(2)}, u32[]{:S(2)}) collective-permute-start(f32[8,9,256]{2,1,0:T(8,128)S(1)} %get-tuple-element.74), channel_id=1, source_target_pairs={{4,0},{8,4},{12,8},{5,1},{9,5},{13,9},{6,2},{10,6},{14,10},{7,3},{... | collective-permute-start | bytes 221192 | tf_op jit(solution)/shard_map/ppermute | solution.py:17
  119.1 33.5 %copy-start.3 = (f32[8,9,256]{2,1,0:T(8,128)}, f32[8,9,256]{2,1,0:T(8,128)S(1)}, u32[]{:S(2)}) copy-start(f32[8,9,256]{2,1,0:T(8,128)S(1)} %collective-permute-done.5) | copy-start | bytes 221188
  120.3 2.9 %collective-permute-start.6 = (f32[8,50,9]{2,1,0:T(8,128)S(1)}, f32[8,50,9]{2,1,0:T(8,128)S(1)}, u32[]{:S(2)}, u32[]{:S(2)}) collective-permute-start(f32[8,50,9]{2,1,0:T(8,128)S(1)} %get-tuple-element.71), channel_id=1, source_target_pairs={{0,1},{1,2},{2,3},{4,5},{5,6},{6,7},{8,9},{9,10},{10,11},{12,13},{... | collective-permute-start | bytes 43208 | tf_op jit(solution)/shard_map/ppermute | solution.py:14
  121.6 3.4 %collective-permute-start.7 = (f32[8,50,9]{2,1,0:T(8,128)S(1)}, f32[8,50,9]{2,1,0:T(8,128)S(1)}, u32[]{:S(2)}, u32[]{:S(2)}) collective-permute-start(f32[8,50,9]{2,1,0:T(8,128)S(1)} %get-tuple-element.72), channel_id=1, source_target_pairs={{1,0},{2,1},{3,2},{5,4},{6,5},{7,6},{9,8},{10,9},{11,10},{13,12},{... | collective-permute-start | bytes 43208 | tf_op jit(solution)/shard_map/ppermute | solution.py:17
where the time goes:
time: 175 us; the launch traced here: 174 us
  other arithmetic  98 us (56%)
  blocking collectives  34.1 us (19%)
  starting transfers between devices  14.3 us (8%)
  local copies, waits for them, and re-layouts  12.2 us (7%)
  waiting for transfers between devices  11.7 us (7%)
  between operations  3.22 us (2%)
    add x54, other arithmetic, box_sum(): second = first[:, 0:rows] + first[:, 1:rows + 1] + first[:, 2:rows + 2]  45.3 us
    add x2, other arithmetic, smooth_once(): tissue * numerator / (denominator + 1.0 - tissue) + (1.0 - tissue) * values  37.7 us
    psum x1, blocking collectives, on_device(): summed, tissue_count = lax.psum((local_sum, local_count), ('gy', 'gx'))  34.1 us
    ppermute x4, waiting for transfers between devices, extended(): lax.ppermute(lax.slice_in_dim(block, 0, width, axis=dim), axis, backward)  10.3 us
    ppermute x4, starting transfers between devices, extended(): lax.ppermute(lax.slice_in_dim(block, block.shape[dim] - width, None, axis...  8.86 us
    convert_element_type x2, local copies, waits for them, and re-layouts, expand_mask(): spread.reshape(blocks_z * 4, blocks_y * 8, blocks_x * 8).astype(jnp.float32)  8.09 us
    mul x6, other arithmetic, smooth_once(): distance = box_sum(differ * differ, depth, rows, cols)  6.78 us
    ppermute x4, starting transfers between devices, extended(): lax.ppermute(lax.slice_in_dim(block, 0, width, axis=dim), axis, backward)  5.43 us
  transfers between devices with their start and end apart: 8, of which 5 were waited for; matrix products, arithmetic and copies ran while one was open for 3% of the time, Pallas kernels for 0%

commit v1 on v0

v1 whole, which is shorter than its diff:
```python
import functools

import jax
import jax.numpy as jnp
from jax import lax
from jax.experimental import pallas as pl
from jax.experimental.pallas import tpu as pltpu
from jax.sharding import PartitionSpec as P

F32 = jnp.float32
HALO = 18
OUT = HALO // 2
VMEM = pltpu.VMEM


def iotas():
    return (
        lax.broadcasted_iota(jnp.int32, (8, 128), 0),
        lax.broadcasted_iota(jnp.int32, (8, 128), 1),
    )


def lane_roll(x, by):
    return pltpu.roll(x, by % 128, 1)


def depth_roll(x, by):
    return pltpu.roll(x, by % 8, 0)


def pack_kernel(vol_ref, mask_ref, own_ref, low_ref, high_ref, sums_ref, stage):
    cols = own_ref.shape[2]
    rows = own_ref.shape[0] - mask_ref.shape[1]
    blocks = mask_ref.shape[1]
    tiles = cols // 128
    sub, lane = iotas()
    wide = lax.broadcasted_iota(jnp.int32, (mask_ref.shape[2], cols), 1) // 8
    spread = (wide == lax.broadcasted_iota(jnp.int32, wide.shape, 0)).astype(F32)
    half = lax.broadcasted_iota(jnp.int32, (8, mask_ref.shape[2]), 0) < 4
    tissue = []
    for b in range(blocks):
        picked = jnp.where(half, mask_ref[0, b : b + 1, :], mask_ref[1, b : b + 1, :])
        t = jnp.dot(picked.astype(F32), spread, preferred_element_type=F32)
        own_ref[rows + b] = t
        tissue.append(t)
    total = jnp.zeros((8, 128), F32)
    count = jnp.zeros((8, 128), F32)
    for t in range(tiles):
        sl = slice(t * 128, (t + 1) * 128)
        stage[...] = vol_ref[:, sl]
        for b in range(blocks):
            part = jnp.zeros((8, 128), F32)
            for y in range(b * 8, b * 8 + 8):
                v = stage[pl.ds(y, 8, stride=rows), :]
                own_ref[y, :, sl] = v
                res = v - 0.5 * (depth_roll(v, 1) + depth_roll(v, -1))
                part = part + res * res
            total = total + part * tissue[b][:, sl]
            count = count + tissue[b][:, sl]
    inner = (sub >= 1) & (sub <= 6)
    total = jnp.where(inner, total * (2.0 / 3.0), 0.0)
    count = jnp.where(inner, count * 8.0, 0.0)
    sums_ref[0] = total
    sums_ref[1] = count
    packs = (rows + blocks) // 4
    group = lane // 32
    for k in range(packs):
        low = own_ref[4 * k, :, 0:128]
        high = lane_roll(own_ref[4 * k, :, cols - 128 : cols], 32)
        for g in range(1, 4):
            low = jnp.where(group == g, lane_roll(own_ref[4 * k + g, :, 0:128], 32 * g), low)
            high = jnp.where(
                group == g, lane_roll(own_ref[4 * k + g, :, cols - 128 : cols], 32 * (g + 1)), high
            )
        low_ref[k] = low
        high_ref[k] = high
    for ref in (low_ref, high_ref):
        ref[packs] = total
        ref[packs + 1] = count


def widen_kernel(own_ref, left_ref, right_ref, own_sum_ref, far_ref, wide_ref, top_ref, bottom_ref, sums_ref):
    cols = own_ref.shape[2]
    count = own_ref.shape[0]
    blocks = count // 9
    rows = count - blocks
    packs = count // 4
    _, lane = iotas()
    place = lax.axis_index("gx")
    has_left = (place > 0).astype(F32)
    has_right = (place < lax.axis_size("gx") - 1).astype(F32)
    for k in range(packs):
        left = left_ref[k] * has_left
        right = right_ref[k] * has_right
        for g in range(4):
            edge = jnp.where(lane < HALO, lane_roll(right, -32 * g), 0.0)
            edge = jnp.where(lane >= 128 - HALO, lane_roll(left, 32 * (3 - g)), edge)
            wide_ref[4 * k + g, :, cols:] = edge
    wide_ref[:, :, 0:cols] = own_ref[...]
    top_ref[0:HALO] = wide_ref[0:HALO]
    bottom_ref[0:HALO] = wide_ref[rows - HALO : rows]
    top_ref[HALO : HALO + 3] = wide_ref[rows : rows + 3]
    bottom_ref[HALO : HALO + 3] = wide_ref[count - 3 : count]
    for i in range(2):
        s = own_sum_ref[i] + left_ref[packs + i] + right_ref[packs + i] + far_ref[i]
        sums_ref[i] = s
        for ref in (top_ref, bottom_ref):
            ref[HALO + 3, :, i * 128 : (i + 1) * 128] = s
    for ref in (top_ref, bottom_ref):
        ref[HALO + 3, :, 256:] = jnp.zeros((8, ref.shape[2] - 256), F32)


FIELDS = [(0, 8), (1, -8), (1, 0), (1, 8), (2, 8), (2, 0), (3, -8), (3, 0), (3, 8)]


def smooth_kernel(
    wide_ref, above_ref, below_ref, sums_ref, far_ref, smoothing_ref, out_ref, val, tis, cor, wgt, pair, stage
):
    count = wide_ref.shape[0]
    blocks = count // 9
    rows = count - blocks
    cols = out_ref.shape[1]
    ring = wide_ref.shape[2]
    tiles = ring // 128
    full = rows + 2 * HALO
    sub, lane = iotas()
    tile = [slice(t * 128, (t + 1) * 128) for t in range(tiles)]

    place = lax.axis_index("gy")
    has_above = (place > 0).astype(F32)
    has_below = (place < lax.axis_size("gy") - 1).astype(F32)

    total = sums_ref[0] + above_ref[HALO + 3, :, 0:128] + below_ref[HALO + 3, :, 0:128] + far_ref[0]
    number = (
        sums_ref[1] + above_ref[HALO + 3, :, 128:256] + below_ref[HALO + 3, :, 128:256] + far_ref[1]
    )
    total = jnp.sum(jnp.sum(total, axis=1, keepdims=True), axis=0, keepdims=True)
    number = jnp.sum(jnp.sum(number, axis=1, keepdims=True), axis=0, keepdims=True)
    variance = total / jnp.maximum(number, 1.0) + 1e-05
    h = smoothing_ref[0]
    inverse = 1.0 / (54.0 * h * h * variance)
    factor = jnp.broadcast_to(inverse * (-1.4426950408889634), (8, 128))

    def shift8(x):
        moved = [lane_roll(v, -8) for v in x]
        return [jnp.where(lane < 120, moved[t], moved[(t + 1) % tiles]) for t in range(tiles)]

    def unshift8(x):
        moved = [lane_roll(v, 8) for v in x]
        return [jnp.where(lane < 8, moved[(t - 1) % tiles], moved[t]) for t in range(tiles)]

    def box_lanes(x):
        up = [lane_roll(v, 1) for v in x]
        down = [lane_roll(v, -1) for v in x]
        return [
            x[t]
            + jnp.where(lane == 0, up[(t - 1) % tiles], up[t])
            + jnp.where(lane == 127, down[(t + 1) % tiles], down[t])
            for t in range(tiles)
        ]

    def load(ref, *idx):
        return [ref[(*idx, slice(None), s)] for s in tile]

    def store(ref, x, *idx):
        for t, s in enumerate(tile):
            ref[(*idx, slice(None), s)] = x[t]

    val[0, HALO : HALO + rows] = wide_ref[0:rows]
    val[0, 0:HALO] = above_ref[0:HALO] * has_above
    val[0, HALO + rows : full] = below_ref[0:HALO] * has_below
    tis[0, 3 : 3 + blocks] = wide_ref[rows:count]
    tis[0, 0:3] = above_ref[HALO : HALO + 3] * has_above
    tis[0, 3 + blocks :] = below_ref[HALO : HALO + 3] * has_below
    spans = blocks + 6
    for b in range(spans):
        t0 = load(tis, 0, b)
        t1 = shift8(t0)
        store(tis, t1, 1, b)
        store(tis, [depth_roll(v, 4) for v in t0], 2, b)
        store(tis, [depth_roll(v, 4) for v in t1], 3, b)
    for f, (kind, step) in enumerate(FIELDS):
        for b in range(spans if step == 0 else spans - 1):
            low, high = b, b + (1 if step else 0)
            p, q = (high, low) if step < 0 else (low, high)
            for s in tile:
                pair[f, b, :, s] = tis[0, p, :, s] * tis[kind, q, :, s]

    edge34 = (sub == 3) | (sub == 4)
    edge04 = (sub == 0) | (sub == 4)
    edge37 = (sub == 3) | (sub == 7)

    def run_rows(start, number, group, fn):
        whole = number // group
        if whole:
            @pl.loop(0, whole)
            def _(i):
                fn(start + i * group, group)
        if number % group:
            fn(start + whole * group, number % group)

    def prepare(r, group):
        for i in range(group):
            v = load(val, 0, r + i)
            v8 = shift8(v)
            store(val, v8, 1, r + i)
            store(val, [depth_roll(x, 4) for x in v], 2, r + i)
            store(val, [depth_roll(x, 4) for x in v8], 3, r + i)

    def corrections(r, group):
        square = []
        for i in range(-1, group + 1):
            square.append([x * x for x in load(val, 0, r + i)])
        for i in range(group):
            s = [square[i][t] + square[i + 1][t] + square[i + 2][t] for t in range(tiles)]
            s = box_lanes(s)
            near = [jnp.where(sub == 3, depth_roll(x, -1), depth_roll(x, 1)) for x in s]
            far = [depth_roll(x, 4) for x in near]
            store(cor, near, 0, r + i)
            store(cor, far, 1, r + i)
            store(cor, shift8(far), 2, r + i)

    def weights(fields):
        def fn(r, group):
            for f in fields:
                kind, step = FIELDS[f]
                p = r + 8 if step < 0 else r
                q = r + 8 if step > 0 else r
                e = []
                for i in range(-1, group + 1):
                    d = [a - b for a, b in zip(load(val, 0, p + i), load(val, kind, q + i))]
                    e.append([x * x for x in d])
                for i in range(group):
                    s = [e[i][t] + e[i + 1][t] + e[i + 2][t] for t in range(tiles)]
                    s = box_lanes(s)
                    up = [depth_roll(x, 1) for x in s]
                    down = [depth_roll(x, -1) for x in s]
                    if kind >= 2:
                        c = [
                            jnp.where(edge34, a, b)
                            for a, b in zip(load(cor, 0, p + i), load(cor, kind - 1, q + i))
                        ]
                        up = [jnp.where(edge04, a, b) for a, b in zip(c, up)]
                        down = [jnp.where(edge37, a, b) for a, b in zip(c, down)]
                    else:
                        up = [jnp.where(sub == 0, 0.0, b) for b in up]
                        down = [jnp.where(sub == 7, 0.0, b) for b in down]
                    block = (r + i + 24 - HALO) // 8
                    both = load(pair, f, block)
                    w = [
                        jnp.exp2((s[t] + up[t] + down[t]) * factor) * both[t] for t in range(tiles)
                    ]
                    store(wgt, w, f, r + i)

        return fn

    def combine(last):
        def fn(r, group):
            for i in range(group):
                y = r + i
                centre = load(val, 0, y)
                own = load(tis, 0, (y + 24 - HALO) // 8)
                den = [None] * 4
                num = [None] * 4

                def add(frame, w, v):
                    if den[frame] is None:
                        den[frame] = list(w)
                        num[frame] = [a * b for a, b in zip(w, v)]
                    else:
                        den[frame] = [a + b for a, b in zip(den[frame], w)]
                        num[frame] = [n + a * b for n, a, b in zip(num[frame], w, v)]

                for f, (kind, step) in enumerate(FIELDS):
                    add(0, load(wgt, f, y - 8 if step < 0 else y), load(val, kind, y + step))
                    if (kind, step) != (2, 0):
                        add(kind, load(wgt, f, y - 8 if step > 0 else y), load(val, 0, y - step))
                result = []
                for acc in (den, num):
                    side = [a + depth_roll(b, 4) for a, b in zip(acc[1], acc[3])]
                    side = unshift8(side)
                    result.append(
                        [a + depth_roll(b, 4) + c for a, b, c in zip(acc[0], acc[2], side)]
                    )
                for t in range(cols // 128 if last else tiles):
                    d = result[0][t] + own[t] + (1.0 - own[t])
                    n = result[1][t] + own[t] * centre[t]
                    new = jnp.where(own[t] > 0.0, n / d, centre[t])
                    if last:
                        stage[t, pl.ds(y - HALO, 8, stride=rows), :] = new
                    else:
                        val[4, y, :, tile[t]] = new

        return fn

    apart = [f for f, (_, step) in enumerate(FIELDS) if step]
    level = [f for f, (_, step) in enumerate(FIELDS) if not step]
    for margin in (OUT, 2 * OUT):
        last = margin == 2 * OUT
        first, number = margin, full - 2 * margin
        run_rows(first - OUT, number + 2 * OUT, 2, prepare)
        run_rows(first - OUT + 1, number + 2 * OUT - 2, 2, corrections)
        for f in apart:
            run_rows(first - 8, number + 8, 4, weights([f]))
        for f in level:
            run_rows(first, number, 4, weights([f]))
        run_rows(first, number, 2, combine(last))
        if last:
            for t in range(cols // 128):
                out_ref[:, tile[t]] = stage[t]
        else:
            val[0, first : first + number] = val[4, first : first + number]


def on_device(volume, tissue_mask, smoothing):
    depth, rows, cols = volume.shape
    blocks = tissue_mask.shape[1]
    count = rows + blocks
    ring = cols + 128
    full = rows + 2 * HALO
    spans = blocks + 6
    vm = pl.BlockSpec(memory_space=VMEM)
    shape = lambda *s: jax.ShapeDtypeStruct(s, F32)
    params = pltpu.CompilerParams(vmem_limit_bytes=32 * 1024 * 1024)
    own, low, high, sums = pl.pallas_call(
        pack_kernel,
        out_shape=(
            shape(count, 8, cols),
            shape(count // 4 + 2, 8, 128),
            shape(count // 4 + 2, 8, 128),
            shape(2, 8, 128),
        ),
        in_specs=[vm, vm],
        out_specs=[vm] * 4,
        scratch_shapes=[pltpu.VMEM((depth * rows, 128), F32)],
        compiler_params=params,
        name="pack",
    )(volume.reshape(depth * rows, cols), tissue_mask)

    def send(x, axis, by):
        size = lax.axis_size(axis)
        return lax.ppermute(x, axis, [(i, (i + by) % size) for i in range(size)])

    def sums_beyond(x, axis):
        return functools.reduce(
            jnp.add, [send(x, axis, by) for by in range(2, lax.axis_size(axis) - 1)]
        )

    right = send(low, "gx", -1)
    left = send(high, "gx", 1)
    far = sums_beyond(sums, "gx")
    wide, top, bottom, sums = pl.pallas_call(
        widen_kernel,
        out_shape=(
            shape(count, 8, ring),
            shape(HALO + 4, 8, ring),
            shape(HALO + 4, 8, ring),
            shape(2, 8, 128),
        ),
        in_specs=[vm] * 5,
        out_specs=[vm] * 4,
        compiler_params=params,
        name="widen",
    )(own, left, right, sums, far)
    below = send(top, "gy", -1)
    above = send(bottom, "gy", 1)
    far = sums_beyond(sums, "gy")
    out = pl.pallas_call(
        smooth_kernel,
        out_shape=shape(depth * rows, cols),
        in_specs=[vm] * 5 + [pl.BlockSpec(memory_space=pltpu.SMEM)],
        out_specs=vm,
        scratch_shapes=[
            pltpu.VMEM((5, full, 8, ring), F32),
            pltpu.VMEM((4, spans, 8, ring), F32),
            pltpu.VMEM((3, full, 8, ring), F32),
            pltpu.VMEM((len(FIELDS), full, 8, ring), F32),
            pltpu.VMEM((len(FIELDS), spans, 8, ring), F32),
            pltpu.VMEM((cols // 128, depth * rows, 128), F32),
        ],
        compiler_params=params,
        name="smooth",
    )(wide, above, below, sums, far, smoothing)
    return out.reshape(depth, rows, cols)


def solution(mesh):
    placed = (P(None, ("slab", "gy"), "gx"), P(None, ("slab", "gy"), "gx"), P())
    return jax.shard_map(
        on_device,
        mesh=mesh,
        in_specs=placed,
        out_specs=P(None, ("slab", "gy"), "gx"),
        check_vma=False,
    )
```

time: 175 us -> 68.3 us (0.39)
  other arithmetic: 98 us -> 0 us
  Pallas kernels: 0 us -> 43.5 us
  blocking collectives: 34.1 us -> 0 us
  local copies, waits for them, and re-layouts: 12.2 us -> 1.64 us
  starting transfers between devices: 14.3 us -> 9.46 us
  between operations: 3.22 us -> 0.67 us
    add x97 -> x0, other arithmetic: 85.5 us -> none  [the longest x54 45.3 us: box_sum(): second = first[:, 0:rows] + first[:, 1:rows + 1] + first[:, 2:rows + 2]]
    pallas_call x0 -> x3, Pallas kernels: none -> 43.5 us  [the longest x1 43.1 us: on_device(): pl.pallas_call(smooth_kernel, out_shape=shape(depth * rows, cols), in_spe...]
    psum x1 -> x0, blocking collectives: 34.1 us -> none  [on_device(): summed, tissue_count = lax.psum((local_sum, local_count), ('gy', 'gx'))]
    convert_element_type x2 -> x0, local copies, waits for them, and re-layouts: 8.09 us -> none  [expand_mask(): spread.reshape(blocks_z * 4, blocks_y * 8, blocks_x * 8).astype(jnp.float32)]
    mul x6 -> x0, other arithmetic: 6.78 us -> none  [smooth_once(): distance = box_sum(differ * differ, depth, rows, cols)]
    ppermute x8 -> x6, starting transfers between devices: 14.3 us -> 9.46 us  [send(): return lax.ppermute(x, axis, [(i, (i + by) % size) for i in range(size)])]
    concatenate x5 -> x0, other arithmetic: 4.35 us -> none  [extended(): block = jnp.concatenate([low, block, high], axis=dim)]
    broadcast_in_dim x1 -> x0, local copies, waits for them, and re-layouts: 2.55 us -> none  [expand_mask(): jnp.broadcast_to(tissue_mask[:, None, :, None, :, None], (blocks_z, 4, bl...]
  transfers between devices with their start and end apart: 8 -> 6, of which waited for: 5 -> 2; matrix products, arithmetic and copies ran while one was open for 3% -> 0% of each run, Pallas kernels for 0% -> 0%
where the time goes in v1:
time: 68.3 us; the launch traced here: 68.1 us
  Pallas kernels  43.5 us (64%)
  waiting for transfers between devices  12.9 us (19%)
  starting transfers between devices  9.46 us (14%)
  local copies, waits for them, and re-layouts  1.64 us (2%)
    pallas_call x1, Pallas kernels, on_device(): pl.pallas_call(smooth_kernel, out_shape=shape(depth * rows, cols), in_spe...  43.1 us
    ppermute x6, waiting for transfers between devices, send(): return lax.ppermute(x, axis, [(i, (i + by) % size) for i in range(size)])  12.9 us
    ppermute x6, starting transfers between devices, send(): return lax.ppermute(x, axis, [(i, (i + by) % size) for i in range(size)])  9.46 us
    unnamed x4, local copies, waits for them, and re-layouts  1.64 us
  transfers between devices with their start and end apart: 6, of which 2 were waited for; matrix products, arithmetic and copies ran while one was open for 0% of the time, Pallas kernels for 0%

profile of v1, /device:TPU:0, one launch (start us, length us, event | category | flops | bytes accessed | tf_op | source)
XLA Modules:
  0.0 68.1 jit_solution(5714898838354055295)
XLA Ops:
  0.0 0.0 copy-start
  0.0 0.9 %copy-done = f32[8,32,256]{2,1,0:T(8,128)S(1)} copy-done((f32[8,32,256]{2,1,0:T(8,128)S(1)}, f32[8,32,256]{2,1,0:T(8,128)}, u32[]{:S(2)}) %copy-start) | copy-done | bytes 262168
  1.0 0.0 copy-start.1
  1.0 0.7 %copy-done.1 = s32[2,4,32]{2,1,0:T(4,128)S(1)} copy-done((s32[2,4,32]{2,1,0:T(4,128)S(1)}, s32[2,4,32]{2,1,0:T(4,128)}, u32[]{:S(2)}) %copy-start.1) | copy-done | bytes 1048
  1.6 0.3 pack.1
  1.9 0.5 collective-permute-start
  2.4 2.0 %collective-permute-start.1 = (f32[11,8,128]{2,1,0:T(8,128)S(1)}, f32[11,8,128]{2,1,0:T(8,128)S(1)}, u32[]{:S(2)}, u32[]{:S(2)}) collective-permute-start(f32[11,8,128]{2,1,0:T(8,128)S(1)} %get-tuple-element.15), channel_id=1, source_target_pairs={{0,3},{1,0},{2,1},{3,2},{4,7},{5,4},{6,5},{7,6},{8,11},{9,8},{10,9... | collective-permute-start | bytes 135176 | tf_op jit(solution)/shard_map/ppermute | solution.py:342
  4.4 2.2 %collective-permute-start.2 = (f32[2,8,128]{2,1,0:T(8,128)S(1)}, f32[2,8,128]{2,1,0:T(8,128)S(1)}, u32[]{:S(2)}, u32[]{:S(2)}) collective-permute-start(f32[2,8,128]{2,1,0:T(8,128)S(1)} %get-tuple-element.16.own_sum_ref), channel_id=1, source_target_pairs={{0,2},{1,3},{2,0},{3,1},{4,6},{5,7},{6,4},{7,5},{8,10},{9,11},{10,... | collective-permute-start | bytes 24584 | tf_op jit(solution)/shard_map/ppermute | solution.py:342
  6.6 2.1 %collective-permute-done.2.far_ref = f32[2,8,128]{2,1,0:T(8,128)S(1)} collective-permute-done((f32[2,8,128]{2,1,0:T(8,128)S(1)}, f32[2,8,128]{2,1,0:T(8,128)S(1)}, u32[]{:S(2)}, u32[]{:S(2)}) %collective-permute-start.2) | collective-permute-done | bytes 8224 | tf_op jit(solution)/shard_map/ppermute | solution.py:342
  8.7 0.0 collective-permute-done.left_ref
  8.7 0.0 collective-permute-done.1.right_ref
  8.7 0.1 widen.1
  8.9 1.7 %collective-permute-start.3 = (f32[22,8,384]{2,1,0:T(8,128)S(1)}, f32[22,8,384]{2,1,0:T(8,128)S(1)}, u32[]{:S(2)}, u32[]{:S(2)}) collective-permute-start(f32[22,8,384]{2,1,0:T(8,128)S(1)} %get-tuple-element.18), channel_id=1, source_target_pairs={{0,4},{4,8},{8,12},{12,0},{1,5},{5,9},{9,13},{13,1},{2,6},{6,10},{... | collective-permute-start | bytes 811016 | tf_op jit(solution)/shard_map/ppermute | solution.py:342
  10.6 2.2 %collective-permute-start.4 = (f32[22,8,384]{2,1,0:T(8,128)S(1)}, f32[22,8,384]{2,1,0:T(8,128)S(1)}, u32[]{:S(2)}, u32[]{:S(2)}) collective-permute-start(f32[22,8,384]{2,1,0:T(8,128)S(1)} %get-tuple-element.19), channel_id=1, source_target_pairs={{0,12},{4,0},{8,4},{12,8},{1,13},{5,1},{9,5},{13,9},{2,14},{6,2},{... | collective-permute-start | bytes 811016 | tf_op jit(solution)/shard_map/ppermute | solution.py:342
  12.8 0.8 %collective-permute-start.5 = (f32[2,8,128]{2,1,0:T(8,128)S(1)}, f32[2,8,128]{2,1,0:T(8,128)S(1)}, u32[]{:S(2)}, u32[]{:S(2)}) collective-permute-start(f32[2,8,128]{2,1,0:T(8,128)S(1)} %get-tuple-element.20.sums_ref), channel_id=1, source_target_pairs={{0,8},{4,12},{8,0},{12,4},{1,9},{5,13},{9,1},{13,5},{2,10},{6,14},... | collective-permute-start | bytes 24584 | tf_op jit(solution)/shard_map/ppermute | solution.py:342
  14.3 10.8 %collective-permute-done.5.far_ref = f32[2,8,128]{2,1,0:T(8,128)S(1)} collective-permute-done((f32[2,8,128]{2,1,0:T(8,128)S(1)}, f32[2,8,128]{2,1,0:T(8,128)S(1)}, u32[]{:S(2)}, u32[]{:S(2)}) %collective-permute-start.5) | collective-permute-done | bytes 8224 | tf_op jit(solution)/shard_map/ppermute | solution.py:342
  25.1 0.0 collective-permute-done.3.above_ref
  25.1 0.0 collective-permute-done.4.below_ref
  25.1 43.1 %smooth.1 = f32[256,256]{1,0:T(8,128)} custom-call(f32[36,8,384]{2,1,0:T(8,128)S(1)} %get-tuple-element.17.wide_ref, f32[22,8,384]{2,1,0:T(8,128)S(1)} %collective-permute-done.3.above_ref, f32[22,8,384]{2,1,0:T(8,128)S(1)} %collective-permute-done.4.below_ref, f32[2,8,128]{2,1,0:T(8,128)S(1)} %get-tuple-element.20.sums_ref, ...), custom_call_target="tpu_custom_call" | custom-call | tf_op jit(solution)/shard_map/smooth/pallas_call | solution.py:368
Async XLA Ops:
  0.0 0.9 %copy-start = (f32[8,32,256]{2,1,0:T(8,128)S(1)}, f32[8,32,256]{2,1,0:T(8,128)}, u32[]{:S(2)}) copy-start(f32[8,32,256]{2,1,0:T(8,128)} %param.3) | copy-start | bytes 786436
  1.0 0.7 %copy-start.1 = (s32[2,4,32]{2,1,0:T(4,128)S(1)}, s32[2,4,32]{2,1,0:T(4,128)}, u32[]{:S(2)}) copy-start(s32[2,4,32]{2,1,0:T(4,128)} %mask_ref.1) | copy-start | bytes 3076
  1.9 6.8 %collective-permute-start = (f32[11,8,128]{2,1,0:T(8,128)S(1)}, f32[11,8,128]{2,1,0:T(8,128)S(1)}, u32[]{:S(2)}, u32[]{:S(2)}) collective-permute-start(f32[11,8,128]{2,1,0:T(8,128)S(1)} %get-tuple-element.14), channel_id=1, source_target_pairs={{0,1},{1,2},{2,3},{3,0},{4,5},{5,6},{6,7},{7,4},{8,9},{9,10},{10,1... | collective-permute-start | bytes 135176 | tf_op jit(solution)/shard_map/ppermute | solution.py:342
  2.4 6.3 %collective-permute-start.1 = (f32[11,8,128]{2,1,0:T(8,128)S(1)}, f32[11,8,128]{2,1,0:T(8,128)S(1)}, u32[]{:S(2)}, u32[]{:S(2)}) collective-permute-start(f32[11,8,128]{2,1,0:T(8,128)S(1)} %get-tuple-element.15), channel_id=1, source_target_pairs={{0,3},{1,0},{2,1},{3,2},{4,7},{5,4},{6,5},{7,6},{8,11},{9,8},{10,9... | collective-permute-start | bytes 135176 | tf_op jit(solution)/shard_map/ppermute | solution.py:342
  4.4 4.3 %collective-permute-start.2 = (f32[2,8,128]{2,1,0:T(8,128)S(1)}, f32[2,8,128]{2,1,0:T(8,128)S(1)}, u32[]{:S(2)}, u32[]{:S(2)}) collective-permute-start(f32[2,8,128]{2,1,0:T(8,128)S(1)} %get-tuple-element.16.own_sum_ref), channel_id=1, source_target_pairs={{0,2},{1,3},{2,0},{3,1},{4,6},{5,7},{6,4},{7,5},{8,10},{9,11},{10,... | collective-permute-start | bytes 24584 | tf_op jit(solution)/shard_map/ppermute | solution.py:342
  8.9 16.2 %collective-permute-start.3 = (f32[22,8,384]{2,1,0:T(8,128)S(1)}, f32[22,8,384]{2,1,0:T(8,128)S(1)}, u32[]{:S(2)}, u32[]{:S(2)}) collective-permute-start(f32[22,8,384]{2,1,0:T(8,128)S(1)} %get-tuple-element.18), channel_id=1, source_target_pairs={{0,4},{4,8},{8,12},{12,0},{1,5},{5,9},{9,13},{13,1},{2,6},{6,10},{... | collective-permute-start | bytes 811016 | tf_op jit(solution)/shard_map/ppermute | solution.py:342
  10.6 14.5 %collective-permute-start.4 = (f32[22,8,384]{2,1,0:T(8,128)S(1)}, f32[22,8,384]{2,1,0:T(8,128)S(1)}, u32[]{:S(2)}, u32[]{:S(2)}) collective-permute-start(f32[22,8,384]{2,1,0:T(8,128)S(1)} %get-tuple-element.19), channel_id=1, source_target_pairs={{0,12},{4,0},{8,4},{12,8},{1,13},{5,1},{9,5},{13,9},{2,14},{6,2},{... | collective-permute-start | bytes 811016 | tf_op jit(solution)/shard_map/ppermute | solution.py:342
  12.8 12.3 %collective-permute-start.5 = (f32[2,8,128]{2,1,0:T(8,128)S(1)}, f32[2,8,128]{2,1,0:T(8,128)S(1)}, u32[]{:S(2)}, u32[]{:S(2)}) collective-permute-start(f32[2,8,128]{2,1,0:T(8,128)S(1)} %get-tuple-element.20.sums_ref), channel_id=1, source_target_pairs={{0,8},{4,12},{8,0},{12,4},{1,9},{5,13},{9,1},{13,5},{2,10},{6,14},... | collective-permute-start | bytes 24584 | tf_op jit(solution)/shard_map/ppermute | solution.py:342

commit v2 on v1

--- a/solution.py
+++ b/solution.py
@@ -26,6 +26,21 @@
 
 def depth_roll(x, by):
     return pltpu.roll(x, by % 8, 0)
+
+
+def permuted(x, source, count):
+    lane = lax.broadcasted_iota(jnp.int32, (8, 128), 1)
+    result = []
+    for t in range(count):
+        column = source(t, lane)
+        index = lax.rem(column, 128)
+        home = lax.div(column, 128)
+        total = None
+        for i, v in enumerate(x):
+            part = jnp.take_along_axis(v, index, axis=1, mode="promise_in_bounds")
+            total = part if total is None else jnp.where(home == i, part, total)
+        result.append(total)
+    return result
 
 
 def pack_kernel(vol_ref, mask_ref, own_ref, low_ref, high_ref, sums_ref, stage):
@@ -79,12 +94,14 @@
         ref[packs + 1] = count
 
 
-def widen_kernel(own_ref, left_ref, right_ref, own_sum_ref, far_ref, wide_ref, top_ref, bottom_ref, sums_ref):
+def widen_kernel(fars, own_ref, left_ref, right_ref, own_sum_ref, *refs):
+    far_refs, (wide_ref, top_ref, bottom_ref, sums_ref) = refs[:fars], refs[fars:]
     cols = own_ref.shape[2]
     count = own_ref.shape[0]
     blocks = count // 9
     rows = count - blocks
     packs = count // 4
+    tiles = cols // 128 + 1
     _, lane = iotas()
     place = lax.axis_index("gx")
     has_left = (place > 0).astype(F32)
@@ -95,14 +112,18 @@
         for g in range(4):
             edge = jnp.where(lane < HALO, lane_roll(right, -32 * g), 0.0)
             edge = jnp.where(lane >= 128 - HALO, lane_roll(left, 32 * (3 - g)), edge)
-            wide_ref[4 * k + g, :, cols:] = edge
-    wide_ref[:, :, 0:cols] = own_ref[...]
+            row = [own_ref[4 * k + g, :, t * 128 : (t + 1) * 128] for t in range(tiles - 1)]
+            row = permuted(row + [edge], lambda t, l: l * tiles + t, tiles)
+            for t in range(tiles):
+                wide_ref[4 * k + g, :, t * 128 : (t + 1) * 128] = row[t]
     top_ref[0:HALO] = wide_ref[0:HALO]
     bottom_ref[0:HALO] = wide_ref[rows - HALO : rows]
     top_ref[HALO : HALO + 3] = wide_ref[rows : rows + 3]
     bottom_ref[HALO : HALO + 3] = wide_ref[count - 3 : count]
     for i in range(2):
-        s = own_sum_ref[i] + left_ref[packs + i] + right_ref[packs + i] + far_ref[i]
+        s = own_sum_ref[i] + left_ref[packs + i] + right_ref[packs + i]
+        for far_ref in far_refs:
+            s = s + far_ref[i]
         sums_ref[i] = s
         for ref in (top_ref, bottom_ref):
             ref[HALO + 3, :, i * 128 : (i + 1) * 128] = s
@@ -113,9 +134,8 @@
 FIELDS = [(0, 8), (1, -8), (1, 0), (1, 8), (2, 8), (2, 0), (3, -8), (3, 0), (3, 8)]
 
 
-def smooth_kernel(
-    wide_ref, above_ref, below_ref, sums_ref, far_ref, smoothing_ref, out_ref, val, tis, cor, wgt, pair, stage
-):
+def smooth_kernel(fars, wide_ref, above_ref, below_ref, sums_ref, smoothing_ref, *refs):
+    far_refs, (out_ref, val, tis, cor, wgt, pair, stage) = refs[:fars], refs[fars:]
     count = wide_ref.shape[0]
     blocks = count // 9
     rows = count - blocks
@@ -126,38 +146,30 @@
     sub, lane = iotas()
     tile = [slice(t * 128, (t + 1) * 128) for t in range(tiles)]
 
-    place = lax.axis_index("gy")
-    has_above = (place > 0).astype(F32)
-    has_below = (place < lax.axis_size("gy") - 1).astype(F32)
-
-    total = sums_ref[0] + above_ref[HALO + 3, :, 0:128] + below_ref[HALO + 3, :, 0:128] + far_ref[0]
-    number = (
-        sums_ref[1] + above_ref[HALO + 3, :, 128:256] + below_ref[HALO + 3, :, 128:256] + far_ref[1]
-    )
-    total = jnp.sum(jnp.sum(total, axis=1, keepdims=True), axis=0, keepdims=True)
-    number = jnp.sum(jnp.sum(number, axis=1, keepdims=True), axis=0, keepdims=True)
+    totals = [
+        functools.reduce(jnp.add, [ref[i] for ref in (sums_ref, *far_refs)])
+        + above_ref[HALO + 3, :, i * 128 : (i + 1) * 128]
+        + below_ref[HALO + 3, :, i * 128 : (i + 1) * 128]
+        for i in range(2)
+    ]
+    total, number = [
+        jnp.sum(jnp.sum(x, axis=1, keepdims=True), axis=0, keepdims=True) for x in totals
+    ]
     variance = total / jnp.maximum(number, 1.0) + 1e-05
     h = smoothing_ref[0]
     inverse = 1.0 / (54.0 * h * h * variance)
     factor = jnp.broadcast_to(inverse * (-1.4426950408889634), (8, 128))
 
-    def shift8(x):
-        moved = [lane_roll(v, -8) for v in x]
-        return [jnp.where(lane < 120, moved[t], moved[(t + 1) % tiles]) for t in range(tiles)]
-
-    def unshift8(x):
-        moved = [lane_roll(v, 8) for v in x]
-        return [jnp.where(lane < 8, moved[(t - 1) % tiles], moved[t]) for t in range(tiles)]
+    def along(x, by):
+        moved = []
+        for j in range(tiles):
+            lanes, source = divmod(j + by, tiles)
+            moved.append(lane_roll(x[source], -lanes) if lanes else x[source])
+        return moved
 
     def box_lanes(x):
-        up = [lane_roll(v, 1) for v in x]
-        down = [lane_roll(v, -1) for v in x]
-        return [
-            x[t]
-            + jnp.where(lane == 0, up[(t - 1) % tiles], up[t])
-            + jnp.where(lane == 127, down[(t + 1) % tiles], down[t])
-            for t in range(tiles)
-        ]
+        down, up = along(x, -1), along(x, 1)
+        return [x[t] + down[t] + up[t] for t in range(tiles)]
 
     def load(ref, *idx):
         return [ref[(*idx, slice(None), s)] for s in tile]
@@ -167,15 +179,15 @@
             ref[(*idx, slice(None), s)] = x[t]
 
     val[0, HALO : HALO + rows] = wide_ref[0:rows]
-    val[0, 0:HALO] = above_ref[0:HALO] * has_above
-    val[0, HALO + rows : full] = below_ref[0:HALO] * has_below
+    val[0, 0:HALO] = above_ref[0:HALO]
+    val[0, HALO + rows : full] = below_ref[0:HALO]
     tis[0, 3 : 3 + blocks] = wide_ref[rows:count]
-    tis[0, 0:3] = above_ref[HALO : HALO + 3] * has_above
-    tis[0, 3 + blocks :] = below_ref[HALO : HALO + 3] * has_below
+    tis[0, 0:3] = above_ref[HALO : HALO + 3]
+    tis[0, 3 + blocks :] = below_ref[HALO : HALO + 3]
     spans = blocks + 6
     for b in range(spans):
         t0 = load(tis, 0, b)
-        t1 = shift8(t0)
+        t1 = along(t0, 8)
         store(tis, t1, 1, b)
         store(tis, [depth_roll(v, 4) for v in t0], 2, b)
         store(tis, [depth_roll(v, 4) for v in t1], 3, b)
@@ -202,7 +214,7 @@
     def prepare(r, group):
         for i in range(group):
             v = load(val, 0, r + i)
-            v8 = shift8(v)
+            v8 = along(v, 8)
             store(val, v8, 1, r + i)
             store(val, [depth_roll(x, 4) for x in v], 2, r + i)
             store(val, [depth_roll(x, 4) for x in v8], 3, r + i)
@@ -218,17 +230,20 @@
             far = [depth_roll(x, 4) for x in near]
             store(cor, near, 0, r + i)
             store(cor, far, 1, r + i)
-            store(cor, shift8(far), 2, r + i)
+            store(cor, along(far, 8), 2, r + i)
 
     def weights(fields):
         def fn(r, group):
+            shared = {}
             for f in fields:
                 kind, step = FIELDS[f]
                 p = r + 8 if step < 0 else r
                 q = r + 8 if step > 0 else r
+                if (step < 0) not in shared:
+                    shared[step < 0] = [load(val, 0, p + i) for i in range(-1, group + 1)]
                 e = []
                 for i in range(-1, group + 1):
-                    d = [a - b for a, b in zip(load(val, 0, p + i), load(val, kind, q + i))]
+                    d = [a - b for a, b in zip(shared[step < 0][i + 1], load(val, kind, q + i))]
                     e.append([x * x for x in d])
                 for i in range(group):
                     s = [e[i][t] + e[i + 1][t] + e[i + 2][t] for t in range(tiles)]
@@ -278,18 +293,24 @@
                 result = []
                 for acc in (den, num):
                     side = [a + depth_roll(b, 4) for a, b in zip(acc[1], acc[3])]
-                    side = unshift8(side)
+                    side = along(side, -8)
                     result.append(
                         [a + depth_roll(b, 4) + c for a, b, c in zip(acc[0], acc[2], side)]
                     )
-                for t in range(cols // 128 if last else tiles):
+                new = []
+                for t in range(tiles):
                     d = result[0][t] + own[t] + (1.0 - own[t])
                     n = result[1][t] + own[t] * centre[t]
-                    new = jnp.where(own[t] > 0.0, n / d, centre[t])
-                    if last:
-                        stage[t, pl.ds(y - HALO, 8, stride=rows), :] = new
-                    else:
-                        val[4, y, :, tile[t]] = new
+                    new.append(jnp.where(own[t] > 0.0, n / d, centre[t]))
+                if last:
+                    column = lambda t, l: l + 128 * t
+                    where = lambda t, l: lax.rem(column(t, l), tiles) * 128 + lax.div(
+                        column(t, l), tiles
+                    )
+                    for t, x in enumerate(permuted(new, where, cols // 128)):
+                        stage[t, pl.ds(y - HALO, 8, stride=rows), :] = x
+                else:
+                    store(val, new, 4, y)
 
         return fn
 
@@ -298,13 +319,11 @@
     for margin in (OUT, 2 * OUT):
         last = margin == 2 * OUT
         first, number = margin, full - 2 * margin
-        run_rows(first - OUT, number + 2 * OUT, 2, prepare)
-        run_rows(first - OUT + 1, number + 2 * OUT - 2, 2, corrections)
-        for f in apart:
-            run_rows(first - 8, number + 8, 4, weights([f]))
-        for f in level:
-            run_rows(first, number, 4, weights([f]))
-        run_rows(first, number, 2, combine(last))
+        run_rows(first - OUT, number + 2 * OUT, 8, prepare)
+        run_rows(first - OUT + 1, number + 2 * OUT - 2, 8, corrections)
+        run_rows(first - 8, number + 8, 4, weights(apart))
+        run_rows(first, number, 4, weights(level))
+        run_rows(first, number, 4, combine(last))
         if last:
             for t in range(cols // 128):
                 out_ref[:, tile[t]] = stage[t]
@@ -316,7 +335,7 @@
     depth, rows, cols = volume.shape
     blocks = tissue_mask.shape[1]
     count = rows + blocks
-    ring = cols + 128
+    lanes = cols + 128
     full = rows + 2 * HALO
     spans = blocks + 6
     vm = pl.BlockSpec(memory_space=VMEM)
@@ -337,50 +356,56 @@
         name="pack",
     )(volume.reshape(depth * rows, cols), tissue_mask)
 
-    def send(x, axis, by):
+    def ring(x, axis, by):
         size = lax.axis_size(axis)
         return lax.ppermute(x, axis, [(i, (i + by) % size) for i in range(size)])
 
-    def sums_beyond(x, axis):
-        return functools.reduce(
-            jnp.add, [send(x, axis, by) for by in range(2, lax.axis_size(axis) - 1)]
-        )
-
-    right = send(low, "gx", -1)
-    left = send(high, "gx", 1)
-    far = sums_beyond(sums, "gx")
+    def line(x, axis, by):
+        size = lax.axis_size(axis)
+        return lax.ppermute(x, axis, [(i, i + by) for i in range(size) if 0 <= i + by < size])
+
+    def beyond(x, axis):
+        return [ring(x, axis, by) for by in range(2, lax.axis_size(axis) - 1)]
+
+    def ends(x, axis):
+        last = lax.axis_size(axis) - 1
+        return [lax.ppermute(x, axis, [(0, last), (last, 0)])] if last > 1 else []
+
+    right = ring(low, "gx", -1)
+    left = ring(high, "gx", 1)
+    far = beyond(sums, "gx")
     wide, top, bottom, sums = pl.pallas_call(
-        widen_kernel,
+        functools.partial(widen_kernel, len(far)),
         out_shape=(
-            shape(count, 8, ring),
-            shape(HALO + 4, 8, ring),
-            shape(HALO + 4, 8, ring),
+            shape(count, 8, lanes),
+            shape(HALO + 4, 8, lanes),
+            shape(HALO + 4, 8, lanes),
             shape(2, 8, 128),
         ),
-        in_specs=[vm] * 5,
+        in_specs=[vm] * (4 + len(far)),
         out_specs=[vm] * 4,
         compiler_params=params,
         name="widen",
-    )(own, left, right, sums, far)
-    below = send(top, "gy", -1)
-    above = send(bottom, "gy", 1)
-    far = sums_beyond(sums, "gy")
+    )(own, left, right, sums, *far)
+    below = line(top, "gy", -1)
+    above = line(bottom, "gy", 1)
+    far = beyond(sums, "gy") + ends(sums, "gy")
     out = pl.pallas_call(
-        smooth_kernel,
+        functools.partial(smooth_kernel, len(far)),
         out_shape=shape(depth * rows, cols),
-        in_specs=[vm] * 5 + [pl.BlockSpec(memory_space=pltpu.SMEM)],
+        in_specs=[vm] * 4 + [pl.BlockSpec(memory_space=pltpu.SMEM)] + [vm] * len(far),
         out_specs=vm,
         scratch_shapes=[
-            pltpu.VMEM((5, full, 8, ring), F32),
-            pltpu.VMEM((4, spans, 8, ring), F32),
-            pltpu.VMEM((3, full, 8, ring), F32),
-            pltpu.VMEM((len(FIELDS), full, 8, ring), F32),
-            pltpu.VMEM((len(FIELDS), spans, 8, ring), F32),
+            pltpu.VMEM((5, full, 8, lanes), F32),
+            pltpu.VMEM((4, spans, 8, lanes), F32),
+            pltpu.VMEM((3, full, 8, lanes), F32),
+            pltpu.VMEM((len(FIELDS), full, 8, lanes), F32),
+            pltpu.VMEM((len(FIELDS), spans, 8, lanes), F32),
             pltpu.VMEM((cols // 128, depth * rows, 128), F32),
         ],
         compiler_params=params,
         name="smooth",
-    )(wide, above, below, sums, far, smoothing)
+    )(wide, above, below, sums, smoothing, *far)
     return out.reshape(depth, rows, cols)
 
 

time: 68.3 us -> 42.5 us (0.62)
  Pallas kernels: 43.5 us -> 17.8 us
  waiting for transfers between devices: 12.9 us -> 5.54 us
  starting transfers between devices: 9.46 us -> 16.5 us
    pallas_call x2, Pallas kernels: 43.2 us -> 17.6 us  [the longest x1 15.3 us: on_device(): pl.pallas_call(functools.partial(smooth_kernel, len(far)), out_shape=shap...]
    ppermute x6 -> x7, waiting for transfers between devices: 12.9 us -> 5.54 us  [the longest x4 4.22 us: ring(): return lax.ppermute(x, axis, [(i, (i + by) % size) for i in range(size)])]
    ppermute x6 -> x7, starting transfers between devices: 9.46 us -> 16.5 us  [the longest x4 8.44 us: ring(): return lax.ppermute(x, axis, [(i, (i + by) % size) for i in range(size)])]
  transfers between devices with their start and end apart: 6 -> 7, of which waited for: 2 -> 3; matrix products, arithmetic and copies ran while one was open for 0% -> 0% of each run, Pallas kernels for 0% -> 0%
where the time goes in v2:
time: 42.5 us; the launch traced here: 42.2 us
  Pallas kernels  17.8 us (42%)
  starting transfers between devices  16.5 us (39%)
  waiting for transfers between devices  5.54 us (13%)
  local copies, waits for them, and re-layouts  1.64 us (4%)
  between operations  0.69 us (2%)
    pallas_call x1, Pallas kernels, on_device(): pl.pallas_call(functools.partial(smooth_kernel, len(far)), out_shape=shap...  15.3 us
    ppermute x4, starting transfers between devices, ring(): return lax.ppermute(x, axis, [(i, (i + by) % size) for i in range(size)])  8.44 us
    ppermute x2, starting transfers between devices, line(): lax.ppermute(x, axis, [(i, i + by) for i in range(size) if 0 <= i + by <...  4.84 us
    ppermute x4, waiting for transfers between devices, ring(): return lax.ppermute(x, axis, [(i, (i + by) % size) for i in range(size)])  4.22 us
    ppermute x1, starting transfers between devices, ends(): return [lax.ppermute(x, axis, [(0, last), (last, 0)])] if last > 1 else []  3.26 us
    pallas_call x1, Pallas kernels, on_device(): pl.pallas_call(functools.partial(widen_kernel, len(far)), out_shape=(shap...  2.3 us
    unnamed x4, local copies, waits for them, and re-layouts  1.64 us
    ppermute x1, waiting for transfers between devices, ends(): return [lax.ppermute(x, axis, [(0, last), (last, 0)])] if last > 1 else []  1.31 us
  transfers between devices with their start and end apart: 7, of which 3 were waited for; matrix products, arithmetic and copies ran while one was open for 0% of the time, Pallas kernels for 0%

profile of v2, /device:TPU:0, one launch (start us, length us, event | category | flops | bytes accessed | tf_op | source)
XLA Modules:
  0.0 42.2 jit_solution(3130402535724108682)
XLA Ops:
  0.0 0.0 copy-start
  0.0 0.9 %copy-done = f32[8,32,256]{2,1,0:T(8,128)S(1)} copy-done((f32[8,32,256]{2,1,0:T(8,128)S(1)}, f32[8,32,256]{2,1,0:T(8,128)}, u32[]{:S(2)}) %copy-start) | copy-done | bytes 262168
  1.0 0.0 copy-start.1
  1.0 0.7 %copy-done.1 = s32[2,4,32]{2,1,0:T(4,128)S(1)} copy-done((s32[2,4,32]{2,1,0:T(4,128)S(1)}, s32[2,4,32]{2,1,0:T(4,128)}, u32[]{:S(2)}) %copy-start.1) | copy-done | bytes 1048
  1.6 0.3 pack.1
  1.9 0.5 %collective-permute-start = (f32[11,8,128]{2,1,0:T(8,128)S(1)}, f32[11,8,128]{2,1,0:T(8,128)S(1)}, u32[]{:S(2)}, u32[]{:S(2)}) collective-permute-start(f32[11,8,128]{2,1,0:T(8,128)S(1)} %get-tuple-element.14), channel_id=1, source_target_pairs={{0,1},{1,2},{2,3},{3,0},{4,5},{5,6},{6,7},{7,4},{8,9},{9,10},{10,1... | collective-permute-start | bytes 135176 | tf_op jit(solution)/shard_map/ppermute | solution.py:361
  2.4 2.0 %collective-permute-start.1 = (f32[11,8,128]{2,1,0:T(8,128)S(1)}, f32[11,8,128]{2,1,0:T(8,128)S(1)}, u32[]{:S(2)}, u32[]{:S(2)}) collective-permute-start(f32[11,8,128]{2,1,0:T(8,128)S(1)} %get-tuple-element.15), channel_id=1, source_target_pairs={{0,3},{1,0},{2,1},{3,2},{4,7},{5,4},{6,5},{7,6},{8,11},{9,8},{10,9... | collective-permute-start | bytes 135176 | tf_op jit(solution)/shard_map/ppermute | solution.py:361
  4.4 2.2 %collective-permute-start.2 = (f32[2,8,128]{2,1,0:T(8,128)S(1)}, f32[2,8,128]{2,1,0:T(8,128)S(1)}, u32[]{:S(2)}, u32[]{:S(2)}) collective-permute-start(f32[2,8,128]{2,1,0:T(8,128)S(1)} %get-tuple-element.16.own_sum_ref), channel_id=1, source_target_pairs={{0,2},{1,3},{2,0},{3,1},{4,6},{5,7},{6,4},{7,5},{8,10},{9,11},{10,... | collective-permute-start | bytes 24584 | tf_op jit(solution)/shard_map/ppermute | solution.py:361
  6.6 2.1 %collective-permute-done.2.refs_0_ = f32[2,8,128]{2,1,0:T(8,128)S(1)} collective-permute-done((f32[2,8,128]{2,1,0:T(8,128)S(1)}, f32[2,8,128]{2,1,0:T(8,128)S(1)}, u32[]{:S(2)}, u32[]{:S(2)}) %collective-permute-start.2) | collective-permute-done | bytes 8224 | tf_op jit(solution)/shard_map/ppermute | solution.py:361
  8.7 0.0 collective-permute-done.left_ref
  8.7 0.0 collective-permute-done.1.right_ref
  8.7 2.3 %widen.1 = (f32[36,8,384]{2,1,0:T(8,128)S(1)}, f32[22,8,384]{2,1,0:T(8,128)S(1)}, f32[22,8,384]{2,1,0:T(8,128)S(1)}, f32[2,8,128]{2,1,0:T(8,128)S(1)}) custom-call(f32[36,8,256]{2,1,0:T(8,128)S(1)} %get-tuple-element.13.own_ref, f32[11,8,128]{2,1,0:T(8,128)S(1)} %collective-permute-done.left_ref, f32[11,8,128]{2,1,0:T(8,128)S(1)} %collective-permute-done.1.right_ref, ...), custom_call_target="tpu_custom_call" | custom-call | tf_op jit(solution)/shard_map/widen/pallas_call | solution.py:377
  11.0 3.5 %collective-permute-start.3 = (f32[22,8,384]{2,1,0:T(8,128)S(1)}, f32[22,8,384]{2,1,0:T(8,128)S(1)}, u32[]{:S(2)}, u32[]{:S(2)}) collective-permute-start(f32[22,8,384]{2,1,0:T(8,128)S(1)} %get-tuple-element.18), channel_id=1, source_target_pairs={{0,4},{4,8},{8,12},{1,5},{5,9},{9,13},{2,6},{6,10},{10,14},{3,7},{... | collective-permute-start | bytes 811016 | tf_op jit(solution)/shard_map/ppermute | solution.py:365
  14.6 1.3 %collective-permute-start.4 = (f32[22,8,384]{2,1,0:T(8,128)S(1)}, f32[22,8,384]{2,1,0:T(8,128)S(1)}, u32[]{:S(2)}, u32[]{:S(2)}) collective-permute-start(f32[22,8,384]{2,1,0:T(8,128)S(1)} %get-tuple-element.19), channel_id=1, source_target_pairs={{4,0},{8,4},{12,8},{5,1},{9,5},{13,9},{6,2},{10,6},{14,10},{7,3},{... | collective-permute-start | bytes 811016 | tf_op jit(solution)/shard_map/ppermute | solution.py:365
  15.9 3.7 %collective-permute-start.5 = (f32[2,8,128]{2,1,0:T(8,128)S(1)}, f32[2,8,128]{2,1,0:T(8,128)S(1)}, u32[]{:S(2)}, u32[]{:S(2)}) collective-permute-start(f32[2,8,128]{2,1,0:T(8,128)S(1)} %get-tuple-element.20.sums_ref), channel_id=1, source_target_pairs={{0,8},{4,12},{8,0},{12,4},{1,9},{5,13},{9,1},{13,5},{2,10},{6,14},... | collective-permute-start | bytes 24584 | tf_op jit(solution)/shard_map/ppermute | solution.py:361
  19.6 3.3 %collective-permute-start.6 = (f32[2,8,128]{2,1,0:T(8,128)S(1)}, f32[2,8,128]{2,1,0:T(8,128)S(1)}, u32[]{:S(2)}, u32[]{:S(2)}) collective-permute-start(f32[2,8,128]{2,1,0:T(8,128)S(1)} %get-tuple-element.20.sums_ref), channel_id=1, source_target_pairs={{0,12},{12,0},{1,13},{13,1},{2,14},{14,2},{3,15},{15,3},{16,28},{2... | collective-permute-start | bytes 24584 | tf_op jit(solution)/shard_map/ppermute | solution.py:372
  23.5 2.1 %collective-permute-done.5.refs_0_ = f32[2,8,128]{2,1,0:T(8,128)S(1)} collective-permute-done((f32[2,8,128]{2,1,0:T(8,128)S(1)}, f32[2,8,128]{2,1,0:T(8,128)S(1)}, u32[]{:S(2)}, u32[]{:S(2)}) %collective-permute-start.5) | collective-permute-done | bytes 8224 | tf_op jit(solution)/shard_map/ppermute | solution.py:361
  25.6 1.3 %collective-permute-done.6.refs_1_ = f32[2,8,128]{2,1,0:T(8,128)S(1)} collective-permute-done((f32[2,8,128]{2,1,0:T(8,128)S(1)}, f32[2,8,128]{2,1,0:T(8,128)S(1)}, u32[]{:S(2)}, u32[]{:S(2)}) %collective-permute-start.6) | collective-permute-done | bytes 8224 | tf_op jit(solution)/shard_map/ppermute | solution.py:372
  26.9 0.0 collective-permute-done.3.above_ref
  26.9 0.0 collective-permute-done.4.below_ref
  27.0 15.3 %smooth.1 = f32[256,256]{1,0:T(8,128)} custom-call(f32[36,8,384]{2,1,0:T(8,128)S(1)} %get-tuple-element.17.wide_ref, f32[22,8,384]{2,1,0:T(8,128)S(1)} %collective-permute-done.3.above_ref, f32[22,8,384]{2,1,0:T(8,128)S(1)} %collective-permute-done.4.below_ref, f32[2,8,128]{2,1,0:T(8,128)S(1)} %get-tuple-element.20.sums_ref, f32[1]{0:T(128)S(6)} %copy.4.smoothing_ref, ...), custom_call_target="tpu_custom_call" | custom-call | tf_op jit(solution)/shard_map/smooth/pallas_call | solution.py:393
Async XLA Ops:
  0.0 0.9 %copy-start = (f32[8,32,256]{2,1,0:T(8,128)S(1)}, f32[8,32,256]{2,1,0:T(8,128)}, u32[]{:S(2)}) copy-start(f32[8,32,256]{2,1,0:T(8,128)} %param.3) | copy-start | bytes 786436
  1.0 0.7 %copy-start.1 = (s32[2,4,32]{2,1,0:T(4,128)S(1)}, s32[2,4,32]{2,1,0:T(4,128)}, u32[]{:S(2)}) copy-start(s32[2,4,32]{2,1,0:T(4,128)} %mask_ref.1) | copy-start | bytes 3076
  1.9 6.8 %collective-permute-start = (f32[11,8,128]{2,1,0:T(8,128)S(1)}, f32[11,8,128]{2,1,0:T(8,128)S(1)}, u32[]{:S(2)}, u32[]{:S(2)}) collective-permute-start(f32[11,8,128]{2,1,0:T(8,128)S(1)} %get-tuple-element.14), channel_id=1, source_target_pairs={{0,1},{1,2},{2,3},{3,0},{4,5},{5,6},{6,7},{7,4},{8,9},{9,10},{10,1... | collective-permute-start | bytes 135176 | tf_op jit(solution)/shard_map/ppermute | solution.py:361
  2.4 6.3 %collective-permute-start.1 = (f32[11,8,128]{2,1,0:T(8,128)S(1)}, f32[11,8,128]{2,1,0:T(8,128)S(1)}, u32[]{:S(2)}, u32[]{:S(2)}) collective-permute-start(f32[11,8,128]{2,1,0:T(8,128)S(1)} %get-tuple-element.15), channel_id=1, source_target_pairs={{0,3},{1,0},{2,1},{3,2},{4,7},{5,4},{6,5},{7,6},{8,11},{9,8},{10,9... | collective-permute-start | bytes 135176 | tf_op jit(solution)/shard_map/ppermute | solution.py:361
  4.4 4.3 %collective-permute-start.2 = (f32[2,8,128]{2,1,0:T(8,128)S(1)}, f32[2,8,128]{2,1,0:T(8,128)S(1)}, u32[]{:S(2)}, u32[]{:S(2)}) collective-permute-start(f32[2,8,128]{2,1,0:T(8,128)S(1)} %get-tuple-element.16.own_sum_ref), channel_id=1, source_target_pairs={{0,2},{1,3},{2,0},{3,1},{4,6},{5,7},{6,4},{7,5},{8,10},{9,11},{10,... | collective-permute-start | bytes 24584 | tf_op jit(solution)/shard_map/ppermute | solution.py:361
  11.0 15.9 %collective-permute-start.3 = (f32[22,8,384]{2,1,0:T(8,128)S(1)}, f32[22,8,384]{2,1,0:T(8,128)S(1)}, u32[]{:S(2)}, u32[]{:S(2)}) collective-permute-start(f32[22,8,384]{2,1,0:T(8,128)S(1)} %get-tuple-element.18), channel_id=1, source_target_pairs={{0,4},{4,8},{8,12},{1,5},{5,9},{9,13},{2,6},{6,10},{10,14},{3,7},{... | collective-permute-start | bytes 811016 | tf_op jit(solution)/shard_map/ppermute | solution.py:365
  14.6 12.3 %collective-permute-start.4 = (f32[22,8,384]{2,1,0:T(8,128)S(1)}, f32[22,8,384]{2,1,0:T(8,128)S(1)}, u32[]{:S(2)}, u32[]{:S(2)}) collective-permute-start(f32[22,8,384]{2,1,0:T(8,128)S(1)} %get-tuple-element.19), channel_id=1, source_target_pairs={{4,0},{8,4},{12,8},{5,1},{9,5},{13,9},{6,2},{10,6},{14,10},{7,3},{... | collective-permute-start | bytes 811016 | tf_op jit(solution)/shard_map/ppermute | solution.py:365
  15.9 9.7 %collective-permute-start.5 = (f32[2,8,128]{2,1,0:T(8,128)S(1)}, f32[2,8,128]{2,1,0:T(8,128)S(1)}, u32[]{:S(2)}, u32[]{:S(2)}) collective-permute-start(f32[2,8,128]{2,1,0:T(8,128)S(1)} %get-tuple-element.20.sums_ref), channel_id=1, source_target_pairs={{0,8},{4,12},{8,0},{12,4},{1,9},{5,13},{9,1},{13,5},{2,10},{6,14},... | collective-permute-start | bytes 24584 | tf_op jit(solution)/shard_map/ppermute | solution.py:361
  19.6 7.3 %collective-permute-start.6 = (f32[2,8,128]{2,1,0:T(8,128)S(1)}, f32[2,8,128]{2,1,0:T(8,128)S(1)}, u32[]{:S(2)}, u32[]{:S(2)}) collective-permute-start(f32[2,8,128]{2,1,0:T(8,128)S(1)} %get-tuple-element.20.sums_ref), channel_id=1, source_target_pairs={{0,12},{12,0},{1,13},{13,1},{2,14},{14,2},{3,15},{15,3},{16,28},{2... | collective-permute-start | bytes 24584 | tf_op jit(solution)/shard_map/ppermute | solution.py:372

commit v3 on v2

v3 whole, which is shorter than its diff:
```python
import functools

import jax
import jax.numpy as jnp
from jax import lax
from jax.experimental import pallas as pl
from jax.experimental.pallas import tpu as pltpu
from jax.sharding import PartitionSpec as P

F32 = jnp.float32
HALO = 18
OUT = HALO // 2
VMEM = pltpu.VMEM


def iotas():
    return (
        lax.broadcasted_iota(jnp.int32, (8, 128), 0),
        lax.broadcasted_iota(jnp.int32, (8, 128), 1),
    )


def lane_roll(x, by):
    return pltpu.roll(x, by % 128, 1)


def depth_roll(x, by):
    return pltpu.roll(x, by % 8, 0)


def permuted(x, source, count):
    lane = lax.broadcasted_iota(jnp.int32, (8, 128), 1)
    result = []
    for t in range(count):
        column = source(t, lane)
        index = lax.rem(column, 128)
        home = lax.div(column, 128)
        total = None
        for i, v in enumerate(x):
            part = jnp.take_along_axis(v, index, axis=1, mode="promise_in_bounds")
            total = part if total is None else jnp.where(home == i, part, total)
        result.append(total)
    return result


def pack_kernel(vol_ref, mask_ref, own_ref, low_ref, high_ref, sums_ref, stage):
    cols = own_ref.shape[2]
    rows = own_ref.shape[0] - mask_ref.shape[1]
    blocks = mask_ref.shape[1]
    tiles = cols // 128
    sub, lane = iotas()
    wide = lax.broadcasted_iota(jnp.int32, (mask_ref.shape[2], cols), 1) // 8
    spread = (wide == lax.broadcasted_iota(jnp.int32, wide.shape, 0)).astype(F32)
    half = lax.broadcasted_iota(jnp.int32, (8, mask_ref.shape[2]), 0) < 4
    tissue = []
    for b in range(blocks):
        picked = jnp.where(half, mask_ref[0, b : b + 1, :], mask_ref[1, b : b + 1, :])
        t = jnp.dot(picked.astype(F32), spread, preferred_element_type=F32)
        own_ref[rows + b] = t
        tissue.append(t)
    total = jnp.zeros((8, 128), F32)
    count = jnp.zeros((8, 128), F32)
    for t in range(tiles):
        sl = slice(t * 128, (t + 1) * 128)
        stage[...] = vol_ref[:, sl]
        for b in range(blocks):
            part = jnp.zeros((8, 128), F32)
            for y in range(b * 8, b * 8 + 8):
                v = stage[pl.ds(y, 8, stride=rows), :]
                own_ref[y, :, sl] = v
                res = v - 0.5 * (depth_roll(v, 1) + depth_roll(v, -1))
                part = part + res * res
            total = total + part * tissue[b][:, sl]
            count = count + tissue[b][:, sl]
    inner = (sub >= 1) & (sub <= 6)
    total = jnp.where(inner, total * (2.0 / 3.0), 0.0)
    count = jnp.where(inner, count * 8.0, 0.0)
    sums_ref[0] = total
    sums_ref[1] = count
    packs = (rows + blocks) // 4
    group = lane // 32
    for k in range(packs):
        low = own_ref[4 * k, :, 0:128]
        high = lane_roll(own_ref[4 * k, :, cols - 128 : cols], 32)
        for g in range(1, 4):
            low = jnp.where(group == g, lane_roll(own_ref[4 * k + g, :, 0:128], 32 * g), low)
            high = jnp.where(
                group == g, lane_roll(own_ref[4 * k + g, :, cols - 128 : cols], 32 * (g + 1)), high
            )
        low_ref[k] = low
        high_ref[k] = high
    for ref in (low_ref, high_ref):
        ref[packs] = total
        ref[packs + 1] = count


def sums_kernel(left_ref, right_ref, *refs):
    packs = left_ref.shape[0] - 2
    ends_ref, all_ref = refs[-1], refs[-2]
    place, last = lax.axis_index("gy"), lax.axis_size("gy") - 1
    at_end = ((place == 0) | (place == last)).astype(F32)
    for i in range(2):
        s = left_ref[packs + i] + right_ref[packs + i]
        for ref in refs[:-2]:
            s = s + ref[i]
        all_ref[i] = s
        ends_ref[i] = s * jnp.where(lax.axis_index("gx") % 2 == 0, 1.0, at_end)


def widen_kernel(own_ref, left_ref, right_ref, sums_ref, wide_ref, top_ref, bottom_ref):
    cols = own_ref.shape[2]
    count = own_ref.shape[0]
    blocks = count // 9
    rows = count - blocks
    packs = count // 4
    tiles = cols // 128 + 1
    _, lane = iotas()
    place = lax.axis_index("gx")
    has_left = (place > 0).astype(F32)
    has_right = (place < lax.axis_size("gx") - 1).astype(F32)
    for k in range(packs):
        left = left_ref[k] * has_left
        right = right_ref[k] * has_right
        for g in range(4):
            edge = jnp.where(lane < HALO, lane_roll(right, -32 * g), 0.0)
            edge = jnp.where(lane >= 128 - HALO, lane_roll(left, 32 * (3 - g)), edge)
            row = [own_ref[4 * k + g, :, t * 128 : (t + 1) * 128] for t in range(tiles - 1)]
            row = permuted(row + [edge], lambda t, l: l * tiles + t, tiles)
            for t in range(tiles):
                wide_ref[4 * k + g, :, t * 128 : (t + 1) * 128] = row[t]
    top_ref[0:HALO] = wide_ref[0:HALO]
    bottom_ref[0:HALO] = wide_ref[rows - HALO : rows]
    top_ref[HALO : HALO + 3] = wide_ref[rows : rows + 3]
    bottom_ref[HALO : HALO + 3] = wide_ref[count - 3 : count]
    for i in range(2):
        for ref in (top_ref, bottom_ref):
            ref[HALO + 3, :, i * 128 : (i + 1) * 128] = sums_ref[i]
    for ref in (top_ref, bottom_ref):
        ref[HALO + 3, :, 256:] = jnp.zeros((8, ref.shape[2] - 256), F32)


FIELDS = [(0, 8), (1, -8), (1, 0), (1, 8), (2, 8), (2, 0), (3, -8), (3, 0), (3, 8)]
APART = [f for f, (_, step) in enumerate(FIELDS) if step]
LEVEL = [f for f, (_, step) in enumerate(FIELDS) if not step]


class Steps:
    def __init__(self, val, cor, dist, tis, pair):
        self.val, self.cor, self.dist, self.tis, self.pair = val, cor, dist, tis, pair
        self.tiles = val.shape[-1] // 128
        self.tile = [slice(t * 128, (t + 1) * 128) for t in range(self.tiles)]
        self.sub, self.lane = iotas()
        self.edge34 = (self.sub == 3) | (self.sub == 4)
        self.edge04 = (self.sub == 0) | (self.sub == 4)
        self.edge37 = (self.sub == 3) | (self.sub == 7)

    def load(self, ref, *idx):
        return [ref[(*idx, slice(None), s)] for s in self.tile]

    def store(self, ref, x, *idx):
        for t, s in enumerate(self.tile):
            ref[(*idx, slice(None), s)] = x[t]

    def along(self, x, by):
        moved = []
        for j in range(self.tiles):
            lanes, source = divmod(j + by, self.tiles)
            moved.append(lane_roll(x[source], -lanes) if lanes else x[source])
        return moved

    def box_lanes(self, x):
        down, up = self.along(x, -1), self.along(x, 1)
        first = x[0] + up[0]
        second = first + up[1]
        return [first + down[0], second] + [
            (x[t] + down[t]) + up[t] for t in range(2, self.tiles)
        ]

    def box_rows(self, e):
        result = []
        for i in range(0, len(e) - 2, 2):
            middle = [a + b for a, b in zip(e[i + 1], e[i + 2])]
            result.append([a + b for a, b in zip(e[i], middle)])
            if i + 3 < len(e):
                result.append([a + b for a, b in zip(middle, e[i + 3])])
        return result

    def run(self, starts, number, group, fn):
        whole = number // group
        if whole:
            @pl.loop(0, whole)
            def _(i):
                for start in starts:
                    fn(start + i * group, group)
        if number % group:
            for start in starts:
                fn(start + whole * group, number % group)

    def tissue(self, spans):
        for b in spans:
            t0 = self.load(self.tis, 0, b)
            t1 = self.along(t0, 8)
            self.store(self.tis, t1, 1, b)
            self.store(self.tis, [depth_roll(v, 4) for v in t0], 2, b)
            self.store(self.tis, [depth_roll(v, 4) for v in t1], 3, b)

    def pairs(self, spans, level_spans):
        for f, (kind, step) in enumerate(FIELDS):
            for b in spans if step else level_spans:
                low, high = b, b + (1 if step else 0)
                p, q = (high, low) if step < 0 else (low, high)
                for s in self.tile:
                    self.pair[f, b, :, s] = self.tis[0, p, :, s] * self.tis[kind, q, :, s]

    def prepare(self, source):
        def fn(r, group):
            for i in range(group):
                v = self.load(self.val, source, r + i)
                v8 = self.along(v, 8)
                if source:
                    self.store(self.val, v, 0, r + i)
                self.store(self.val, v8, 1, r + i)
                self.store(self.val, [depth_roll(x, 4) for x in v], 2, r + i)
                self.store(self.val, [depth_roll(x, 4) for x in v8], 3, r + i)

        return fn

    def corrections(self, r, group):
        square = []
        for i in range(-1, group + 1):
            square.append([x * x for x in self.load(self.val, 0, r + i)])
        sums = self.box_rows(square)
        for base in range(0, group, 4):
            some = sums[base : base + 4]
            packed = [depth_roll(x, 4) for x in some[0]]
            for i, row in enumerate(some):
                for place, by in ((2 * i, 2 * i - 4), (2 * i + 1, 2 * i - 2)):
                    if place:
                        here = self.sub == place
                        packed = [
                            jnp.where(here, depth_roll(x, by), y) for x, y in zip(row, packed)
                        ]
            packed = self.box_lanes(packed)
            moved = self.along(packed, 8)
            for i in range(len(some)):
                y = r + base + i
                self.store(self.cor, [depth_roll(x, 3 - 2 * i) for x in packed], 0, y)
                self.store(self.cor, [depth_roll(x, 7 - 2 * i) for x in packed], 1, y)
                self.store(self.cor, [depth_roll(x, 7 - 2 * i) for x in moved], 2, y)

    def distances(self, fields):
        def fn(r, group):
            shared = {}
            for f in fields:
                kind, step = FIELDS[f]
                p = r + 8 if step < 0 else r
                q = r + 8 if step > 0 else r
                if (step < 0) not in shared:
                    shared[step < 0] = [
                        self.load(self.val, 0, p + i) for i in range(-1, group + 1)
                    ]
                e = []
                for i in range(-1, group + 1):
                    other = self.load(self.val, kind, q + i)
                    d = [a - b for a, b in zip(shared[step < 0][i + 1], other)]
                    e.append([x * x for x in d])
                for i, s in enumerate(self.box_rows(e)):
                    s = self.box_lanes(s)
                    up = [depth_roll(x, 1) for x in s]
                    down = [depth_roll(x, -1) for x in s]
                    if kind >= 2:
                        near = self.load(self.cor, 0, p + i)
                        far = self.load(self.cor, kind - 1, q + i)
                        c = [jnp.where(self.edge34, a, b) for a, b in zip(near, far)]
                        up = [jnp.where(self.edge04, a, b) for a, b in zip(c, up)]
                        down = [jnp.where(self.edge37, a, b) for a, b in zip(c, down)]
                    else:
                        up = [jnp.where(self.sub == 0, 0.0, b) for b in up]
                        down = [jnp.where(self.sub == 7, 0.0, b) for b in down]
                    self.store(
                        self.dist, [a + b + c for a, b, c in zip(s, up, down)], f, r + i
                    )

        return fn

    def weight(self, f, r, factor):
        both = self.load(self.pair, f, (r + 24 - HALO) // 8)
        d = self.load(self.dist, f, r)
        return [jnp.exp2(a * factor) * b for a, b in zip(d, both)]

    def early(self, factor):
        def fn(r, group):
            for i in range(group):
                for f in APART:
                    self.store(self.dist, self.weight(f, r + i, factor), f, r + i)

        return fn

    def combine(self, factor, put):
        def fn(r, group):
            for i in range(group):
                y = r + i
                centre = self.load(self.val, 0, y)
                own = self.load(self.tis, 0, (y + 24 - HALO) // 8)
                den = [None] * 4
                num = [None] * 4

                def add(frame, w, v):
                    if den[frame] is None:
                        den[frame] = list(w)
                        num[frame] = [a * b for a, b in zip(w, v)]
                    else:
                        den[frame] = [a + b for a, b in zip(den[frame], w)]
                        num[frame] = [n + a * b for n, a, b in zip(num[frame], w, v)]

                for f, (kind, step) in enumerate(FIELDS):
                    w = self.weight(f, y, factor)
                    before = w
                    if step:
                        before = self.load(self.dist, f, y - 8)
                        self.store(self.dist, w, f, y)
                    at_p, at_q = (before, w) if step < 0 else (w, before)
                    add(0, at_p, self.load(self.val, kind, y + step))
                    if (kind, step) != (2, 0):
                        add(kind, at_q, self.load(self.val, 0, y - step))
                result = []
                for acc in (den, num):
                    side = [a + depth_roll(b, 4) for a, b in zip(acc[1], acc[3])]
                    side = self.along(side, -8)
                    result.append(
                        [a + depth_roll(b, 4) + c for a, b, c in zip(acc[0], acc[2], side)]
                    )
                new = []
                for t in range(self.tiles):
                    d = result[0][t] + own[t] + (1.0 - own[t])
                    n = result[1][t] + own[t] * centre[t]
                    new.append(jnp.where(own[t] > 0.0, n / d, centre[t]))
                put(y, new)

        return fn


def inner_kernel(wide_ref, val, cor, dist, tis, pair):
    count = wide_ref.shape[0]
    blocks = count // 9
    rows = count - blocks
    low, high = HALO, HALO + rows
    steps = Steps(val, cor, dist, tis, pair)
    val[0, low:high] = wide_ref[0:rows]
    tis[0, 3 : 3 + blocks] = wide_ref[rows:count]
    steps.tissue(range(3, 3 + blocks))
    steps.pairs(range(3, 2 + blocks), range(3, 3 + blocks))
    steps.run([low], rows, 8, steps.prepare(0))
    steps.run([low + 1], rows - 2, 8, steps.corrections)
    steps.run([low + 1], rows - 10, 8, steps.distances(APART))
    steps.run([low + 1], rows - 2, 8, steps.distances(LEVEL))


def outer_kernel(above_ref, below_ref, sums_ref, *refs):
    part_ref, val, cor, dist, tis, pair = refs[5:]
    full = val.shape[1]
    rows = full - 2 * HALO
    spans = tis.shape[1]
    low, high = HALO, HALO + rows
    steps = Steps(val, cor, dist, tis, pair)

    val[0, 0:low] = above_ref[0:HALO]
    val[0, high:full] = below_ref[0:HALO]
    tis[0, 0:3] = above_ref[HALO : HALO + 3]
    tis[0, spans - 3 :] = below_ref[HALO : HALO + 3]
    ends = [*range(0, 3), *range(spans - 3, spans)]
    steps.tissue(ends)
    steps.pairs([*range(0, 3), *range(spans - 4, spans - 1)], ends)
    for i in range(2):
        lanes = slice(i * 128, (i + 1) * 128)
        part_ref[i] = sums_ref[i] + above_ref[HALO + 3, :, lanes] + below_ref[HALO + 3, :, lanes]

    steps.run([0, high], HALO, 6, steps.prepare(0))
    steps.run([1, high - 1], HALO, 6, steps.corrections)
    steps.run([OUT - 8, high - 9], low + 1 - (OUT - 8), 6, steps.distances(APART))
    steps.run([OUT, high - 1], low + 1 - OUT, 5, steps.distances(LEVEL))


def smooth_kernel(fars, part_ref, smoothing_ref, *refs):
    far_refs, refs = refs[:fars], refs[fars + 5 :]
    out_ref, val, cor, dist, tis, pair, stage = refs
    cols = out_ref.shape[1]
    full = val.shape[1]
    rows = full - 2 * HALO
    low = HALO
    steps = Steps(val, cor, dist, tis, pair)

    total, number = [
        jnp.sum(
            jnp.sum(
                functools.reduce(jnp.add, [ref[i] for ref in (part_ref, *far_refs)]),
                axis=1,
                keepdims=True,
            ),
            axis=0,
            keepdims=True,
        )
        for i in range(2)
    ]
    variance = total / jnp.maximum(number, 1.0) + 1e-05
    h = smoothing_ref[0]
    inverse = 1.0 / (54.0 * h * h * variance)
    factor = jnp.broadcast_to(inverse * (-1.4426950408889634), (8, 128))

    def keep(y, new):
        steps.store(val, new, 4, y)

    def finish(y, new):
        column = lambda t, l: l + 128 * t
        where = lambda t, l: lax.rem(column(t, l), steps.tiles) * 128 + lax.div(
            column(t, l), steps.tiles
        )
        for t, x in enumerate(permuted(new, where, cols // 128)):
            stage[t, pl.ds(y - HALO, 8, stride=rows), :] = x

    steps.run([OUT - 8], 8, 2, steps.early(factor))
    steps.run([OUT], full - 2 * OUT, 2, steps.combine(factor, keep))

    steps.run([OUT], full - 2 * OUT, 10, steps.prepare(4))
    steps.run([OUT + 1], full - 2 * OUT - 2, 8, steps.corrections)
    steps.run([low - 8], rows + 8, 8, steps.distances(APART))
    steps.run([low], rows, 8, steps.distances(LEVEL))
    steps.run([low - 8], 8, 2, steps.early(factor))
    steps.run([low], rows, 4, steps.combine(factor, finish))
    for t in range(cols // 128):
        out_ref[:, t * 128 : (t + 1) * 128] = stage[t]


def on_device(volume, tissue_mask, smoothing):
    depth, rows, cols = volume.shape
    blocks = tissue_mask.shape[1]
    count = rows + blocks
    lanes = cols + 128
    full = rows + 2 * HALO
    spans = blocks + 6
    vm = pl.BlockSpec(memory_space=VMEM)
    shape = lambda *s: jax.ShapeDtypeStruct(s, F32)
    params = pltpu.CompilerParams(vmem_limit_bytes=32 * 1024 * 1024)
    own, low, high, sums = pl.pallas_call(
        pack_kernel,
        out_shape=(
            shape(count, 8, cols),
            shape(count // 4 + 2, 8, 128),
            shape(count // 4 + 2, 8, 128),
            shape(2, 8, 128),
        ),
        in_specs=[vm, vm],
        out_specs=[vm] * 4,
        scratch_shapes=[pltpu.VMEM((depth * rows, 128), F32)],
        compiler_params=params,
        name="pack",
    )(volume.reshape(depth * rows, cols), tissue_mask)

    def ring(x, axis, by):
        size = lax.axis_size(axis)
        return lax.ppermute(x, axis, [(i, (i + by) % size) for i in range(size)])

    def line(x, axis, by):
        size = lax.axis_size(axis)
        return lax.ppermute(x, axis, [(i, i + by) for i in range(size) if 0 <= i + by < size])

    def beyond(x, axis):
        return [ring(x, axis, by) for by in range(2, lax.axis_size(axis) - 1)]

    def far_rows(x, ends):
        ny, nx = lax.axis_size("gy"), lax.axis_size("gx")
        shifts = list(range(2, ny - 1)) + [None]
        got = []
        for even, odd in zip(shifts[0::2], shifts[1::2]):
            pairs = []
            for y in range(ny):
                for c in range(nx):
                    by = odd if c % 2 else even
                    to = ny - 1 - y if by is None else (y + by) % ny
                    pairs.append((y * nx + c, to * nx + c))
            got.append(lax.ppermute(ends if odd is None else x, ("gy", "gx"), pairs))
        return functools.reduce(jnp.add, got)

    right = ring(low, "gx", -1)
    left = ring(high, "gx", 1)
    far = beyond(sums, "gx")
    sums, ends = pl.pallas_call(
        sums_kernel,
        out_shape=[shape(2, 8, 128)] * 2,
        in_specs=[vm] * (3 + len(far)),
        out_specs=[vm] * 2,
        compiler_params=params,
        name="sums",
    )(left, right, sums, *far)
    wide, top, bottom = pl.pallas_call(
        widen_kernel,
        out_shape=(
            shape(count, 8, lanes),
            shape(HALO + 4, 8, lanes),
            shape(HALO + 4, 8, lanes),
        ),
        in_specs=[vm] * 4,
        out_specs=[vm] * 3,
        compiler_params=params,
        name="widen",
    )(own, left, right, sums)
    below = line(top, "gy", -1)
    above = line(bottom, "gy", 1)
    state = [
        shape(5, full, 8, lanes),
        shape(3, full, 8, lanes),
        shape(len(FIELDS), full, 8, lanes),
        shape(4, spans, 8, lanes),
        shape(len(FIELDS), spans, 8, lanes),
    ]
    held = pl.pallas_call(
        inner_kernel,
        out_shape=state,
        in_specs=[vm],
        out_specs=[vm] * 5,
        compiler_params=params,
        cost_estimate=pl.CostEstimate(flops=20_000_000, bytes_accessed=8_000_000, transcendentals=0),
        name="inner",
    )(wide)
    sums, ends, *held = lax.optimization_barrier((sums, ends, *held))
    far = far_rows(sums, ends)
    part, *held = pl.pallas_call(
        outer_kernel,
        out_shape=[shape(2, 8, 128)] + state,
        in_specs=[vm] * 8,
        out_specs=[vm] * 6,
        input_output_aliases={3 + i: 1 + i for i in range(5)},
        compiler_params=params,
        cost_estimate=pl.CostEstimate(flops=20_000_000, bytes_accessed=8_000_000, transcendentals=0),
        name="outer",
    )(above, below, sums, *held)
    part, far = lax.optimization_barrier((part, far))
    far = [far, lax.ppermute(far, "gx", [(c, c ^ 1) for c in range(lax.axis_size("gx"))])]
    out = pl.pallas_call(
        functools.partial(smooth_kernel, len(far)),
        out_shape=[shape(depth * rows, cols)] + state,
        in_specs=[vm] + [pl.BlockSpec(memory_space=pltpu.SMEM)] + [vm] * (len(far) + 5),
        out_specs=[vm] * 6,
        input_output_aliases={2 + len(far) + i: 1 + i for i in range(5)},
        scratch_shapes=[pltpu.VMEM((cols // 128, depth * rows, 128), F32)],
        compiler_params=params,
        name="smooth",
    )(part, smoothing, *far, *held)[0]
    return out.reshape(depth, rows, cols)


def solution(mesh):
    placed = (P(None, ("slab", "gy"), "gx"), P(None, ("slab", "gy"), "gx"), P())
    return jax.shard_map(
        on_device,
        mesh=mesh,
        in_specs=placed,
        out_specs=P(None, ("slab", "gy"), "gx"),
        check_vma=False,
    )
```

time: 42.5 us -> 37.8 us (0.89)
  starting transfers between devices: 16.5 us -> 13.4 us
  Pallas kernels: 17.8 us -> 16.9 us
  waiting for transfers between devices: 5.54 us -> 5 us
    ppermute x4 -> x3, starting transfers between devices: 8.44 us -> 4.74 us  [ring(): return lax.ppermute(x, axis, [(i, (i + by) % size) for i in range(size)])]
    ppermute x2, waiting for transfers between devices: 0.01 us -> 2.37 us  [line(): lax.ppermute(x, axis, [(i, i + by) for i in range(size) if 0 <= i + by <...]
    ppermute x4 -> x3, waiting for transfers between devices: 4.22 us -> 2.11 us  [ring(): return lax.ppermute(x, axis, [(i, (i + by) % size) for i in range(size)])]
    pallas_call x2 -> x5, Pallas kernels: 17.6 us -> 16.6 us  [the longest x1 9.61 us: on_device(): pl.pallas_call(functools.partial(smooth_kernel, len(far)), out_shape=[sha...]
    ppermute x1 -> x2, waiting for transfers between devices: 1.31 us -> 0.51 us  [the longest x1 0.51 us: on_device(): lax.ppermute(far, 'gx', [(c, c ^ 1) for c in range(lax.axis_size('gx'))])]
    ppermute x1 -> x2, starting transfers between devices: 3.26 us -> 3.78 us  [the longest x1 3.71 us: far_rows(): got.append(lax.ppermute(ends if odd is None else x, ('gy', 'gx'), pairs))]
  transfers between devices with their start and end apart: 7 -> 7, of which waited for: 3 -> 3; matrix products, arithmetic and copies ran while one was open for 0% -> 0% of each run, Pallas kernels for 0% -> 12%
where the time goes in v3:
time: 37.8 us; the launch traced here: 37.6 us
  Pallas kernels  16.9 us (45%)
  starting transfers between devices  13.4 us (35%)
  waiting for transfers between devices  5 us (13%)
  local copies, waits for them, and re-layouts  1.64 us (4%)
  between operations  0.71 us (2%)
    pallas_call x1, Pallas kernels, on_device(): pl.pallas_call(functools.partial(smooth_kernel, len(far)), out_shape=[sha...  9.61 us
    ppermute x2, starting transfers between devices, line(): lax.ppermute(x, axis, [(i, i + by) for i in range(size) if 0 <= i + by <...  4.84 us
    ppermute x3, starting transfers between devices, ring(): return lax.ppermute(x, axis, [(i, (i + by) % size) for i in range(size)])  4.74 us
    ppermute x1, starting transfers between devices, far_rows(): got.append(lax.ppermute(ends if odd is None else x, ('gy', 'gx'), pairs))  3.71 us
    pallas_call x1, Pallas kernels, on_device(): pl.pallas_call(outer_kernel, out_shape=[shape(2, 8, 128)] + state, in_spe...  2.42 us
    ppermute x2, waiting for transfers between devices, line(): lax.ppermute(x, axis, [(i, i + by) for i in range(size) if 0 <= i + by <...  2.37 us
    pallas_call x1, Pallas kernels, on_device(): pl.pallas_call(widen_kernel, out_shape=(shape(count, 8, lanes), shape(HAL...  2.3 us
    pallas_call x1, Pallas kernels, on_device(): pl.pallas_call(inner_kernel, out_shape=state, in_specs=[vm], out_specs=[v...  2.28 us
  transfers between devices with their start and end apart: 7, of which 3 were waited for; matrix products, arithmetic and copies ran while one was open for 0% of the time, Pallas kernels for 12%

profile of v3, /device:TPU:0, one launch (start us, length us, event | category | flops | bytes accessed | tf_op | source)
XLA Modules:
  0.0 37.6 jit_solution(12771186968135218607)
XLA Ops:
  0.0 0.0 copy-start
  0.0 0.9 %copy-done = f32[8,32,256]{2,1,0:T(8,128)S(1)} copy-done((f32[8,32,256]{2,1,0:T(8,128)S(1)}, f32[8,32,256]{2,1,0:T(8,128)}, u32[]{:S(2)}) %copy-start) | copy-done | bytes 262168
  1.0 0.0 copy-start.1
  1.0 0.7 %copy-done.1 = s32[2,4,32]{2,1,0:T(4,128)S(1)} copy-done((s32[2,4,32]{2,1,0:T(4,128)S(1)}, s32[2,4,32]{2,1,0:T(4,128)}, u32[]{:S(2)}) %copy-start.1) | copy-done | bytes 1048
  1.6 0.3 pack.1
  1.9 0.5 %collective-permute-start = (f32[11,8,128]{2,1,0:T(8,128)S(1)}, f32[11,8,128]{2,1,0:T(8,128)S(1)}, u32[]{:S(2)}, u32[]{:S(2)}) collective-permute-start(f32[11,8,128]{2,1,0:T(8,128)S(1)} %get-tuple-element.36), channel_id=1, source_target_pairs={{0,1},{1,2},{2,3},{3,0},{4,5},{5,6},{6,7},{7,4},{8,9},{9,10},{10,1... | collective-permute-start | bytes 135176 | tf_op jit(solution)/shard_map/ppermute | solution.py:461
  2.4 2.0 %collective-permute-start.1 = (f32[11,8,128]{2,1,0:T(8,128)S(1)}, f32[11,8,128]{2,1,0:T(8,128)S(1)}, u32[]{:S(2)}, u32[]{:S(2)}) collective-permute-start(f32[11,8,128]{2,1,0:T(8,128)S(1)} %get-tuple-element.37), channel_id=1, source_target_pairs={{0,3},{1,0},{2,1},{3,2},{4,7},{5,4},{6,5},{7,6},{8,11},{9,8},{10,9... | collective-permute-start | bytes 135176 | tf_op jit(solution)/shard_map/ppermute | solution.py:461
  4.4 2.2 %collective-permute-start.2 = (f32[2,8,128]{2,1,0:T(8,128)S(1)}, f32[2,8,128]{2,1,0:T(8,128)S(1)}, u32[]{:S(2)}, u32[]{:S(2)}) collective-permute-start(f32[2,8,128]{2,1,0:T(8,128)S(1)} %get-tuple-element.38.refs_0_), channel_id=1, source_target_pairs={{0,2},{1,3},{2,0},{3,1},{4,6},{5,7},{6,4},{7,5},{8,10},{9,11},{10,... | collective-permute-start | bytes 24584 | tf_op jit(solution)/shard_map/ppermute | solution.py:461
  6.6 2.1 %collective-permute-done.2.refs_1_ = f32[2,8,128]{2,1,0:T(8,128)S(1)} collective-permute-done((f32[2,8,128]{2,1,0:T(8,128)S(1)}, f32[2,8,128]{2,1,0:T(8,128)S(1)}, u32[]{:S(2)}, u32[]{:S(2)}) %collective-permute-start.2) | collective-permute-done | bytes 8224 | tf_op jit(solution)/shard_map/ppermute | solution.py:461
  8.7 0.0 collective-permute-done.left_ref
  8.7 0.0 collective-permute-done.1.right_ref
  8.8 2.3 %widen.1 = (f32[36,8,384]{2,1,0:T(8,128)S(1)}, f32[22,8,384]{2,1,0:T(8,128)S(1)}, f32[22,8,384]{2,1,0:T(8,128)S(1)}) custom-call(f32[36,8,256]{2,1,0:T(8,128)S(1)} %get-tuple-element.35.own_ref, f32[11,8,128]{2,1,0:T(8,128)S(1)} %collective-permute-done.left_ref, f32[11,8,128]{2,1,0:T(8,128)S(1)} %collective-permute-done.1.right_ref, ...), custom_call_target="tpu_custom_call" | custom-call | tf_op jit(solution)/shard_map/widen/pallas_call | solution.py:495
  11.1 3.5 %collective-permute-start.3 = (f32[22,8,384]{2,1,0:T(8,128)S(1)}, f32[22,8,384]{2,1,0:T(8,128)S(1)}, u32[]{:S(2)}, u32[]{:S(2)}) collective-permute-start(f32[22,8,384]{2,1,0:T(8,128)S(1)} %get-tuple-element.40), channel_id=1, source_target_pairs={{0,4},{4,8},{8,12},{1,5},{5,9},{9,13},{2,6},{6,10},{10,14},{3,7},{... | collective-permute-start | bytes 811016 | tf_op jit(solution)/shard_map/ppermute | solution.py:465
  14.6 1.3 %collective-permute-start.4 = (f32[22,8,384]{2,1,0:T(8,128)S(1)}, f32[22,8,384]{2,1,0:T(8,128)S(1)}, u32[]{:S(2)}, u32[]{:S(2)}) collective-permute-start(f32[22,8,384]{2,1,0:T(8,128)S(1)} %get-tuple-element.41), channel_id=1, source_target_pairs={{4,0},{8,4},{12,8},{5,1},{9,5},{13,9},{6,2},{10,6},{14,10},{7,3},{... | collective-permute-start | bytes 811016 | tf_op jit(solution)/shard_map/ppermute | solution.py:465
  15.9 2.3 %inner.1 = (f32[5,68,8,384]{3,2,1,0:T(8,128)S(1)}, f32[3,68,8,384]{3,2,1,0:T(8,128)S(1)}, f32[9,68,8,384]{3,2,1,0:T(8,128)S(1)}, f32[4,10,8,384]{3,2,1,0:T(8,128)S(1)}, f32[9,10,8,384]{3,2,1,0:T(8,128)S(1)}) custom-call(f32[36,8,384]{2,1,0:T(8,128)S(1)} %get-tuple-element.43.wide_ref), custom_call_target="tpu_custom_call" | custom-call | flops 20000000 | bytes 8000000 | tf_op jit(solution)/shard_map/inner/pallas_call | solution.py:516
  18.2 3.7 %collective-permute-start.5 = (f32[2,8,128]{2,1,0:T(8,128)S(1)}, f32[2,8,128]{2,1,0:T(8,128)S(1)}, u32[]{:S(2)}, u32[]{:S(2)}) collective-permute-start(f32[2,8,128]{2,1,0:T(8,128)S(1)} %get-tuple-element.56), channel_id=1, source_target_pairs={{0,8},{1,13},{2,10},{3,15},{4,12},{5,9},{6,14},{7,11},{8,0},{9,5},... | collective-permute-start | bytes 24584 | tf_op jit(solution)/shard_map/ppermute | solution.py:481
  21.9 0.0 collective-permute-done.3.above_ref
  21.9 2.4 %collective-permute-done.4.below_ref = f32[22,8,384]{2,1,0:T(8,128)S(1)} collective-permute-done((f32[22,8,384]{2,1,0:T(8,128)S(1)}, f32[22,8,384]{2,1,0:T(8,128)S(1)}, u32[]{:S(2)}, u32[]{:S(2)}) %collective-permute-start.4) | collective-permute-done | bytes 270368 | tf_op jit(solution)/shard_map/ppermute | solution.py:465
  24.3 2.4 %outer.1 = (f32[2,8,128]{2,1,0:T(8,128)S(1)}, f32[5,68,8,384]{3,2,1,0:T(8,128)S(1)}, f32[3,68,8,384]{3,2,1,0:T(8,128)S(1)}, f32[9,68,8,384]{3,2,1,0:T(8,128)S(1)...) custom-call(f32[22,8,384]{2,1,0:T(8,128)S(1)} %collective-permute-do, ...), custom_call_target="tpu_custom_call", output_to_operand_aliasing={{1}: (3, {}), {2}: (4, {}), {3}: (5, {}), {4}: (6, {}), {5}... | custom-call | flops 20000000 | bytes 8000000 | tf_op jit(solution)/shard_map/outer/pallas_call | solution.py:527
  26.7 0.0 collective-permute-done.5.refs_0_
  26.7 0.1 collective-permute-start.6
  27.4 0.5 %collective-permute-done.6.refs_1_ = f32[2,8,128]{2,1,0:T(8,128)S(1)} collective-permute-done((f32[2,8,128]{2,1,0:T(8,128)S(1)}, f32[2,8,128]{2,1,0:T(8,128)S(1)}, u32[]{:S(2)}, u32[]{:S(2)}) %collective-permute-start.6) | collective-permute-done | bytes 8224 | tf_op jit(solution)/shard_map/ppermute | solution.py:538
  28.0 9.6 %smooth.1 = (f32[256,256]{1,0:T(8,128)}, f32[5,68,8,384]{3,2,1,0:T(8,128)S(1)}, f32[3,68,8,384]{3,2,1,0:T(8,128)S(1)}, f32[9,68,8,384]{3,2,1,0:T(8,128)S(1)}, f3...) custom-call(f32[2,8,128]{2,1,0:T(8,128)S(1)} %get-tuple-element.57.p, ...), custom_call_target="tpu_custom_call", output_to_operand_aliasing={{1}: (4, {}), {2}: (5, {}), {3}: (6, {}), {4}: (7, {}), {5}... | custom-call | tf_op jit(solution)/shard_map/smooth/pallas_call | solution.py:539
  (1 shorter events, 0.0 us)
Async XLA Ops:
  0.0 0.9 %copy-start = (f32[8,32,256]{2,1,0:T(8,128)S(1)}, f32[8,32,256]{2,1,0:T(8,128)}, u32[]{:S(2)}) copy-start(f32[8,32,256]{2,1,0:T(8,128)} %param.3) | copy-start | bytes 786436
  1.0 0.7 %copy-start.1 = (s32[2,4,32]{2,1,0:T(4,128)S(1)}, s32[2,4,32]{2,1,0:T(4,128)}, u32[]{:S(2)}) copy-start(s32[2,4,32]{2,1,0:T(4,128)} %mask_ref.1) | copy-start | bytes 3076
  1.9 6.8 %collective-permute-start = (f32[11,8,128]{2,1,0:T(8,128)S(1)}, f32[11,8,128]{2,1,0:T(8,128)S(1)}, u32[]{:S(2)}, u32[]{:S(2)}) collective-permute-start(f32[11,8,128]{2,1,0:T(8,128)S(1)} %get-tuple-element.36), channel_id=1, source_target_pairs={{0,1},{1,2},{2,3},{3,0},{4,5},{5,6},{6,7},{7,4},{8,9},{9,10},{10,1... | collective-permute-start | bytes 135176 | tf_op jit(solution)/shard_map/ppermute | solution.py:461
  2.4 6.3 %collective-permute-start.1 = (f32[11,8,128]{2,1,0:T(8,128)S(1)}, f32[11,8,128]{2,1,0:T(8,128)S(1)}, u32[]{:S(2)}, u32[]{:S(2)}) collective-permute-start(f32[11,8,128]{2,1,0:T(8,128)S(1)} %get-tuple-element.37), channel_id=1, source_target_pairs={{0,3},{1,0},{2,1},{3,2},{4,7},{5,4},{6,5},{7,6},{8,11},{9,8},{10,9... | collective-permute-start | bytes 135176 | tf_op jit(solution)/shard_map/ppermute | solution.py:461
  4.4 4.3 %collective-permute-start.2 = (f32[2,8,128]{2,1,0:T(8,128)S(1)}, f32[2,8,128]{2,1,0:T(8,128)S(1)}, u32[]{:S(2)}, u32[]{:S(2)}) collective-permute-start(f32[2,8,128]{2,1,0:T(8,128)S(1)} %get-tuple-element.38.refs_0_), channel_id=1, source_target_pairs={{0,2},{1,3},{2,0},{3,1},{4,6},{5,7},{6,4},{7,5},{8,10},{9,11},{10,... | collective-permute-start | bytes 24584 | tf_op jit(solution)/shard_map/ppermute | solution.py:461
  11.1 10.9 %collective-permute-start.3 = (f32[22,8,384]{2,1,0:T(8,128)S(1)}, f32[22,8,384]{2,1,0:T(8,128)S(1)}, u32[]{:S(2)}, u32[]{:S(2)}) collective-permute-start(f32[22,8,384]{2,1,0:T(8,128)S(1)} %get-tuple-element.40), channel_id=1, source_target_pairs={{0,4},{4,8},{8,12},{1,5},{5,9},{9,13},{2,6},{6,10},{10,14},{3,7},{... | collective-permute-start | bytes 811016 | tf_op jit(solution)/shard_map/ppermute | solution.py:465
  14.6 9.7 %collective-permute-start.4 = (f32[22,8,384]{2,1,0:T(8,128)S(1)}, f32[22,8,384]{2,1,0:T(8,128)S(1)}, u32[]{:S(2)}, u32[]{:S(2)}) collective-permute-start(f32[22,8,384]{2,1,0:T(8,128)S(1)} %get-tuple-element.41), channel_id=1, source_target_pairs={{4,0},{8,4},{12,8},{5,1},{9,5},{13,9},{6,2},{10,6},{14,10},{7,3},{... | collective-permute-start | bytes 811016 | tf_op jit(solution)/shard_map/ppermute | solution.py:465
  18.2 8.5 %collective-permute-start.5 = (f32[2,8,128]{2,1,0:T(8,128)S(1)}, f32[2,8,128]{2,1,0:T(8,128)S(1)}, u32[]{:S(2)}, u32[]{:S(2)}) collective-permute-start(f32[2,8,128]{2,1,0:T(8,128)S(1)} %get-tuple-element.56), channel_id=1, source_target_pairs={{0,8},{1,13},{2,10},{3,15},{4,12},{5,9},{6,14},{7,11},{8,0},{9,5},... | collective-permute-start | bytes 24584 | tf_op jit(solution)/shard_map/ppermute | solution.py:481
  26.7 1.2 %collective-permute-start.6 = (f32[2,8,128]{2,1,0:T(8,128)S(1)}, f32[2,8,128]{2,1,0:T(8,128)S(1)}, u32[]{:S(2)}, u32[]{:S(2)}) collective-permute-start(f32[2,8,128]{2,1,0:T(8,128)S(1)} %collective-permute-done.5.refs_0_), channel_id=1, source_target_pairs={{0,1},{1,0},{2,3},{3,2},{4,5},{5,4},{6,7},{7,6},{8,9},{9,8},{10,11... | collective-permute-start | bytes 24584 | tf_op jit(solution)/shard_map/ppermute | solution.py:538

commit v4 on v3

--- a/solution.py
+++ b/solution.py
@@ -28,19 +28,58 @@
     return pltpu.roll(x, by % 8, 0)
 
 
-def permuted(x, source, count):
-    lane = lax.broadcasted_iota(jnp.int32, (8, 128), 1)
-    result = []
-    for t in range(count):
-        column = source(t, lane)
-        index = lax.rem(column, 128)
-        home = lax.div(column, 128)
-        total = None
-        for i, v in enumerate(x):
-            part = jnp.take_along_axis(v, index, axis=1, mode="promise_in_bounds")
-            total = part if total is None else jnp.where(home == i, part, total)
-        result.append(total)
-    return result
+def picked(x, index):
+    return jnp.take_along_axis(x, index, axis=1, mode="promise_in_bounds")
+
+
+class Ring:
+    def __init__(self, tiles):
+        self.tiles = tiles
+        lane = iotas()[1]
+        self.lane = lane
+        column = [lane * tiles + t for t in range(tiles)]
+        self.index = [lax.rem(c, 128) for c in column]
+        self.home = [lax.div(c, 128) for c in column]
+
+    def own(self, x):
+        result = []
+        for index, home in zip(self.index, self.home):
+            total = picked(x[0], index)
+            for i in range(1, len(x)):
+                total = jnp.where(home == i, picked(x[i], index), total)
+            result.append(total)
+        return result
+
+    def edges(self, x, edge):
+        last = self.tiles - 1
+        return [
+            jnp.where(home == last, picked(edge, index), v)
+            for v, index, home in zip(x, self.index, self.home)
+        ]
+
+    def unpacked(self, left, right, group):
+        edge = jnp.where(self.lane < HALO, lane_roll(right, -32 * group), 0.0)
+        return jnp.where(self.lane >= 128 - HALO, lane_roll(left, 32 * (3 - group)), edge)
+
+    def plain(self, x, count):
+        result = []
+        for t in range(count):
+            column = self.lane + 128 * t
+            index, home = lax.div(column, self.tiles), lax.rem(column, self.tiles)
+            total = picked(x[0], index)
+            for i in range(1, self.tiles):
+                total = jnp.where(home == i, picked(x[i], index), total)
+            result.append(total)
+        return result
+
+
+def split(ref, row, tiles):
+    return [ref[row, :, t * 128 : (t + 1) * 128] for t in range(tiles)]
+
+
+def put(ref, row, x):
+    for t, v in enumerate(x):
+        ref[row, :, t * 128 : (t + 1) * 128] = v
 
 
 def pack_kernel(vol_ref, mask_ref, own_ref, low_ref, high_ref, sums_ref, stage):
@@ -94,49 +133,58 @@
         ref[packs + 1] = count
 
 
-def sums_kernel(left_ref, right_ref, *refs):
+def half_kernel(left_ref, right_ref, own_ref, *refs):
     packs = left_ref.shape[0] - 2
-    ends_ref, all_ref = refs[-1], refs[-2]
+    odd = lax.rem(lax.axis_index("gx"), 2).astype(F32)
+    for i in range(2):
+        left, right = left_ref[packs + i], right_ref[packs + i]
+        if len(refs) == 1:
+            refs[-1][i] = own_ref[i] + left * (1.0 - odd) + right * odd
+        else:
+            refs[-1][i] = 0.5 * functools.reduce(
+                jnp.add, [ref[i] for ref in refs[:-1]], own_ref[i] + left + right
+            )
+
+
+def whole_kernel(half_ref, other_ref, sums_ref, ends_ref):
     place, last = lax.axis_index("gy"), lax.axis_size("gy") - 1
     at_end = ((place == 0) | (place == last)).astype(F32)
     for i in range(2):
-        s = left_ref[packs + i] + right_ref[packs + i]
-        for ref in refs[:-2]:
-            s = s + ref[i]
-        all_ref[i] = s
-        ends_ref[i] = s * jnp.where(lax.axis_index("gx") % 2 == 0, 1.0, at_end)
-
-
-def widen_kernel(own_ref, left_ref, right_ref, sums_ref, wide_ref, top_ref, bottom_ref):
-    cols = own_ref.shape[2]
-    count = own_ref.shape[0]
-    blocks = count // 9
-    rows = count - blocks
-    packs = count // 4
-    tiles = cols // 128 + 1
-    _, lane = iotas()
+        sums_ref[i] = half_ref[i] + other_ref[i]
+        ends_ref[i] = sums_ref[i] * jnp.where(lax.rem(lax.axis_index("gx"), 2) == 0, 1.0, at_end)
+
+
+def order_kernel(own_ref, wide_ref):
+    tiles = own_ref.shape[2] // 128
+    ring = Ring(tiles + 1)
+    for i in range(own_ref.shape[0]):
+        put(wide_ref, i, ring.own(split(own_ref, i, tiles)))
+
+
+def widen_kernel(part_ref, left_ref, right_ref, half_ref, wide_ref, top_ref, bottom_ref):
+    tiles = wide_ref.shape[2] // 128
+    count = wide_ref.shape[0]
+    rows = count - count // 9
+    ring = Ring(tiles)
     place = lax.axis_index("gx")
     has_left = (place > 0).astype(F32)
     has_right = (place < lax.axis_size("gx") - 1).astype(F32)
-    for k in range(packs):
+    for k in range(count // 4):
         left = left_ref[k] * has_left
         right = right_ref[k] * has_right
         for g in range(4):
-            edge = jnp.where(lane < HALO, lane_roll(right, -32 * g), 0.0)
-            edge = jnp.where(lane >= 128 - HALO, lane_roll(left, 32 * (3 - g)), edge)
-            row = [own_ref[4 * k + g, :, t * 128 : (t + 1) * 128] for t in range(tiles - 1)]
-            row = permuted(row + [edge], lambda t, l: l * tiles + t, tiles)
-            for t in range(tiles):
-                wide_ref[4 * k + g, :, t * 128 : (t + 1) * 128] = row[t]
-    top_ref[0:HALO] = wide_ref[0:HALO]
-    bottom_ref[0:HALO] = wide_ref[rows - HALO : rows]
-    top_ref[HALO : HALO + 3] = wide_ref[rows : rows + 3]
-    bottom_ref[HALO : HALO + 3] = wide_ref[count - 3 : count]
-    for i in range(2):
-        for ref in (top_ref, bottom_ref):
-            ref[HALO + 3, :, i * 128 : (i + 1) * 128] = sums_ref[i]
-    for ref in (top_ref, bottom_ref):
-        ref[HALO + 3, :, 256:] = jnp.zeros((8, ref.shape[2] - 256), F32)
+            i = 4 * k + g
+            put(wide_ref, i, ring.edges(split(part_ref, i, tiles), ring.unpacked(left, right, g)))
+    sub = iotas()[0]
+    for ref, row, block in ((top_ref, 0, rows), (bottom_ref, rows - HALO, count - 3)):
+        ref[0:HALO] = wide_ref[row : row + HALO]
+        packed = [jnp.zeros((8, 128), F32)] * tiles
+        for b in range(3):
+            for i in range(2):
+                some = [v[4 * i : 4 * i + 1] for v in split(wide_ref, block + b, tiles)]
+                packed = [jnp.where(sub == 2 * b + i, x, y) for x, y in zip(some, packed)]
+        put(ref, HALO, packed)
+        put(ref, HALO + 1, [half_ref[0], half_ref[1]] + [packed[0]] * (tiles - 2))
 
 
 FIELDS = [(0, 8), (1, -8), (1, 0), (1, 8), (2, 8), (2, 0), (3, -8), (3, 0), (3, 8)]
@@ -332,8 +380,7 @@
                     )
                 new = []
                 for t in range(self.tiles):
-                    d = result[0][t] + own[t] + (1.0 - own[t])
-                    n = result[1][t] + own[t] * centre[t]
+                    n, d = result[1][t] + centre[t], result[0][t] + 1.0
                     new.append(jnp.where(own[t] > 0.0, n / d, centre[t]))
                 put(y, new)
 
@@ -356,7 +403,7 @@
     steps.run([low + 1], rows - 2, 8, steps.distances(LEVEL))
 
 
-def outer_kernel(above_ref, below_ref, sums_ref, *refs):
+def outer_kernel(above_ref, below_ref, *refs):
     part_ref, val, cor, dist, tis, pair = refs[5:]
     full = val.shape[1]
     rows = full - 2 * HALO
@@ -364,16 +411,25 @@
     low, high = HALO, HALO + rows
     steps = Steps(val, cor, dist, tis, pair)
 
-    val[0, 0:low] = above_ref[0:HALO]
-    val[0, high:full] = below_ref[0:HALO]
-    tis[0, 0:3] = above_ref[HALO : HALO + 3]
-    tis[0, spans - 3 :] = below_ref[HALO : HALO + 3]
+    for ref, row, block in ((above_ref, 0, 0), (below_ref, high, spans - 3)):
+        val[0, row : row + HALO] = ref[0:HALO]
+        packed = split(ref, HALO, steps.tiles)
+        for b in range(3):
+            steps.store(
+                tis,
+                [
+                    jnp.where(steps.sub < 4, v[2 * b : 2 * b + 1], v[2 * b + 1 : 2 * b + 2])
+                    for v in packed
+                ],
+                0,
+                block + b,
+            )
     ends = [*range(0, 3), *range(spans - 3, spans)]
     steps.tissue(ends)
     steps.pairs([*range(0, 3), *range(spans - 4, spans - 1)], ends)
     for i in range(2):
         lanes = slice(i * 128, (i + 1) * 128)
-        part_ref[i] = sums_ref[i] + above_ref[HALO + 3, :, lanes] + below_ref[HALO + 3, :, lanes]
+        part_ref[i] = above_ref[HALO + 1, :, lanes] + below_ref[HALO + 1, :, lanes]
 
     steps.run([0, high], HALO, 6, steps.prepare(0))
     steps.run([1, high - 1], HALO, 6, steps.corrections)
@@ -381,7 +437,7 @@
     steps.run([OUT, high - 1], low + 1 - OUT, 5, steps.distances(LEVEL))
 
 
-def smooth_kernel(fars, part_ref, smoothing_ref, *refs):
+def smooth_kernel(fars, sums_ref, smoothing_ref, *refs):
     far_refs, refs = refs[:fars], refs[fars + 5 :]
     out_ref, val, cor, dist, tis, pair, stage = refs
     cols = out_ref.shape[1]
@@ -389,11 +445,12 @@
     rows = full - 2 * HALO
     low = HALO
     steps = Steps(val, cor, dist, tis, pair)
+    ring = Ring(steps.tiles)
 
     total, number = [
         jnp.sum(
             jnp.sum(
-                functools.reduce(jnp.add, [ref[i] for ref in (part_ref, *far_refs)]),
+                functools.reduce(jnp.add, [ref[i] for ref in (sums_ref, *far_refs)]),
                 axis=1,
                 keepdims=True,
             ),
@@ -411,22 +468,18 @@
         steps.store(val, new, 4, y)
 
     def finish(y, new):
-        column = lambda t, l: l + 128 * t
-        where = lambda t, l: lax.rem(column(t, l), steps.tiles) * 128 + lax.div(
-            column(t, l), steps.tiles
-        )
-        for t, x in enumerate(permuted(new, where, cols // 128)):
+        for t, x in enumerate(ring.plain(new, cols // 128)):
             stage[t, pl.ds(y - HALO, 8, stride=rows), :] = x
 
-    steps.run([OUT - 8], 8, 2, steps.early(factor))
-    steps.run([OUT], full - 2 * OUT, 2, steps.combine(factor, keep))
+    steps.run([OUT - 8], 8, 4, steps.early(factor))
+    steps.run([OUT], full - 2 * OUT, 5, steps.combine(factor, keep))
 
     steps.run([OUT], full - 2 * OUT, 10, steps.prepare(4))
     steps.run([OUT + 1], full - 2 * OUT - 2, 8, steps.corrections)
     steps.run([low - 8], rows + 8, 8, steps.distances(APART))
     steps.run([low], rows, 8, steps.distances(LEVEL))
-    steps.run([low - 8], 8, 2, steps.early(factor))
-    steps.run([low], rows, 4, steps.combine(factor, finish))
+    steps.run([low - 8], 8, 4, steps.early(factor))
+    steps.run([low], rows, 8, steps.combine(factor, finish))
     for t in range(cols // 128):
         out_ref[:, t * 128 : (t + 1) * 128] = stage[t]
 
@@ -467,6 +520,9 @@
     def beyond(x, axis):
         return [ring(x, axis, by) for by in range(2, lax.axis_size(axis) - 1)]
 
+    def swap(x):
+        return lax.ppermute(x, "gx", [(c, c ^ 1) for c in range(lax.axis_size("gx"))])
+
     def far_rows(x, ends):
         ny, nx = lax.axis_size("gy"), lax.axis_size("gx")
         shifts = list(range(2, ny - 1)) + [None]
@@ -483,27 +539,38 @@
 
     right = ring(low, "gx", -1)
     left = ring(high, "gx", 1)
-    far = beyond(sums, "gx")
-    sums, ends = pl.pallas_call(
-        sums_kernel,
-        out_shape=[shape(2, 8, 128)] * 2,
+    far = [] if lax.axis_size("gx") == 4 else beyond(sums, "gx")
+    ordered = pl.pallas_call(
+        order_kernel,
+        out_shape=shape(count, 8, lanes),
+        in_specs=[vm],
+        out_specs=vm,
+        compiler_params=params,
+        cost_estimate=pl.CostEstimate(flops=5_000_000, bytes_accessed=1_000_000, transcendentals=0),
+        name="order",
+    )(own)
+    half = pl.pallas_call(
+        half_kernel,
+        out_shape=shape(2, 8, 128),
         in_specs=[vm] * (3 + len(far)),
-        out_specs=[vm] * 2,
-        compiler_params=params,
-        name="sums",
+        out_specs=vm,
+        compiler_params=params,
+        name="half",
     )(left, right, sums, *far)
+    other = swap(half)
     wide, top, bottom = pl.pallas_call(
         widen_kernel,
         out_shape=(
             shape(count, 8, lanes),
-            shape(HALO + 4, 8, lanes),
-            shape(HALO + 4, 8, lanes),
+            shape(HALO + 2, 8, lanes),
+            shape(HALO + 2, 8, lanes),
         ),
         in_specs=[vm] * 4,
         out_specs=[vm] * 3,
+        input_output_aliases={0: 0},
         compiler_params=params,
         name="widen",
-    )(own, left, right, sums)
+    )(ordered, left, right, half)
     below = line(top, "gy", -1)
     above = line(bottom, "gy", 1)
     state = [
@@ -522,20 +589,28 @@
         cost_estimate=pl.CostEstimate(flops=20_000_000, bytes_accessed=8_000_000, transcendentals=0),
         name="inner",
     )(wide)
-    sums, ends, *held = lax.optimization_barrier((sums, ends, *held))
+    other, *held = lax.optimization_barrier((other, *held))
+    sums, ends = pl.pallas_call(
+        whole_kernel,
+        out_shape=[shape(2, 8, 128)] * 2,
+        in_specs=[vm] * 2,
+        out_specs=[vm] * 2,
+        compiler_params=params,
+        name="whole",
+    )(half, other)
     far = far_rows(sums, ends)
     part, *held = pl.pallas_call(
         outer_kernel,
         out_shape=[shape(2, 8, 128)] + state,
-        in_specs=[vm] * 8,
+        in_specs=[vm] * 7,
         out_specs=[vm] * 6,
-        input_output_aliases={3 + i: 1 + i for i in range(5)},
+        input_output_aliases={2 + i: 1 + i for i in range(5)},
         compiler_params=params,
         cost_estimate=pl.CostEstimate(flops=20_000_000, bytes_accessed=8_000_000, transcendentals=0),
         name="outer",
-    )(above, below, sums, *held)
+    )(above, below, *held)
     part, far = lax.optimization_barrier((part, far))
-    far = [far, lax.ppermute(far, "gx", [(c, c ^ 1) for c in range(lax.axis_size("gx"))])]
+    far = [part, swap(part), far, swap(far)]
     out = pl.pallas_call(
         functools.partial(smooth_kernel, len(far)),
         out_shape=[shape(depth * rows, cols)] + state,
@@ -545,7 +620,7 @@
         scratch_shapes=[pltpu.VMEM((cols // 128, depth * rows, 128), F32)],
         compiler_params=params,
         name="smooth",
-    )(part, smoothing, *far, *held)[0]
+    )(sums, smoothing, *far, *held)[0]
     return out.reshape(depth, rows, cols)
 
 

time: 37.8 us -> 34.4 us (0.910)
  Pallas kernels: 16.9 us -> 15 us
  waiting for transfers between devices: 5 us -> 3.59 us
    ppermute x3 -> x2, starting transfers between devices: 4.74 us -> 2.49 us  [ring(): return lax.ppermute(x, axis, [(i, (i + by) % size) for i in range(size)])]
    ppermute x1 -> x3, starting transfers between devices: 0.07 us -> 1.96 us  [swap(): lax.ppermute(x, 'gx', [(c, c ^ 1) for c in range(lax.axis_size('gx'))])]
    pallas_call x1, Pallas kernels: 2.3 us -> 1.05 us  [on_device(): pl.pallas_call(widen_kernel, out_shape=(shape(count, 8, lanes), shape(HAL...]
    pallas_call x1, Pallas kernels: 9.61 us -> 8.43 us  [on_device(): pl.pallas_call(functools.partial(smooth_kernel, len(far)), out_shape=[sha...]
    ppermute x3 -> x2, waiting for transfers between devices: 2.11 us -> 1.38 us  [ring(): return lax.ppermute(x, axis, [(i, (i + by) % size) for i in range(size)])]
    pallas_call x1 -> x3, Pallas kernels: 0.01 us -> 0.61 us  [the longest x1 0.58 us: on_device(): pl.pallas_call(order_kernel, out_shape=shape(count, 8, lanes), in_specs=[...]
    ppermute x2, starting transfers between devices: 4.84 us -> 5.3 us  [line(): lax.ppermute(x, axis, [(i, i + by) for i in range(size) if 0 <= i + by <...]
  transfers between devices with their start and end apart: 7 -> 8, of which waited for: 3 -> 4; matrix products, arithmetic and copies ran while one was open for 0% -> 0% of each run, Pallas kernels for 12% -> 15%
where the time goes in v4:
time: 34.4 us; the launch traced here: 34.2 us
  Pallas kernels  15 us (44%)
  starting transfers between devices  13.2 us (38%)
  waiting for transfers between devices  3.59 us (10%)
  local copies, waits for them, and re-layouts  1.64 us (5%)
  between operations  0.73 us (2%)
    pallas_call x1, Pallas kernels, on_device(): pl.pallas_call(functools.partial(smooth_kernel, len(far)), out_shape=[sha...  8.43 us
    ppermute x2, starting transfers between devices, line(): lax.ppermute(x, axis, [(i, i + by) for i in range(size) if 0 <= i + by <...  5.3 us
    ppermute x1, starting transfers between devices, far_rows(): got.append(lax.ppermute(ends if odd is None else x, ('gy', 'gx'), pairs))  3.43 us
    ppermute x2, starting transfers between devices, ring(): return lax.ppermute(x, axis, [(i, (i + by) % size) for i in range(size)])  2.49 us
    pallas_call x1, Pallas kernels, on_device(): pl.pallas_call(outer_kernel, out_shape=[shape(2, 8, 128)] + state, in_spe...  2.42 us
    pallas_call x1, Pallas kernels, on_device(): pl.pallas_call(inner_kernel, out_shape=state, in_specs=[vm], out_specs=[v...  2.28 us
    ppermute x2, waiting for transfers between devices, line(): lax.ppermute(x, axis, [(i, i + by) for i in range(size) if 0 <= i + by <...  2.03 us
    ppermute x3, starting transfers between devices, swap(): lax.ppermute(x, 'gx', [(c, c ^ 1) for c in range(lax.axis_size('gx'))])  1.96 us
  transfers between devices with their start and end apart: 8, of which 4 were waited for; matrix products, arithmetic and copies ran while one was open for 0% of the time, Pallas kernels for 15%

profile of v4, /device:TPU:0, one launch (start us, length us, event | category | flops | bytes accessed | tf_op | source)
XLA Modules:
  0.0 34.2 jit_solution(7875453907542361104)
XLA Ops:
  0.0 0.0 copy-start
  0.0 0.9 %copy-done = f32[8,32,256]{2,1,0:T(8,128)S(1)} copy-done((f32[8,32,256]{2,1,0:T(8,128)S(1)}, f32[8,32,256]{2,1,0:T(8,128)}, u32[]{:S(2)}) %copy-start) | copy-done | bytes 262168
  1.0 0.0 copy-start.1
  1.0 0.7 %copy-done.1 = s32[2,4,32]{2,1,0:T(4,128)S(1)} copy-done((s32[2,4,32]{2,1,0:T(4,128)S(1)}, s32[2,4,32]{2,1,0:T(4,128)}, u32[]{:S(2)}) %copy-start.1) | copy-done | bytes 1048
  1.6 0.3 pack.1
  1.9 0.5 %collective-permute-start = (f32[11,8,128]{2,1,0:T(8,128)S(1)}, f32[11,8,128]{2,1,0:T(8,128)S(1)}, u32[]{:S(2)}, u32[]{:S(2)}) collective-permute-start(f32[11,8,128]{2,1,0:T(8,128)S(1)} %get-tuple-element.34), channel_id=1, source_target_pairs={{0,1},{1,2},{2,3},{3,0},{4,5},{5,6},{6,7},{7,4},{8,9},{9,10},{10,1... | collective-permute-start | bytes 135176 | tf_op jit(solution)/shard_map/ppermute | solution.py:514
  2.4 2.0 %collective-permute-start.1 = (f32[11,8,128]{2,1,0:T(8,128)S(1)}, f32[11,8,128]{2,1,0:T(8,128)S(1)}, u32[]{:S(2)}, u32[]{:S(2)}) collective-permute-start(f32[11,8,128]{2,1,0:T(8,128)S(1)} %get-tuple-element.35), channel_id=1, source_target_pairs={{0,3},{1,0},{2,1},{3,2},{4,7},{5,4},{6,5},{7,6},{8,11},{9,8},{10,9... | collective-permute-start | bytes 135176 | tf_op jit(solution)/shard_map/ppermute | solution.py:514
  4.4 0.6 %order.1.part_ref = f32[36,8,384]{2,1,0:T(8,128)S(1)} custom-call(f32[36,8,256]{2,1,0:T(8,128)S(1)} %get-tuple-element.37.own_ref), custom_call_target="tpu_custom_call" | custom-call | flops 5000000 | bytes 1000000 | tf_op jit(solution)/shard_map/order/pallas_call | solution.py:543
  5.0 1.1 %collective-permute-done.left_ref = f32[11,8,128]{2,1,0:T(8,128)S(1)} collective-permute-done((f32[11,8,128]{2,1,0:T(8,128)S(1)}, f32[11,8,128]{2,1,0:T(8,128)S(1)}, u32[]{:S(2)}, u32[]{:S(2)}) %collective-permute-start) | collective-permute-done | bytes 45088 | tf_op jit(solution)/shard_map/ppermute | solution.py:514
  6.1 0.3 collective-permute-done.1.right_ref
  6.4 1.1 %widen.1 = (f32[36,8,384]{2,1,0:T(8,128)S(1)}, f32[20,8,384]{2,1,0:T(8,128)S(1)}, f32[20,8,384]{2,1,0:T(8,128)S(1)}) custom-call(f32[36,8,384]{2,1,0:T(8,128)S(1)} %order.1.part_ref, f32[11,8,128]{2,1,0:T(8,128)S(1)} %collective-permute-done.left_ref, f32[11,8,128]{2,1,0:T(8,128)S(1)} %collective-permute-done.1.right_ref, ...), custom_call_target="tpu_custom_call", output_to_operand_aliasing={{0}: (0, {})} | custom-call | tf_op jit(solution)/shard_map/widen/pallas_call | solution.py:561
  7.4 4.0 %collective-permute-start.3 = (f32[20,8,384]{2,1,0:T(8,128)S(1)}, f32[20,8,384]{2,1,0:T(8,128)S(1)}, u32[]{:S(2)}, u32[]{:S(2)}) collective-permute-start(f32[20,8,384]{2,1,0:T(8,128)S(1)} %get-tuple-element.46), channel_id=1, source_target_pairs={{0,4},{4,8},{8,12},{1,5},{5,9},{9,13},{2,6},{6,10},{10,14},{3,7},{... | collective-permute-start | bytes 737288 | tf_op jit(solution)/shard_map/ppermute | solution.py:518
  11.5 1.3 %collective-permute-start.4 = (f32[20,8,384]{2,1,0:T(8,128)S(1)}, f32[20,8,384]{2,1,0:T(8,128)S(1)}, u32[]{:S(2)}, u32[]{:S(2)}) collective-permute-start(f32[20,8,384]{2,1,0:T(8,128)S(1)} %get-tuple-element.47), channel_id=1, source_target_pairs={{4,0},{8,4},{12,8},{5,1},{9,5},{13,9},{6,2},{10,6},{14,10},{7,3},{... | collective-permute-start | bytes 737288 | tf_op jit(solution)/shard_map/ppermute | solution.py:518
  12.8 1.4 %collective-permute-start.2 = (f32[2,8,128]{2,1,0:T(8,128)S(1)}, f32[2,8,128]{2,1,0:T(8,128)S(1)}, u32[]{:S(2)}, u32[]{:S(2)}) collective-permute-start(f32[2,8,128]{2,1,0:T(8,128)S(1)} %half.1.half_ref), channel_id=1, source_target_pairs={{0,1},{1,0},{2,3},{3,2},{4,5},{5,4},{6,7},{7,6},{8,9},{9,8},{10,11... | collective-permute-start | bytes 24584 | tf_op jit(solution)/shard_map/ppermute | solution.py:524
  14.1 2.3 %inner.1 = (f32[5,68,8,384]{3,2,1,0:T(8,128)S(1)}, f32[3,68,8,384]{3,2,1,0:T(8,128)S(1)}, f32[9,68,8,384]{3,2,1,0:T(8,128)S(1)}, f32[4,10,8,384]{3,2,1,0:T(8,128)S(1)}, f32[9,10,8,384]{3,2,1,0:T(8,128)S(1)}) custom-call(f32[36,8,384]{2,1,0:T(8,128)S(1)} %get-tuple-element.38.wide_ref), custom_call_target="tpu_custom_call" | custom-call | flops 20000000 | bytes 8000000 | tf_op jit(solution)/shard_map/inner/pallas_call | solution.py:583
  16.4 0.0 collective-permute-done.2.other_ref
  16.5 3.4 %collective-permute-start.5 = (f32[2,8,128]{2,1,0:T(8,128)S(1)}, f32[2,8,128]{2,1,0:T(8,128)S(1)}, u32[]{:S(2)}, u32[]{:S(2)}) collective-permute-start(f32[2,8,128]{2,1,0:T(8,128)S(1)} %get-tuple-element.54), channel_id=1, source_target_pairs={{0,8},{1,13},{2,10},{3,15},{4,12},{5,9},{6,14},{7,11},{8,0},{9,5},... | collective-permute-start | bytes 24584 | tf_op jit(solution)/shard_map/ppermute | solution.py:537
  19.9 0.0 collective-permute-done.3.above_ref
  19.9 2.0 %collective-permute-done.4.below_ref = f32[20,8,384]{2,1,0:T(8,128)S(1)} collective-permute-done((f32[20,8,384]{2,1,0:T(8,128)S(1)}, f32[20,8,384]{2,1,0:T(8,128)S(1)}, u32[]{:S(2)}, u32[]{:S(2)}) %collective-permute-start.4) | collective-permute-done | bytes 245792 | tf_op jit(solution)/shard_map/ppermute | solution.py:518
  21.9 2.4 %outer.1 = (f32[2,8,128]{2,1,0:T(8,128)S(1)}, f32[5,68,8,384]{3,2,1,0:T(8,128)S(1)}, f32[3,68,8,384]{3,2,1,0:T(8,128)S(1)}, f32[9,68,8,384]{3,2,1,0:T(8,128)S(1)...) custom-call(f32[20,8,384]{2,1,0:T(8,128)S(1)} %collective-permute-do, ...), custom_call_target="tpu_custom_call", output_to_operand_aliasing={{1}: (2, {}), {2}: (3, {}), {3}: (4, {}), {4}: (5, {}), {5}... | custom-call | flops 20000000 | bytes 8000000 | tf_op jit(solution)/shard_map/outer/pallas_call | solution.py:602
  24.3 0.0 collective-permute-done.5.refs_2_
  24.4 0.2 collective-permute-start.6
  24.5 0.4 %collective-permute-start.7 = (f32[2,8,128]{2,1,0:T(8,128)S(1)}, f32[2,8,128]{2,1,0:T(8,128)S(1)}, u32[]{:S(2)}, u32[]{:S(2)}) collective-permute-start(f32[2,8,128]{2,1,0:T(8,128)S(1)} %collective-permute-done.5.refs_2_), channel_id=1, source_target_pairs={{0,1},{1,0},{2,3},{3,2},{4,5},{5,4},{6,7},{7,6},{8,9},{9,8},{10,11... | collective-permute-start | bytes 24584 | tf_op jit(solution)/shard_map/ppermute | solution.py:524
  25.6 0.0 collective-permute-done.6.refs_1_
  25.6 0.2 collective-permute-done.7.refs_3_
  25.8 8.4 %smooth.1 = (f32[256,256]{1,0:T(8,128)}, f32[5,68,8,384]{3,2,1,0:T(8,128)S(1)}, f32[3,68,8,384]{3,2,1,0:T(8,128)S(1)}, f32[9,68,8,384]{3,2,1,0:T(8,128)S(1)}, f3...) custom-call(f32[2,8,128]{2,1,0:T(8,128)S(1)} %get-tuple-element.45.s, ...), custom_call_target="tpu_custom_call", output_to_operand_aliasing={{1}: (6, {}), {2}: (7, {}), {3}: (8, {}), {4}: (9, {}), {5}... | custom-call | tf_op jit(solution)/shard_map/smooth/pallas_call | solution.py:614
  (2 shorter events, 0.0 us)
Async XLA Ops:
  0.0 0.9 %copy-start = (f32[8,32,256]{2,1,0:T(8,128)S(1)}, f32[8,32,256]{2,1,0:T(8,128)}, u32[]{:S(2)}) copy-start(f32[8,32,256]{2,1,0:T(8,128)} %param.3) | copy-start | bytes 786436
  1.0 0.7 %copy-start.1 = (s32[2,4,32]{2,1,0:T(4,128)S(1)}, s32[2,4,32]{2,1,0:T(4,128)}, u32[]{:S(2)}) copy-start(s32[2,4,32]{2,1,0:T(4,128)} %mask_ref.1) | copy-start | bytes 3076
  1.9 4.2 %collective-permute-start = (f32[11,8,128]{2,1,0:T(8,128)S(1)}, f32[11,8,128]{2,1,0:T(8,128)S(1)}, u32[]{:S(2)}, u32[]{:S(2)}) collective-permute-start(f32[11,8,128]{2,1,0:T(8,128)S(1)} %get-tuple-element.34), channel_id=1, source_target_pairs={{0,1},{1,2},{2,3},{3,0},{4,5},{5,6},{6,7},{7,4},{8,9},{9,10},{10,1... | collective-permute-start | bytes 135176 | tf_op jit(solution)/shard_map/ppermute | solution.py:514
  2.4 4.0 %collective-permute-start.1 = (f32[11,8,128]{2,1,0:T(8,128)S(1)}, f32[11,8,128]{2,1,0:T(8,128)S(1)}, u32[]{:S(2)}, u32[]{:S(2)}) collective-permute-start(f32[11,8,128]{2,1,0:T(8,128)S(1)} %get-tuple-element.35), channel_id=1, source_target_pairs={{0,3},{1,0},{2,1},{3,2},{4,7},{5,4},{6,5},{7,6},{8,11},{9,8},{10,9... | collective-permute-start | bytes 135176 | tf_op jit(solution)/shard_map/ppermute | solution.py:514
  7.4 12.5 %collective-permute-start.3 = (f32[20,8,384]{2,1,0:T(8,128)S(1)}, f32[20,8,384]{2,1,0:T(8,128)S(1)}, u32[]{:S(2)}, u32[]{:S(2)}) collective-permute-start(f32[20,8,384]{2,1,0:T(8,128)S(1)} %get-tuple-element.46), channel_id=1, source_target_pairs={{0,4},{4,8},{8,12},{1,5},{5,9},{9,13},{2,6},{6,10},{10,14},{3,7},{... | collective-permute-start | bytes 737288 | tf_op jit(solution)/shard_map/ppermute | solution.py:518
  11.5 10.5 %collective-permute-start.4 = (f32[20,8,384]{2,1,0:T(8,128)S(1)}, f32[20,8,384]{2,1,0:T(8,128)S(1)}, u32[]{:S(2)}, u32[]{:S(2)}) collective-permute-start(f32[20,8,384]{2,1,0:T(8,128)S(1)} %get-tuple-element.47), channel_id=1, source_target_pairs={{4,0},{8,4},{12,8},{5,1},{9,5},{13,9},{6,2},{10,6},{14,10},{7,3},{... | collective-permute-start | bytes 737288 | tf_op jit(solution)/shard_map/ppermute | solution.py:518
  12.8 3.7 %collective-permute-start.2 = (f32[2,8,128]{2,1,0:T(8,128)S(1)}, f32[2,8,128]{2,1,0:T(8,128)S(1)}, u32[]{:S(2)}, u32[]{:S(2)}) collective-permute-start(f32[2,8,128]{2,1,0:T(8,128)S(1)} %half.1.half_ref), channel_id=1, source_target_pairs={{0,1},{1,0},{2,3},{3,2},{4,5},{5,4},{6,7},{7,6},{8,9},{9,8},{10,11... | collective-permute-start | bytes 24584 | tf_op jit(solution)/shard_map/ppermute | solution.py:524
  16.5 7.9 %collective-permute-start.5 = (f32[2,8,128]{2,1,0:T(8,128)S(1)}, f32[2,8,128]{2,1,0:T(8,128)S(1)}, u32[]{:S(2)}, u32[]{:S(2)}) collective-permute-start(f32[2,8,128]{2,1,0:T(8,128)S(1)} %get-tuple-element.54), channel_id=1, source_target_pairs={{0,8},{1,13},{2,10},{3,15},{4,12},{5,9},{6,14},{7,11},{8,0},{9,5},... | collective-permute-start | bytes 24584 | tf_op jit(solution)/shard_map/ppermute | solution.py:537
  24.4 1.2 %collective-permute-start.6 = (f32[2,8,128]{2,1,0:T(8,128)S(1)}, f32[2,8,128]{2,1,0:T(8,128)S(1)}, u32[]{:S(2)}, u32[]{:S(2)}) collective-permute-start(f32[2,8,128]{2,1,0:T(8,128)S(1)} %get-tuple-element.55.refs_0_), channel_id=1, source_target_pairs={{0,1},{1,0},{2,3},{3,2},{4,5},{5,4},{6,7},{7,6},{8,9},{9,8},{10,11... | collective-permute-start | bytes 24584 | tf_op jit(solution)/shard_map/ppermute | solution.py:524
  24.5 1.2 %collective-permute-start.7 = (f32[2,8,128]{2,1,0:T(8,128)S(1)}, f32[2,8,128]{2,1,0:T(8,128)S(1)}, u32[]{:S(2)}, u32[]{:S(2)}) collective-permute-start(f32[2,8,128]{2,1,0:T(8,128)S(1)} %collective-permute-done.5.refs_2_), channel_id=1, source_target_pairs={{0,1},{1,0},{2,3},{3,2},{4,5},{5,4},{6,7},{7,6},{8,9},{9,8},{10,11... | collective-permute-start | bytes 24584 | tf_op jit(solution)/shard_map/ppermute | solution.py:524

commit v5 on v4

--- a/solution.py
+++ b/solution.py
@@ -397,10 +397,10 @@
     tis[0, 3 : 3 + blocks] = wide_ref[rows:count]
     steps.tissue(range(3, 3 + blocks))
     steps.pairs(range(3, 2 + blocks), range(3, 3 + blocks))
-    steps.run([low], rows, 8, steps.prepare(0))
-    steps.run([low + 1], rows - 2, 8, steps.corrections)
-    steps.run([low + 1], rows - 10, 8, steps.distances(APART))
-    steps.run([low + 1], rows - 2, 8, steps.distances(LEVEL))
+    steps.run([low], rows, 16, steps.prepare(0))
+    steps.run([low + 1], rows - 2, 15, steps.corrections)
+    steps.run([low + 1], rows - 10, 11, steps.distances(APART))
+    steps.run([low + 1], rows - 2, 10, steps.distances(LEVEL))
 
 
 def outer_kernel(above_ref, below_ref, *refs):
@@ -431,10 +431,10 @@
         lanes = slice(i * 128, (i + 1) * 128)
         part_ref[i] = above_ref[HALO + 1, :, lanes] + below_ref[HALO + 1, :, lanes]
 
-    steps.run([0, high], HALO, 6, steps.prepare(0))
-    steps.run([1, high - 1], HALO, 6, steps.corrections)
-    steps.run([OUT - 8, high - 9], low + 1 - (OUT - 8), 6, steps.distances(APART))
-    steps.run([OUT, high - 1], low + 1 - OUT, 5, steps.distances(LEVEL))
+    steps.run([0, high], HALO, 18, steps.prepare(0))
+    steps.run([1, high - 1], HALO, 18, steps.corrections)
+    steps.run([OUT - 8, high - 9], low + 1 - (OUT - 8), 9, steps.distances(APART))
+    steps.run([OUT, high - 1], low + 1 - OUT, 10, steps.distances(LEVEL))
 
 
 def smooth_kernel(fars, sums_ref, smoothing_ref, *refs):
@@ -471,14 +471,14 @@
         for t, x in enumerate(ring.plain(new, cols // 128)):
             stage[t, pl.ds(y - HALO, 8, stride=rows), :] = x
 
-    steps.run([OUT - 8], 8, 4, steps.early(factor))
+    steps.run([OUT - 8], 8, 8, steps.early(factor))
     steps.run([OUT], full - 2 * OUT, 5, steps.combine(factor, keep))
 
-    steps.run([OUT], full - 2 * OUT, 10, steps.prepare(4))
-    steps.run([OUT + 1], full - 2 * OUT - 2, 8, steps.corrections)
-    steps.run([low - 8], rows + 8, 8, steps.distances(APART))
+    steps.run([OUT], full - 2 * OUT, 25, steps.prepare(4))
+    steps.run([OUT + 1], full - 2 * OUT - 2, 16, steps.corrections)
+    steps.run([low - 8], rows + 8, 10, steps.distances(APART))
     steps.run([low], rows, 8, steps.distances(LEVEL))
-    steps.run([low - 8], 8, 4, steps.early(factor))
+    steps.run([low - 8], 8, 8, steps.early(factor))
     steps.run([low], rows, 8, steps.combine(factor, finish))
     for t in range(cols // 128):
         out_ref[:, t * 128 : (t + 1) * 128] = stage[t]

time: 34.4 us -> 33.3 us (0.968)
  Pallas kernels: 15 us -> 13.3 us
  waiting for transfers between devices: 3.59 us -> 4.28 us
    pallas_call x1, Pallas kernels: 2.42 us -> 1.73 us  [on_device(): pl.pallas_call(outer_kernel, out_shape=[shape(2, 8, 128)] + state, in_spe...]
    pallas_call x1, Pallas kernels: 8.43 us -> 7.75 us  [on_device(): pl.pallas_call(functools.partial(smooth_kernel, len(far)), out_shape=[sha...]
    pallas_call x1, Pallas kernels: 2.28 us -> 1.87 us  [on_device(): pl.pallas_call(inner_kernel, out_shape=state, in_specs=[vm], out_specs=[v...]
    ppermute x2, waiting for transfers between devices: 2.03 us -> 2.43 us  [line(): lax.ppermute(x, axis, [(i, i + by) for i in range(size) if 0 <= i + by <...]
  transfers between devices with their start and end apart: 8 -> 8, of which waited for: 4 -> 5; matrix products, arithmetic and copies ran while one was open for 0% -> 0% of each run, Pallas kernels for 15% -> 13%
where the time goes in v5:
time: 33.3 us; the launch traced here: 33.1 us
  Pallas kernels  13.3 us (40%)
  starting transfers between devices  13.2 us (40%)
  waiting for transfers between devices  4.28 us (13%)
  local copies, waits for them, and re-layouts  1.64 us (5%)
  between operations  0.73 us (2%)
    pallas_call x1, Pallas kernels, on_device(): pl.pallas_call(functools.partial(smooth_kernel, len(far)), out_shape=[sha...  7.75 us
    ppermute x2, starting transfers between devices, line(): lax.ppermute(x, axis, [(i, i + by) for i in range(size) if 0 <= i + by <...  5.3 us
    ppermute x1, starting transfers between devices, far_rows(): got.append(lax.ppermute(ends if odd is None else x, ('gy', 'gx'), pairs))  3.43 us
    ppermute x2, starting transfers between devices, ring(): return lax.ppermute(x, axis, [(i, (i + by) % size) for i in range(size)])  2.49 us
    ppermute x2, waiting for transfers between devices, line(): lax.ppermute(x, axis, [(i, i + by) for i in range(size) if 0 <= i + by <...  2.43 us
    ppermute x3, starting transfers between devices, swap(): lax.ppermute(x, 'gx', [(c, c ^ 1) for c in range(lax.axis_size('gx'))])  1.96 us
    pallas_call x1, Pallas kernels, on_device(): pl.pallas_call(inner_kernel, out_shape=state, in_specs=[vm], out_specs=[v...  1.87 us
    pallas_call x1, Pallas kernels, on_device(): pl.pallas_call(outer_kernel, out_shape=[shape(2, 8, 128)] + state, in_spe...  1.73 us
  transfers between devices with their start and end apart: 8, of which 5 were waited for; matrix products, arithmetic and copies ran while one was open for 0% of the time, Pallas kernels for 13%

profile of v5, /device:TPU:0, one launch (start us, length us, event | category | flops | bytes accessed | tf_op | source)
XLA Modules:
  0.0 33.1 jit_solution(16992208907763013326)
XLA Ops:
  0.0 0.0 copy-start
  0.0 0.9 %copy-done = f32[8,32,256]{2,1,0:T(8,128)S(1)} copy-done((f32[8,32,256]{2,1,0:T(8,128)S(1)}, f32[8,32,256]{2,1,0:T(8,128)}, u32[]{:S(2)}) %copy-start) | copy-done | bytes 262168
  1.0 0.0 copy-start.1
  1.0 0.7 %copy-done.1 = s32[2,4,32]{2,1,0:T(4,128)S(1)} copy-done((s32[2,4,32]{2,1,0:T(4,128)S(1)}, s32[2,4,32]{2,1,0:T(4,128)}, u32[]{:S(2)}) %copy-start.1) | copy-done | bytes 1048
  1.6 0.3 pack.1
  1.9 0.5 %collective-permute-start = (f32[11,8,128]{2,1,0:T(8,128)S(1)}, f32[11,8,128]{2,1,0:T(8,128)S(1)}, u32[]{:S(2)}, u32[]{:S(2)}) collective-permute-start(f32[11,8,128]{2,1,0:T(8,128)S(1)} %get-tuple-element.34), channel_id=1, source_target_pairs={{0,1},{1,2},{2,3},{3,0},{4,5},{5,6},{6,7},{7,4},{8,9},{9,10},{10,1... | collective-permute-start | bytes 135176 | tf_op jit(solution)/shard_map/ppermute | solution.py:514
  2.4 2.0 %collective-permute-start.1 = (f32[11,8,128]{2,1,0:T(8,128)S(1)}, f32[11,8,128]{2,1,0:T(8,128)S(1)}, u32[]{:S(2)}, u32[]{:S(2)}) collective-permute-start(f32[11,8,128]{2,1,0:T(8,128)S(1)} %get-tuple-element.35), channel_id=1, source_target_pairs={{0,3},{1,0},{2,1},{3,2},{4,7},{5,4},{6,5},{7,6},{8,11},{9,8},{10,9... | collective-permute-start | bytes 135176 | tf_op jit(solution)/shard_map/ppermute | solution.py:514
  4.4 0.6 %order.1.part_ref = f32[36,8,384]{2,1,0:T(8,128)S(1)} custom-call(f32[36,8,256]{2,1,0:T(8,128)S(1)} %get-tuple-element.37.own_ref), custom_call_target="tpu_custom_call" | custom-call | flops 5000000 | bytes 1000000 | tf_op jit(solution)/shard_map/order/pallas_call | solution.py:543
  5.0 1.1 %collective-permute-done.left_ref = f32[11,8,128]{2,1,0:T(8,128)S(1)} collective-permute-done((f32[11,8,128]{2,1,0:T(8,128)S(1)}, f32[11,8,128]{2,1,0:T(8,128)S(1)}, u32[]{:S(2)}, u32[]{:S(2)}) %collective-permute-start) | collective-permute-done | bytes 45088 | tf_op jit(solution)/shard_map/ppermute | solution.py:514
  6.1 0.3 collective-permute-done.1.right_ref
  6.4 1.1 %widen.1 = (f32[36,8,384]{2,1,0:T(8,128)S(1)}, f32[20,8,384]{2,1,0:T(8,128)S(1)}, f32[20,8,384]{2,1,0:T(8,128)S(1)}) custom-call(f32[36,8,384]{2,1,0:T(8,128)S(1)} %order.1.part_ref, f32[11,8,128]{2,1,0:T(8,128)S(1)} %collective-permute-done.left_ref, f32[11,8,128]{2,1,0:T(8,128)S(1)} %collective-permute-done.1.right_ref, ...), custom_call_target="tpu_custom_call", output_to_operand_aliasing={{0}: (0, {})} | custom-call | tf_op jit(solution)/shard_map/widen/pallas_call | solution.py:561
  7.4 4.0 %collective-permute-start.3 = (f32[20,8,384]{2,1,0:T(8,128)S(1)}, f32[20,8,384]{2,1,0:T(8,128)S(1)}, u32[]{:S(2)}, u32[]{:S(2)}) collective-permute-start(f32[20,8,384]{2,1,0:T(8,128)S(1)} %get-tuple-element.46), channel_id=1, source_target_pairs={{0,4},{4,8},{8,12},{1,5},{5,9},{9,13},{2,6},{6,10},{10,14},{3,7},{... | collective-permute-start | bytes 737288 | tf_op jit(solution)/shard_map/ppermute | solution.py:518
  11.5 1.3 %collective-permute-start.4 = (f32[20,8,384]{2,1,0:T(8,128)S(1)}, f32[20,8,384]{2,1,0:T(8,128)S(1)}, u32[]{:S(2)}, u32[]{:S(2)}) collective-permute-start(f32[20,8,384]{2,1,0:T(8,128)S(1)} %get-tuple-element.47), channel_id=1, source_target_pairs={{4,0},{8,4},{12,8},{5,1},{9,5},{13,9},{6,2},{10,6},{14,10},{7,3},{... | collective-permute-start | bytes 737288 | tf_op jit(solution)/shard_map/ppermute | solution.py:518
  12.8 1.4 %collective-permute-start.2 = (f32[2,8,128]{2,1,0:T(8,128)S(1)}, f32[2,8,128]{2,1,0:T(8,128)S(1)}, u32[]{:S(2)}, u32[]{:S(2)}) collective-permute-start(f32[2,8,128]{2,1,0:T(8,128)S(1)} %half.1.half_ref), channel_id=1, source_target_pairs={{0,1},{1,0},{2,3},{3,2},{4,5},{5,4},{6,7},{7,6},{8,9},{9,8},{10,11... | collective-permute-start | bytes 24584 | tf_op jit(solution)/shard_map/ppermute | solution.py:524
  14.1 1.9 %inner.1 = (f32[5,68,8,384]{3,2,1,0:T(8,128)S(1)}, f32[3,68,8,384]{3,2,1,0:T(8,128)S(1)}, f32[9,68,8,384]{3,2,1,0:T(8,128)S(1)}, f32[4,10,8,384]{3,2,1,0:T(8,128)S(1)}, f32[9,10,8,384]{3,2,1,0:T(8,128)S(1)}) custom-call(f32[36,8,384]{2,1,0:T(8,128)S(1)} %get-tuple-element.38.wide_ref), custom_call_target="tpu_custom_call" | custom-call | flops 20000000 | bytes 8000000 | tf_op jit(solution)/shard_map/inner/pallas_call | solution.py:583
  16.0 0.0 collective-permute-done.2.other_ref
  16.1 3.4 %collective-permute-start.5 = (f32[2,8,128]{2,1,0:T(8,128)S(1)}, f32[2,8,128]{2,1,0:T(8,128)S(1)}, u32[]{:S(2)}, u32[]{:S(2)}) collective-permute-start(f32[2,8,128]{2,1,0:T(8,128)S(1)} %get-tuple-element.54), channel_id=1, source_target_pairs={{0,8},{1,13},{2,10},{3,15},{4,12},{5,9},{6,14},{7,11},{8,0},{9,5},... | collective-permute-start | bytes 24584 | tf_op jit(solution)/shard_map/ppermute | solution.py:537
  19.5 0.0 collective-permute-done.3.above_ref
  19.5 2.4 %collective-permute-done.4.below_ref = f32[20,8,384]{2,1,0:T(8,128)S(1)} collective-permute-done((f32[20,8,384]{2,1,0:T(8,128)S(1)}, f32[20,8,384]{2,1,0:T(8,128)S(1)}, u32[]{:S(2)}, u32[]{:S(2)}) %collective-permute-start.4) | collective-permute-done | bytes 245792 | tf_op jit(solution)/shard_map/ppermute | solution.py:518
  21.9 1.7 %outer.1 = (f32[2,8,128]{2,1,0:T(8,128)S(1)}, f32[5,68,8,384]{3,2,1,0:T(8,128)S(1)}, f32[3,68,8,384]{3,2,1,0:T(8,128)S(1)}, f32[9,68,8,384]{3,2,1,0:T(8,128)S(1)...) custom-call(f32[20,8,384]{2,1,0:T(8,128)S(1)} %collective-permute-do, ...), custom_call_target="tpu_custom_call", output_to_operand_aliasing={{1}: (2, {}), {2}: (3, {}), {3}: (4, {}), {4}: (5, {}), {5}... | custom-call | flops 20000000 | bytes 8000000 | tf_op jit(solution)/shard_map/outer/pallas_call | solution.py:602
  23.7 0.0 collective-permute-done.5.refs_2_
  23.7 0.5 %collective-permute-start.6 = (f32[2,8,128]{2,1,0:T(8,128)S(1)}, f32[2,8,128]{2,1,0:T(8,128)S(1)}, u32[]{:S(2)}, u32[]{:S(2)}) collective-permute-start(f32[2,8,128]{2,1,0:T(8,128)S(1)} %get-tuple-element.55.refs_0_), channel_id=1, source_target_pairs={{0,1},{1,0},{2,3},{3,2},{4,5},{5,4},{6,7},{7,6},{8,9},{9,8},{10,11... | collective-permute-start | bytes 24584 | tf_op jit(solution)/shard_map/ppermute | solution.py:524
  24.2 0.1 collective-permute-start.7
  24.9 0.1 collective-permute-done.6.refs_1_
  25.0 0.3 %collective-permute-done.7.refs_3_ = f32[2,8,128]{2,1,0:T(8,128)S(1)} collective-permute-done((f32[2,8,128]{2,1,0:T(8,128)S(1)}, f32[2,8,128]{2,1,0:T(8,128)S(1)}, u32[]{:S(2)}, u32[]{:S(2)}) %collective-permute-start.7) | collective-permute-done | bytes 8224 | tf_op jit(solution)/shard_map/ppermute | solution.py:524
  25.4 7.7 %smooth.1 = (f32[256,256]{1,0:T(8,128)}, f32[5,68,8,384]{3,2,1,0:T(8,128)S(1)}, f32[3,68,8,384]{3,2,1,0:T(8,128)S(1)}, f32[9,68,8,384]{3,2,1,0:T(8,128)S(1)}, f3...) custom-call(f32[2,8,128]{2,1,0:T(8,128)S(1)} %get-tuple-element.45.s, ...), custom_call_target="tpu_custom_call", output_to_operand_aliasing={{1}: (6, {}), {2}: (7, {}), {3}: (8, {}), {4}: (9, {}), {5}... | custom-call | tf_op jit(solution)/shard_map/smooth/pallas_call | solution.py:614
  (2 shorter events, 0.0 us)
Async XLA Ops:
  0.0 0.9 %copy-start = (f32[8,32,256]{2,1,0:T(8,128)S(1)}, f32[8,32,256]{2,1,0:T(8,128)}, u32[]{:S(2)}) copy-start(f32[8,32,256]{2,1,0:T(8,128)} %param.3) | copy-start | bytes 786436
  1.0 0.7 %copy-start.1 = (s32[2,4,32]{2,1,0:T(4,128)S(1)}, s32[2,4,32]{2,1,0:T(4,128)}, u32[]{:S(2)}) copy-start(s32[2,4,32]{2,1,0:T(4,128)} %mask_ref.1) | copy-start | bytes 3076
  1.9 4.2 %collective-permute-start = (f32[11,8,128]{2,1,0:T(8,128)S(1)}, f32[11,8,128]{2,1,0:T(8,128)S(1)}, u32[]{:S(2)}, u32[]{:S(2)}) collective-permute-start(f32[11,8,128]{2,1,0:T(8,128)S(1)} %get-tuple-element.34), channel_id=1, source_target_pairs={{0,1},{1,2},{2,3},{3,0},{4,5},{5,6},{6,7},{7,4},{8,9},{9,10},{10,1... | collective-permute-start | bytes 135176 | tf_op jit(solution)/shard_map/ppermute | solution.py:514
  2.4 4.0 %collective-permute-start.1 = (f32[11,8,128]{2,1,0:T(8,128)S(1)}, f32[11,8,128]{2,1,0:T(8,128)S(1)}, u32[]{:S(2)}, u32[]{:S(2)}) collective-permute-start(f32[11,8,128]{2,1,0:T(8,128)S(1)} %get-tuple-element.35), channel_id=1, source_target_pairs={{0,3},{1,0},{2,1},{3,2},{4,7},{5,4},{6,5},{7,6},{8,11},{9,8},{10,9... | collective-permute-start | bytes 135176 | tf_op jit(solution)/shard_map/ppermute | solution.py:514
  7.4 12.1 %collective-permute-start.3 = (f32[20,8,384]{2,1,0:T(8,128)S(1)}, f32[20,8,384]{2,1,0:T(8,128)S(1)}, u32[]{:S(2)}, u32[]{:S(2)}) collective-permute-start(f32[20,8,384]{2,1,0:T(8,128)S(1)} %get-tuple-element.46), channel_id=1, source_target_pairs={{0,4},{4,8},{8,12},{1,5},{5,9},{9,13},{2,6},{6,10},{10,14},{3,7},{... | collective-permute-start | bytes 737288 | tf_op jit(solution)/shard_map/ppermute | solution.py:518
  11.5 10.5 %collective-permute-start.4 = (f32[20,8,384]{2,1,0:T(8,128)S(1)}, f32[20,8,384]{2,1,0:T(8,128)S(1)}, u32[]{:S(2)}, u32[]{:S(2)}) collective-permute-start(f32[20,8,384]{2,1,0:T(8,128)S(1)} %get-tuple-element.47), channel_id=1, source_target_pairs={{4,0},{8,4},{12,8},{5,1},{9,5},{13,9},{6,2},{10,6},{14,10},{7,3},{... | collective-permute-start | bytes 737288 | tf_op jit(solution)/shard_map/ppermute | solution.py:518
  12.8 3.3 %collective-permute-start.2 = (f32[2,8,128]{2,1,0:T(8,128)S(1)}, f32[2,8,128]{2,1,0:T(8,128)S(1)}, u32[]{:S(2)}, u32[]{:S(2)}) collective-permute-start(f32[2,8,128]{2,1,0:T(8,128)S(1)} %half.1.half_ref), channel_id=1, source_target_pairs={{0,1},{1,0},{2,3},{3,2},{4,5},{5,4},{6,7},{7,6},{8,9},{9,8},{10,11... | collective-permute-start | bytes 24584 | tf_op jit(solution)/shard_map/ppermute | solution.py:524
  16.1 7.6 %collective-permute-start.5 = (f32[2,8,128]{2,1,0:T(8,128)S(1)}, f32[2,8,128]{2,1,0:T(8,128)S(1)}, u32[]{:S(2)}, u32[]{:S(2)}) collective-permute-start(f32[2,8,128]{2,1,0:T(8,128)S(1)} %get-tuple-element.54), channel_id=1, source_target_pairs={{0,8},{1,13},{2,10},{3,15},{4,12},{5,9},{6,14},{7,11},{8,0},{9,5},... | collective-permute-start | bytes 24584 | tf_op jit(solution)/shard_map/ppermute | solution.py:537
  23.7 1.4 %collective-permute-start.6 = (f32[2,8,128]{2,1,0:T(8,128)S(1)}, f32[2,8,128]{2,1,0:T(8,128)S(1)}, u32[]{:S(2)}, u32[]{:S(2)}) collective-permute-start(f32[2,8,128]{2,1,0:T(8,128)S(1)} %get-tuple-element.55.refs_0_), channel_id=1, source_target_pairs={{0,1},{1,0},{2,3},{3,2},{4,5},{5,4},{6,7},{7,6},{8,9},{9,8},{10,11... | collective-permute-start | bytes 24584 | tf_op jit(solution)/shard_map/ppermute | solution.py:524
  24.2 1.2 %collective-permute-start.7 = (f32[2,8,128]{2,1,0:T(8,128)S(1)}, f32[2,8,128]{2,1,0:T(8,128)S(1)}, u32[]{:S(2)}, u32[]{:S(2)}) collective-permute-start(f32[2,8,128]{2,1,0:T(8,128)S(1)} %collective-permute-done.5.refs_2_), channel_id=1, source_target_pairs={{0,1},{1,0},{2,3},{3,2},{4,5},{5,4},{6,7},{7,6},{8,9},{9,8},{10,11... | collective-permute-start | bytes 24584 | tf_op jit(solution)/shard_map/ppermute | solution.py:524

commit v6 on v5

--- a/solution.py
+++ b/solution.py
@@ -146,12 +146,8 @@
             )
 
 
-def whole_kernel(half_ref, other_ref, sums_ref, ends_ref):
-    place, last = lax.axis_index("gy"), lax.axis_size("gy") - 1
-    at_end = ((place == 0) | (place == last)).astype(F32)
-    for i in range(2):
-        sums_ref[i] = half_ref[i] + other_ref[i]
-        ends_ref[i] = sums_ref[i] * jnp.where(lax.rem(lax.axis_index("gx"), 2) == 0, 1.0, at_end)
+def add_kernel(a_ref, b_ref, out_ref):
+    out_ref[...] = a_ref[...] + b_ref[...]
 
 
 def order_kernel(own_ref, wide_ref):
@@ -161,7 +157,7 @@
         put(wide_ref, i, ring.own(split(own_ref, i, tiles)))
 
 
-def widen_kernel(part_ref, left_ref, right_ref, half_ref, wide_ref, top_ref, bottom_ref):
+def widen_kernel(part_ref, left_ref, right_ref, wide_ref, top_ref, bottom_ref):
     tiles = wide_ref.shape[2] // 128
     count = wide_ref.shape[0]
     rows = count - count // 9
@@ -184,7 +180,6 @@
                 some = [v[4 * i : 4 * i + 1] for v in split(wide_ref, block + b, tiles)]
                 packed = [jnp.where(sub == 2 * b + i, x, y) for x, y in zip(some, packed)]
         put(ref, HALO, packed)
-        put(ref, HALO + 1, [half_ref[0], half_ref[1]] + [packed[0]] * (tiles - 2))
 
 
 FIELDS = [(0, 8), (1, -8), (1, 0), (1, 8), (2, 8), (2, 0), (3, -8), (3, 0), (3, 8)]
@@ -404,7 +399,7 @@
 
 
 def outer_kernel(above_ref, below_ref, *refs):
-    part_ref, val, cor, dist, tis, pair = refs[5:]
+    val, cor, dist, tis, pair = refs[5:]
     full = val.shape[1]
     rows = full - 2 * HALO
     spans = tis.shape[1]
@@ -427,10 +422,6 @@
     ends = [*range(0, 3), *range(spans - 3, spans)]
     steps.tissue(ends)
     steps.pairs([*range(0, 3), *range(spans - 4, spans - 1)], ends)
-    for i in range(2):
-        lanes = slice(i * 128, (i + 1) * 128)
-        part_ref[i] = above_ref[HALO + 1, :, lanes] + below_ref[HALO + 1, :, lanes]
-
     steps.run([0, high], HALO, 18, steps.prepare(0))
     steps.run([1, high - 1], HALO, 18, steps.corrections)
     steps.run([OUT - 8, high - 9], low + 1 - (OUT - 8), 9, steps.distances(APART))
@@ -523,20 +514,6 @@
     def swap(x):
         return lax.ppermute(x, "gx", [(c, c ^ 1) for c in range(lax.axis_size("gx"))])
 
-    def far_rows(x, ends):
-        ny, nx = lax.axis_size("gy"), lax.axis_size("gx")
-        shifts = list(range(2, ny - 1)) + [None]
-        got = []
-        for even, odd in zip(shifts[0::2], shifts[1::2]):
-            pairs = []
-            for y in range(ny):
-                for c in range(nx):
-                    by = odd if c % 2 else even
-                    to = ny - 1 - y if by is None else (y + by) % ny
-                    pairs.append((y * nx + c, to * nx + c))
-            got.append(lax.ppermute(ends if odd is None else x, ("gy", "gx"), pairs))
-        return functools.reduce(jnp.add, got)
-
     right = ring(low, "gx", -1)
     left = ring(high, "gx", 1)
     far = [] if lax.axis_size("gx") == 4 else beyond(sums, "gx")
@@ -562,15 +539,15 @@
         widen_kernel,
         out_shape=(
             shape(count, 8, lanes),
-            shape(HALO + 2, 8, lanes),
-            shape(HALO + 2, 8, lanes),
+            shape(HALO + 1, 8, lanes),
+            shape(HALO + 1, 8, lanes),
         ),
-        in_specs=[vm] * 4,
+        in_specs=[vm] * 3,
         out_specs=[vm] * 3,
         input_output_aliases={0: 0},
         compiler_params=params,
         name="widen",
-    )(ordered, left, right, half)
+    )(ordered, left, right)
     below = line(top, "gy", -1)
     above = line(bottom, "gy", 1)
     state = [
@@ -590,27 +567,25 @@
         name="inner",
     )(wide)
     other, *held = lax.optimization_barrier((other, *held))
-    sums, ends = pl.pallas_call(
-        whole_kernel,
-        out_shape=[shape(2, 8, 128)] * 2,
+    sums = pl.pallas_call(
+        add_kernel,
+        out_shape=shape(2, 8, 128),
         in_specs=[vm] * 2,
-        out_specs=[vm] * 2,
-        compiler_params=params,
-        name="whole",
+        out_specs=vm,
+        compiler_params=params,
+        name="add",
     )(half, other)
-    far = far_rows(sums, ends)
-    part, *held = pl.pallas_call(
+    far = [ring(sums, "gy", by) for by in range(1, lax.axis_size("gy"))]
+    held = pl.pallas_call(
         outer_kernel,
-        out_shape=[shape(2, 8, 128)] + state,
+        out_shape=state,
         in_specs=[vm] * 7,
-        out_specs=[vm] * 6,
-        input_output_aliases={2 + i: 1 + i for i in range(5)},
+        out_specs=[vm] * 5,
+        input_output_aliases={2 + i: i for i in range(5)},
         compiler_params=params,
         cost_estimate=pl.CostEstimate(flops=20_000_000, bytes_accessed=8_000_000, transcendentals=0),
         name="outer",
     )(above, below, *held)
-    part, far = lax.optimization_barrier((part, far))
-    far = [part, swap(part), far, swap(far)]
     out = pl.pallas_call(
         functools.partial(smooth_kernel, len(far)),
         out_shape=[shape(depth * rows, cols)] + state,

time: 33.3 us -> 32.8 us (0.985)
  waiting for transfers between devices: 4.28 us -> 1.39 us
  starting transfers between devices: 13.2 us -> 15.5 us
    ppermute x2 -> x5, starting transfers between devices: 2.49 us -> 8.84 us  [ring(): return lax.ppermute(x, axis, [(i, (i + by) % size) for i in range(size)])]
    ppermute x1 -> x0, starting transfers between devices: 3.43 us -> none  [far_rows(): got.append(lax.ppermute(ends if odd is None else x, ('gy', 'gx'), pairs))]
    ppermute x2, waiting for transfers between devices: 2.43 us -> 0.01 us  [line(): lax.ppermute(x, axis, [(i, i + by) for i in range(size) if 0 <= i + by <...]
    ppermute x3 -> x1, starting transfers between devices: 1.96 us -> 1.39 us  [swap(): lax.ppermute(x, 'gx', [(c, c ^ 1) for c in range(lax.axis_size('gx'))])]
    ppermute x3 -> x1, waiting for transfers between devices: 0.47 us -> 0.01 us  [swap(): lax.ppermute(x, 'gx', [(c, c ^ 1) for c in range(lax.axis_size('gx'))])]
    ppermute x2 -> x5, waiting for transfers between devices: 1.38 us -> 1.39 us  [ring(): return lax.ppermute(x, axis, [(i, (i + by) % size) for i in range(size)])]
  transfers between devices with their start and end apart: 8 -> 8, of which waited for: 5 -> 2; matrix products, arithmetic and copies ran while one was open for 0% -> 0% of each run, Pallas kernels for 13% -> 13%
where the time goes in v6:
time: 32.8 us; the launch traced here: 32.6 us
  starting transfers between devices  15.5 us (47%)
  Pallas kernels  13.3 us (41%)
  local copies, waits for them, and re-layouts  1.64 us (5%)
  waiting for transfers between devices  1.39 us (4%)
  between operations  0.77 us (2%)
    ppermute x5, starting transfers between devices, ring(): return lax.ppermute(x, axis, [(i, (i + by) % size) for i in range(size)])  8.84 us
    pallas_call x1, Pallas kernels, on_device(): pl.pallas_call(functools.partial(smooth_kernel, len(far)), out_shape=[sha...  7.75 us
    ppermute x2, starting transfers between devices, line(): lax.ppermute(x, axis, [(i, i + by) for i in range(size) if 0 <= i + by <...  5.3 us
    pallas_call x1, Pallas kernels, on_device(): pl.pallas_call(inner_kernel, out_shape=state, in_specs=[vm], out_specs=[v...  1.87 us
    pallas_call x1, Pallas kernels, on_device(): pl.pallas_call(outer_kernel, out_shape=state, in_specs=[vm] * 7, out_spec...  1.74 us
    unnamed x4, local copies, waits for them, and re-layouts  1.64 us
    ppermute x1, starting transfers between devices, swap(): lax.ppermute(x, 'gx', [(c, c ^ 1) for c in range(lax.axis_size('gx'))])  1.39 us
    ppermute x5, waiting for transfers between devices, ring(): return lax.ppermute(x, axis, [(i, (i + by) % size) for i in range(size)])  1.39 us
  transfers between devices with their start and end apart: 8, of which 2 were waited for; matrix products, arithmetic and copies ran while one was open for 0% of the time, Pallas kernels for 13%

profile of v6, /device:TPU:0, one launch (start us, length us, event | category | flops | bytes accessed | tf_op | source)
XLA Modules:
  0.0 32.6 jit_solution(7511003301516542769)
XLA Ops:
  0.0 0.0 copy-start
  0.0 0.9 %copy-done = f32[8,32,256]{2,1,0:T(8,128)S(1)} copy-done((f32[8,32,256]{2,1,0:T(8,128)S(1)}, f32[8,32,256]{2,1,0:T(8,128)}, u32[]{:S(2)}) %copy-start) | copy-done | bytes 262168
  1.0 0.0 copy-start.1
  1.0 0.7 %copy-done.1 = s32[2,4,32]{2,1,0:T(4,128)S(1)} copy-done((s32[2,4,32]{2,1,0:T(4,128)S(1)}, s32[2,4,32]{2,1,0:T(4,128)}, u32[]{:S(2)}) %copy-start.1) | copy-done | bytes 1048
  1.6 0.3 pack.1
  1.9 0.5 %collective-permute-start = (f32[11,8,128]{2,1,0:T(8,128)S(1)}, f32[11,8,128]{2,1,0:T(8,128)S(1)}, u32[]{:S(2)}, u32[]{:S(2)}) collective-permute-start(f32[11,8,128]{2,1,0:T(8,128)S(1)} %get-tuple-element.29), channel_id=1, source_target_pairs={{0,1},{1,2},{2,3},{3,0},{4,5},{5,6},{6,7},{7,4},{8,9},{9,10},{10,1... | collective-permute-start | bytes 135176 | tf_op jit(solution)/shard_map/ppermute | solution.py:505
  2.4 2.0 %collective-permute-start.1 = (f32[11,8,128]{2,1,0:T(8,128)S(1)}, f32[11,8,128]{2,1,0:T(8,128)S(1)}, u32[]{:S(2)}, u32[]{:S(2)}) collective-permute-start(f32[11,8,128]{2,1,0:T(8,128)S(1)} %get-tuple-element.30), channel_id=1, source_target_pairs={{0,3},{1,0},{2,1},{3,2},{4,7},{5,4},{6,5},{7,6},{8,11},{9,8},{10,9... | collective-permute-start | bytes 135176 | tf_op jit(solution)/shard_map/ppermute | solution.py:505
  4.4 0.6 %order.1.part_ref = f32[36,8,384]{2,1,0:T(8,128)S(1)} custom-call(f32[36,8,256]{2,1,0:T(8,128)S(1)} %get-tuple-element.32.own_ref), custom_call_target="tpu_custom_call" | custom-call | flops 5000000 | bytes 1000000 | tf_op jit(solution)/shard_map/order/pallas_call | solution.py:520
  5.0 1.1 %collective-permute-done.left_ref = f32[11,8,128]{2,1,0:T(8,128)S(1)} collective-permute-done((f32[11,8,128]{2,1,0:T(8,128)S(1)}, f32[11,8,128]{2,1,0:T(8,128)S(1)}, u32[]{:S(2)}, u32[]{:S(2)}) %collective-permute-start) | collective-permute-done | bytes 45088 | tf_op jit(solution)/shard_map/ppermute | solution.py:505
  6.1 0.3 collective-permute-done.1.right_ref
  6.4 1.1 %widen.1 = (f32[36,8,384]{2,1,0:T(8,128)S(1)}, f32[19,8,384]{2,1,0:T(8,128)S(1)}, f32[19,8,384]{2,1,0:T(8,128)S(1)}) custom-call(f32[36,8,384]{2,1,0:T(8,128)S(1)} %order.1.part_ref, f32[11,8,128]{2,1,0:T(8,128)S(1)} %collective-permute-done.left_ref, f32[11,8,128]{2,1,0:T(8,128)S(1)} %collective-permute-done.1.right_ref), custom_call_target="tpu_custom_call", output_to_operand_aliasing={{0}: (0, {})} | custom-call | tf_op jit(solution)/shard_map/widen/pallas_call | solution.py:538
  7.4 4.0 %collective-permute-start.6 = (f32[19,8,384]{2,1,0:T(8,128)S(1)}, f32[19,8,384]{2,1,0:T(8,128)S(1)}, u32[]{:S(2)}, u32[]{:S(2)}) collective-permute-start(f32[19,8,384]{2,1,0:T(8,128)S(1)} %get-tuple-element.40), channel_id=1, source_target_pairs={{0,4},{4,8},{8,12},{1,5},{5,9},{9,13},{2,6},{6,10},{10,14},{3,7},{... | collective-permute-start | bytes 700424 | tf_op jit(solution)/shard_map/ppermute | solution.py:509
  11.4 1.3 %collective-permute-start.7 = (f32[19,8,384]{2,1,0:T(8,128)S(1)}, f32[19,8,384]{2,1,0:T(8,128)S(1)}, u32[]{:S(2)}, u32[]{:S(2)}) collective-permute-start(f32[19,8,384]{2,1,0:T(8,128)S(1)} %get-tuple-element.41), channel_id=1, source_target_pairs={{4,0},{8,4},{12,8},{5,1},{9,5},{13,9},{6,2},{10,6},{14,10},{7,3},{... | collective-permute-start | bytes 700424 | tf_op jit(solution)/shard_map/ppermute | solution.py:509
  12.8 1.4 %collective-permute-start.2 = (f32[2,8,128]{2,1,0:T(8,128)S(1)}, f32[2,8,128]{2,1,0:T(8,128)S(1)}, u32[]{:S(2)}, u32[]{:S(2)}) collective-permute-start(f32[2,8,128]{2,1,0:T(8,128)S(1)} %half.1.a_ref), channel_id=1, source_target_pairs={{0,1},{1,0},{2,3},{3,2},{4,5},{5,4},{6,7},{7,6},{8,9},{9,8},{10,11... | collective-permute-start | bytes 24584 | tf_op jit(solution)/shard_map/ppermute | solution.py:515
  14.2 1.9 %inner.1 = (f32[5,68,8,384]{3,2,1,0:T(8,128)S(1)}, f32[3,68,8,384]{3,2,1,0:T(8,128)S(1)}, f32[9,68,8,384]{3,2,1,0:T(8,128)S(1)}, f32[4,10,8,384]{3,2,1,0:T(8,128)S(1)}, f32[9,10,8,384]{3,2,1,0:T(8,128)S(1)}) custom-call(f32[36,8,384]{2,1,0:T(8,128)S(1)} %get-tuple-element.33.wide_ref), custom_call_target="tpu_custom_call" | custom-call | flops 20000000 | bytes 8000000 | tf_op jit(solution)/shard_map/inner/pallas_call | solution.py:560
  16.0 0.0 collective-permute-done.2.b_ref
  16.1 2.4 %collective-permute-start.3 = (f32[2,8,128]{2,1,0:T(8,128)S(1)}, f32[2,8,128]{2,1,0:T(8,128)S(1)}, u32[]{:S(2)}, u32[]{:S(2)}) collective-permute-start(f32[2,8,128]{2,1,0:T(8,128)S(1)} %add.1.sums_ref), channel_id=1, source_target_pairs={{0,4},{4,8},{8,12},{12,0},{1,5},{5,9},{9,13},{13,1},{2,6},{6,10},{... | collective-permute-start | bytes 24584 | tf_op jit(solution)/shard_map/ppermute | solution.py:505
  18.5 2.6 %collective-permute-start.4 = (f32[2,8,128]{2,1,0:T(8,128)S(1)}, f32[2,8,128]{2,1,0:T(8,128)S(1)}, u32[]{:S(2)}, u32[]{:S(2)}) collective-permute-start(f32[2,8,128]{2,1,0:T(8,128)S(1)} %add.1.sums_ref), channel_id=1, source_target_pairs={{0,8},{4,12},{8,0},{12,4},{1,9},{5,13},{9,1},{13,5},{2,10},{6,14},... | collective-permute-start | bytes 24584 | tf_op jit(solution)/shard_map/ppermute | solution.py:505
  21.1 1.3 %collective-permute-start.5 = (f32[2,8,128]{2,1,0:T(8,128)S(1)}, f32[2,8,128]{2,1,0:T(8,128)S(1)}, u32[]{:S(2)}, u32[]{:S(2)}) collective-permute-start(f32[2,8,128]{2,1,0:T(8,128)S(1)} %add.1.sums_ref), channel_id=1, source_target_pairs={{0,12},{4,0},{8,4},{12,8},{1,13},{5,1},{9,5},{13,9},{2,14},{6,2},{... | collective-permute-start | bytes 24584 | tf_op jit(solution)/shard_map/ppermute | solution.py:505
  23.1 0.0 collective-permute-done.6.above_ref
  23.1 0.0 collective-permute-done.7.below_ref
  23.1 1.7 %outer.1 = (f32[5,68,8,384]{3,2,1,0:T(8,128)S(1)}, f32[3,68,8,384]{3,2,1,0:T(8,128)S(1)}, f32[9,68,8,384]{3,2,1,0:T(8,128)S(1)}, f32[4,10,8,384]{3,2,1,0:T(8,128)S(1)}, f32[9,10,8,384]{3,2,1,0:T(8,128)S(1)}) custom-call(f32[19,8,384]{2,1,0:T(8,128)S(1)} %collective-permute-done.6.above, ...), custom_call_target="tpu_custom_call", output_to_operand_aliasing={{0}: (2, {}), {1}: (3, {}), {2}: (4, {}), {3}: (5, {}), {4}... | custom-call | flops 20000000 | bytes 8000000 | tf_op jit(solution)/shard_map/outer/pallas_call | solution.py:579
  24.8 0.0 collective-permute-done.3.refs_0_
  24.8 0.0 collective-permute-done.4.refs_1_
  24.8 0.0 collective-permute-done.5.refs_2_
  24.8 7.8 %smooth.1 = (f32[256,256]{1,0:T(8,128)}, f32[5,68,8,384]{3,2,1,0:T(8,128)S(1)}, f32[3,68,8,384]{3,2,1,0:T(8,128)S(1)}, f32[9,68,8,384]{3,2,1,0:T(8,128)S(1)}, f3...) custom-call(f32[2,8,128]{2,1,0:T(8,128)S(1)} %add.1.sums_ref, ...), custom_call_target="tpu_custom_call", output_to_operand_aliasing={{1}: (5, {}), {2}: (6, {}), {3}: (7, {}), {4}: (8, {}), {5}... | custom-call | tf_op jit(solution)/shard_map/smooth/pallas_call | solution.py:589
  (2 shorter events, 0.0 us)
Async XLA Ops:
  0.0 0.9 %copy-start = (f32[8,32,256]{2,1,0:T(8,128)S(1)}, f32[8,32,256]{2,1,0:T(8,128)}, u32[]{:S(2)}) copy-start(f32[8,32,256]{2,1,0:T(8,128)} %param.3) | copy-start | bytes 786436
  1.0 0.7 %copy-start.1 = (s32[2,4,32]{2,1,0:T(4,128)S(1)}, s32[2,4,32]{2,1,0:T(4,128)}, u32[]{:S(2)}) copy-start(s32[2,4,32]{2,1,0:T(4,128)} %mask_ref.1) | copy-start | bytes 3076
  1.9 4.2 %collective-permute-start = (f32[11,8,128]{2,1,0:T(8,128)S(1)}, f32[11,8,128]{2,1,0:T(8,128)S(1)}, u32[]{:S(2)}, u32[]{:S(2)}) collective-permute-start(f32[11,8,128]{2,1,0:T(8,128)S(1)} %get-tuple-element.29), channel_id=1, source_target_pairs={{0,1},{1,2},{2,3},{3,0},{4,5},{5,6},{6,7},{7,4},{8,9},{9,10},{10,1... | collective-permute-start | bytes 135176 | tf_op jit(solution)/shard_map/ppermute | solution.py:505
  2.4 4.0 %collective-permute-start.1 = (f32[11,8,128]{2,1,0:T(8,128)S(1)}, f32[11,8,128]{2,1,0:T(8,128)S(1)}, u32[]{:S(2)}, u32[]{:S(2)}) collective-permute-start(f32[11,8,128]{2,1,0:T(8,128)S(1)} %get-tuple-element.30), channel_id=1, source_target_pairs={{0,3},{1,0},{2,1},{3,2},{4,7},{5,4},{6,5},{7,6},{8,11},{9,8},{10,9... | collective-permute-start | bytes 135176 | tf_op jit(solution)/shard_map/ppermute | solution.py:505
  7.4 15.6 %collective-permute-start.6 = (f32[19,8,384]{2,1,0:T(8,128)S(1)}, f32[19,8,384]{2,1,0:T(8,128)S(1)}, u32[]{:S(2)}, u32[]{:S(2)}) collective-permute-start(f32[19,8,384]{2,1,0:T(8,128)S(1)} %get-tuple-element.40), channel_id=1, source_target_pairs={{0,4},{4,8},{8,12},{1,5},{5,9},{9,13},{2,6},{6,10},{10,14},{3,7},{... | collective-permute-start | bytes 700424 | tf_op jit(solution)/shard_map/ppermute | solution.py:509
  11.4 11.6 %collective-permute-start.7 = (f32[19,8,384]{2,1,0:T(8,128)S(1)}, f32[19,8,384]{2,1,0:T(8,128)S(1)}, u32[]{:S(2)}, u32[]{:S(2)}) collective-permute-start(f32[19,8,384]{2,1,0:T(8,128)S(1)} %get-tuple-element.41), channel_id=1, source_target_pairs={{4,0},{8,4},{12,8},{5,1},{9,5},{13,9},{6,2},{10,6},{14,10},{7,3},{... | collective-permute-start | bytes 700424 | tf_op jit(solution)/shard_map/ppermute | solution.py:509
  12.8 3.3 %collective-permute-start.2 = (f32[2,8,128]{2,1,0:T(8,128)S(1)}, f32[2,8,128]{2,1,0:T(8,128)S(1)}, u32[]{:S(2)}, u32[]{:S(2)}) collective-permute-start(f32[2,8,128]{2,1,0:T(8,128)S(1)} %half.1.a_ref), channel_id=1, source_target_pairs={{0,1},{1,0},{2,3},{3,2},{4,5},{5,4},{6,7},{7,6},{8,9},{9,8},{10,11... | collective-permute-start | bytes 24584 | tf_op jit(solution)/shard_map/ppermute | solution.py:515
  16.1 8.8 %collective-permute-start.3 = (f32[2,8,128]{2,1,0:T(8,128)S(1)}, f32[2,8,128]{2,1,0:T(8,128)S(1)}, u32[]{:S(2)}, u32[]{:S(2)}) collective-permute-start(f32[2,8,128]{2,1,0:T(8,128)S(1)} %add.1.sums_ref), channel_id=1, source_target_pairs={{0,4},{4,8},{8,12},{12,0},{1,5},{5,9},{9,13},{13,1},{2,6},{6,10},{... | collective-permute-start | bytes 24584 | tf_op jit(solution)/shard_map/ppermute | solution.py:505
  18.5 6.4 %collective-permute-start.4 = (f32[2,8,128]{2,1,0:T(8,128)S(1)}, f32[2,8,128]{2,1,0:T(8,128)S(1)}, u32[]{:S(2)}, u32[]{:S(2)}) collective-permute-start(f32[2,8,128]{2,1,0:T(8,128)S(1)} %add.1.sums_ref), channel_id=1, source_target_pairs={{0,8},{4,12},{8,0},{12,4},{1,9},{5,13},{9,1},{13,5},{2,10},{6,14},... | collective-permute-start | bytes 24584 | tf_op jit(solution)/shard_map/ppermute | solution.py:505
  21.1 3.8 %collective-permute-start.5 = (f32[2,8,128]{2,1,0:T(8,128)S(1)}, f32[2,8,128]{2,1,0:T(8,128)S(1)}, u32[]{:S(2)}, u32[]{:S(2)}) collective-permute-start(f32[2,8,128]{2,1,0:T(8,128)S(1)} %add.1.sums_ref), channel_id=1, source_target_pairs={{0,12},{4,0},{8,4},{12,8},{1,13},{5,1},{9,5},{13,9},{2,14},{6,2},{... | collective-permute-start | bytes 24584 | tf_op jit(solution)/shard_map/ppermute | solution.py:505

commit v7 on v6

--- a/solution.py
+++ b/solution.py
@@ -82,7 +82,17 @@
         ref[row, :, t * 128 : (t + 1) * 128] = v
 
 
-def pack_kernel(vol_ref, mask_ref, own_ref, low_ref, high_ref, sums_ref, stage):
+def odd_place():
+    return lax.rem(lax.axis_index("gx"), 2)
+
+
+def sides(core, chip):
+    even = odd_place() == 0
+    return jnp.where(even, chip, core), jnp.where(even, core, chip)
+
+
+def pack_kernel(vol_ref, mask_ref, own_ref, core_ref, chip_ref, sums_ref, stage):
+    even = odd_place() == 0
     cols = own_ref.shape[2]
     rows = own_ref.shape[0] - mask_ref.shape[1]
     blocks = mask_ref.shape[1]
@@ -126,23 +136,22 @@
             high = jnp.where(
                 group == g, lane_roll(own_ref[4 * k + g, :, cols - 128 : cols], 32 * (g + 1)), high
             )
-        low_ref[k] = low
-        high_ref[k] = high
-    for ref in (low_ref, high_ref):
+        core_ref[k] = jnp.where(even, high, low)
+        chip_ref[k] = jnp.where(even, low, high)
+    for ref in (core_ref, chip_ref):
         ref[packs] = total
         ref[packs + 1] = count
 
 
-def half_kernel(left_ref, right_ref, own_ref, *refs):
-    packs = left_ref.shape[0] - 2
-    odd = lax.rem(lax.axis_index("gx"), 2).astype(F32)
+def half_kernel(core_ref, chip_ref, own_ref, *refs):
+    packs = core_ref.shape[0] - 2
     for i in range(2):
-        left, right = left_ref[packs + i], right_ref[packs + i]
+        beyond = own_ref[i] + chip_ref[packs + i]
         if len(refs) == 1:
-            refs[-1][i] = own_ref[i] + left * (1.0 - odd) + right * odd
+            refs[-1][i] = beyond
         else:
             refs[-1][i] = 0.5 * functools.reduce(
-                jnp.add, [ref[i] for ref in refs[:-1]], own_ref[i] + left + right
+                jnp.add, [ref[i] for ref in refs[:-1]], beyond + core_ref[packs + i]
             )
 
 
@@ -157,7 +166,7 @@
         put(wide_ref, i, ring.own(split(own_ref, i, tiles)))
 
 
-def widen_kernel(part_ref, left_ref, right_ref, wide_ref, top_ref, bottom_ref):
+def widen_kernel(part_ref, core_ref, chip_ref, wide_ref, top_ref, bottom_ref):
     tiles = wide_ref.shape[2] // 128
     count = wide_ref.shape[0]
     rows = count - count // 9
@@ -166,8 +175,8 @@
     has_left = (place > 0).astype(F32)
     has_right = (place < lax.axis_size("gx") - 1).astype(F32)
     for k in range(count // 4):
-        left = left_ref[k] * has_left
-        right = right_ref[k] * has_right
+        left, right = sides(core_ref[k], chip_ref[k])
+        left, right = left * has_left, right * has_right
         for g in range(4):
             i = 4 * k + g
             put(wide_ref, i, ring.edges(split(part_ref, i, tiles), ring.unpacked(left, right, g)))
@@ -485,7 +494,7 @@
     vm = pl.BlockSpec(memory_space=VMEM)
     shape = lambda *s: jax.ShapeDtypeStruct(s, F32)
     params = pltpu.CompilerParams(vmem_limit_bytes=32 * 1024 * 1024)
-    own, low, high, sums = pl.pallas_call(
+    own, core, chip, sums = pl.pallas_call(
         pack_kernel,
         out_shape=(
             shape(count, 8, cols),
@@ -514,8 +523,9 @@
     def swap(x):
         return lax.ppermute(x, "gx", [(c, c ^ 1) for c in range(lax.axis_size("gx"))])
 
-    right = ring(low, "gx", -1)
-    left = ring(high, "gx", 1)
+    size = lax.axis_size("gx")
+    chip = lax.ppermute(chip, "gx", [(i, (i + (1 if i % 2 else -1)) % size) for i in range(size)])
+    core = swap(core)
     far = [] if lax.axis_size("gx") == 4 else beyond(sums, "gx")
     ordered = pl.pallas_call(
         order_kernel,
@@ -533,7 +543,7 @@
         out_specs=vm,
         compiler_params=params,
         name="half",
-    )(left, right, sums, *far)
+    )(core, chip, sums, *far)
     other = swap(half)
     wide, top, bottom = pl.pallas_call(
         widen_kernel,
@@ -547,7 +557,7 @@
         input_output_aliases={0: 0},
         compiler_params=params,
         name="widen",
-    )(ordered, left, right)
+    )(ordered, core, chip)
     below = line(top, "gy", -1)
     above = line(bottom, "gy", 1)
     state = [

time: 32.8 us -> 31.9 us (0.973)
  starting transfers between devices: 15.5 us -> 14.6 us
    ppermute x0 -> x1, starting transfers between devices: none -> 2.61 us  [on_device(): lax.ppermute(chip, 'gx', [(i, (i + (1 if i % 2 else -1)) % size) for i in...]
    ppermute x5 -> x3, starting transfers between devices: 8.84 us -> 6.47 us  [ring(): return lax.ppermute(x, axis, [(i, (i + by) % size) for i in range(size)])]
    ppermute x5 -> x3, waiting for transfers between devices: 1.39 us -> 0.01 us  [ring(): return lax.ppermute(x, axis, [(i, (i + by) % size) for i in range(size)])]
    ppermute x0 -> x1, waiting for transfers between devices: none -> 1.33 us  [on_device(): lax.ppermute(chip, 'gx', [(i, (i + (1 if i % 2 else -1)) % size) for i in...]
    ppermute x1 -> x2, starting transfers between devices: 1.39 us -> 0.75 us  [swap(): lax.ppermute(x, 'gx', [(c, c ^ 1) for c in range(lax.axis_size('gx'))])]
    ppermute x2, starting transfers between devices: 5.3 us -> 4.78 us  [line(): lax.ppermute(x, axis, [(i, i + by) for i in range(size) if 0 <= i + by <...]
  transfers between devices with their start and end apart: 8 -> 8, of which waited for: 2 -> 1; matrix products, arithmetic and copies ran while one was open for 0% -> 0% of each run, Pallas kernels for 13% -> 13%
where the time goes in v7:
time: 31.9 us; the launch traced here: 31.7 us
  starting transfers between devices  14.6 us (46%)
  Pallas kernels  13.3 us (42%)
  local copies, waits for them, and re-layouts  1.64 us (5%)
  waiting for transfers between devices  1.35 us (4%)
  between operations  0.77 us (2%)
    pallas_call x1, Pallas kernels, on_device(): pl.pallas_call(functools.partial(smooth_kernel, len(far)), out_shape=[sha...  7.75 us
    ppermute x3, starting transfers between devices, ring(): return lax.ppermute(x, axis, [(i, (i + by) % size) for i in range(size)])  6.47 us
    ppermute x2, starting transfers between devices, line(): lax.ppermute(x, axis, [(i, i + by) for i in range(size) if 0 <= i + by <...  4.78 us
    ppermute x1, starting transfers between devices, on_device(): lax.ppermute(chip, 'gx', [(i, (i + (1 if i % 2 else -1)) % size) for i in...  2.61 us
    pallas_call x1, Pallas kernels, on_device(): pl.pallas_call(inner_kernel, out_shape=state, in_specs=[vm], out_specs=[v...  1.87 us
    pallas_call x1, Pallas kernels, on_device(): pl.pallas_call(outer_kernel, out_shape=state, in_specs=[vm] * 7, out_spec...  1.74 us
    unnamed x4, local copies, waits for them, and re-layouts  1.64 us
    ppermute x1, waiting for transfers between devices, on_device(): lax.ppermute(chip, 'gx', [(i, (i + (1 if i % 2 else -1)) % size) for i in...  1.33 us
  transfers between devices with their start and end apart: 8, of which 1 were waited for; matrix products, arithmetic and copies ran while one was open for 0% of the time, Pallas kernels for 13%

profile of v7, /device:TPU:0, one launch (start us, length us, event | category | flops | bytes accessed | tf_op | source)
XLA Modules:
  0.0 31.7 jit_solution(13255497360949769898)
XLA Ops:
  0.0 0.0 copy-start
  0.0 0.9 %copy-done = f32[8,32,256]{2,1,0:T(8,128)S(1)} copy-done((f32[8,32,256]{2,1,0:T(8,128)S(1)}, f32[8,32,256]{2,1,0:T(8,128)}, u32[]{:S(2)}) %copy-start) | copy-done | bytes 262168
  1.0 0.0 copy-start.1
  1.0 0.7 %copy-done.1 = s32[2,4,32]{2,1,0:T(4,128)S(1)} copy-done((s32[2,4,32]{2,1,0:T(4,128)S(1)}, s32[2,4,32]{2,1,0:T(4,128)}, u32[]{:S(2)}) %copy-start.1) | copy-done | bytes 1048
  1.6 0.3 pack.1
  1.9 0.5 %collective-permute-start = (f32[11,8,128]{2,1,0:T(8,128)S(1)}, f32[11,8,128]{2,1,0:T(8,128)S(1)}, u32[]{:S(2)}, u32[]{:S(2)}) collective-permute-start(f32[11,8,128]{2,1,0:T(8,128)S(1)} %get-tuple-element.29), channel_id=1, source_target_pairs={{0,1},{1,0},{2,3},{3,2},{4,5},{5,4},{6,7},{7,6},{8,9},{9,8},{10,11... | collective-permute-start | bytes 135176 | tf_op jit(solution)/shard_map/ppermute | solution.py:524
  2.4 2.6 %collective-permute-start.1 = (f32[11,8,128]{2,1,0:T(8,128)S(1)}, f32[11,8,128]{2,1,0:T(8,128)S(1)}, u32[]{:S(2)}, u32[]{:S(2)}) collective-permute-start(f32[11,8,128]{2,1,0:T(8,128)S(1)} %get-tuple-element.30), channel_id=1, source_target_pairs={{0,3},{1,2},{2,1},{3,0},{4,7},{5,6},{6,5},{7,4},{8,11},{9,10},{10,... | collective-permute-start | bytes 135176 | tf_op jit(solution)/shard_map/ppermute | solution.py:527
  5.0 0.6 %order.1.part_ref = f32[36,8,384]{2,1,0:T(8,128)S(1)} custom-call(f32[36,8,256]{2,1,0:T(8,128)S(1)} %get-tuple-element.32.own_ref), custom_call_target="tpu_custom_call" | custom-call | flops 5000000 | bytes 1000000 | tf_op jit(solution)/shard_map/order/pallas_call | solution.py:530
  5.6 0.0 collective-permute-done.core_ref
  5.6 1.3 %collective-permute-done.1.chip_ref = f32[11,8,128]{2,1,0:T(8,128)S(1)} collective-permute-done((f32[11,8,128]{2,1,0:T(8,128)S(1)}, f32[11,8,128]{2,1,0:T(8,128)S(1)}, u32[]{:S(2)}, u32[]{:S(2)}) %collective-permute-start.1) | collective-permute-done | bytes 45088 | tf_op jit(solution)/shard_map/ppermute | solution.py:527
  7.0 1.1 %widen.1 = (f32[36,8,384]{2,1,0:T(8,128)S(1)}, f32[19,8,384]{2,1,0:T(8,128)S(1)}, f32[19,8,384]{2,1,0:T(8,128)S(1)}) custom-call(f32[36,8,384]{2,1,0:T(8,128)S(1)} %order.1.part_ref, f32[11,8,128]{2,1,0:T(8,128)S(1)} %collective-permute-done.core_ref, f32[11,8,128]{2,1,0:T(8,128)S(1)} %collective-permute-done.1.chip_ref), custom_call_target="tpu_custom_call", output_to_operand_aliasing={{0}: (0, {})} | custom-call | tf_op jit(solution)/shard_map/widen/pallas_call | solution.py:548
  8.0 3.5 %collective-permute-start.6 = (f32[19,8,384]{2,1,0:T(8,128)S(1)}, f32[19,8,384]{2,1,0:T(8,128)S(1)}, u32[]{:S(2)}, u32[]{:S(2)}) collective-permute-start(f32[19,8,384]{2,1,0:T(8,128)S(1)} %get-tuple-element.40), channel_id=1, source_target_pairs={{0,4},{4,8},{8,12},{1,5},{5,9},{9,13},{2,6},{6,10},{10,14},{3,7},{... | collective-permute-start | bytes 700424 | tf_op jit(solution)/shard_map/ppermute | solution.py:518
  11.5 1.3 %collective-permute-start.7 = (f32[19,8,384]{2,1,0:T(8,128)S(1)}, f32[19,8,384]{2,1,0:T(8,128)S(1)}, u32[]{:S(2)}, u32[]{:S(2)}) collective-permute-start(f32[19,8,384]{2,1,0:T(8,128)S(1)} %get-tuple-element.41), channel_id=1, source_target_pairs={{4,0},{8,4},{12,8},{5,1},{9,5},{13,9},{6,2},{10,6},{14,10},{7,3},{... | collective-permute-start | bytes 700424 | tf_op jit(solution)/shard_map/ppermute | solution.py:518
  12.8 0.2 collective-permute-start.2
  13.1 1.9 %inner.1 = (f32[5,68,8,384]{3,2,1,0:T(8,128)S(1)}, f32[3,68,8,384]{3,2,1,0:T(8,128)S(1)}, f32[9,68,8,384]{3,2,1,0:T(8,128)S(1)}, f32[4,10,8,384]{3,2,1,0:T(8,128)S(1)}, f32[9,10,8,384]{3,2,1,0:T(8,128)S(1)}) custom-call(f32[36,8,384]{2,1,0:T(8,128)S(1)} %get-tuple-element.33.wide_ref), custom_call_target="tpu_custom_call" | custom-call | flops 20000000 | bytes 8000000 | tf_op jit(solution)/shard_map/inner/pallas_call | solution.py:570
  15.0 0.0 collective-permute-done.2.b_ref
  15.0 2.5 %collective-permute-start.3 = (f32[2,8,128]{2,1,0:T(8,128)S(1)}, f32[2,8,128]{2,1,0:T(8,128)S(1)}, u32[]{:S(2)}, u32[]{:S(2)}) collective-permute-start(f32[2,8,128]{2,1,0:T(8,128)S(1)} %add.1.sums_ref), channel_id=1, source_target_pairs={{0,4},{4,8},{8,12},{12,0},{1,5},{5,9},{9,13},{13,1},{2,6},{6,10},{... | collective-permute-start | bytes 24584 | tf_op jit(solution)/shard_map/ppermute | solution.py:514
  17.5 2.6 %collective-permute-start.4 = (f32[2,8,128]{2,1,0:T(8,128)S(1)}, f32[2,8,128]{2,1,0:T(8,128)S(1)}, u32[]{:S(2)}, u32[]{:S(2)}) collective-permute-start(f32[2,8,128]{2,1,0:T(8,128)S(1)} %add.1.sums_ref), channel_id=1, source_target_pairs={{0,8},{4,12},{8,0},{12,4},{1,9},{5,13},{9,1},{13,5},{2,10},{6,14},... | collective-permute-start | bytes 24584 | tf_op jit(solution)/shard_map/ppermute | solution.py:514
  20.1 1.3 %collective-permute-start.5 = (f32[2,8,128]{2,1,0:T(8,128)S(1)}, f32[2,8,128]{2,1,0:T(8,128)S(1)}, u32[]{:S(2)}, u32[]{:S(2)}) collective-permute-start(f32[2,8,128]{2,1,0:T(8,128)S(1)} %add.1.sums_ref), channel_id=1, source_target_pairs={{0,12},{4,0},{8,4},{12,8},{1,13},{5,1},{9,5},{13,9},{2,14},{6,2},{... | collective-permute-start | bytes 24584 | tf_op jit(solution)/shard_map/ppermute | solution.py:514
  22.1 0.0 collective-permute-done.6.above_ref
  22.1 0.0 collective-permute-done.7.below_ref
  22.1 1.7 %outer.1 = (f32[5,68,8,384]{3,2,1,0:T(8,128)S(1)}, f32[3,68,8,384]{3,2,1,0:T(8,128)S(1)}, f32[9,68,8,384]{3,2,1,0:T(8,128)S(1)}, f32[4,10,8,384]{3,2,1,0:T(8,128)S(1)}, f32[9,10,8,384]{3,2,1,0:T(8,128)S(1)}) custom-call(f32[19,8,384]{2,1,0:T(8,128)S(1)} %collective-permute-done.6.above, ...), custom_call_target="tpu_custom_call", output_to_operand_aliasing={{0}: (2, {}), {1}: (3, {}), {2}: (4, {}), {3}: (5, {}), {4}... | custom-call | flops 20000000 | bytes 8000000 | tf_op jit(solution)/shard_map/outer/pallas_call | solution.py:589
  23.9 0.0 collective-permute-done.3.refs_0_
  23.9 0.0 collective-permute-done.4.refs_1_
  23.9 0.0 collective-permute-done.5.refs_2_
  23.9 7.8 %smooth.1 = (f32[256,256]{1,0:T(8,128)}, f32[5,68,8,384]{3,2,1,0:T(8,128)S(1)}, f32[3,68,8,384]{3,2,1,0:T(8,128)S(1)}, f32[9,68,8,384]{3,2,1,0:T(8,128)S(1)}, f3...) custom-call(f32[2,8,128]{2,1,0:T(8,128)S(1)} %add.1.sums_ref, ...), custom_call_target="tpu_custom_call", output_to_operand_aliasing={{1}: (5, {}), {2}: (6, {}), {3}: (7, {}), {4}: (8, {}), {5}... | custom-call | tf_op jit(solution)/shard_map/smooth/pallas_call | solution.py:599
  (2 shorter events, 0.0 us)
Async XLA Ops:
  0.0 0.9 %copy-start = (f32[8,32,256]{2,1,0:T(8,128)S(1)}, f32[8,32,256]{2,1,0:T(8,128)}, u32[]{:S(2)}) copy-start(f32[8,32,256]{2,1,0:T(8,128)} %param.3) | copy-start | bytes 786436
  1.0 0.7 %copy-start.1 = (s32[2,4,32]{2,1,0:T(4,128)S(1)}, s32[2,4,32]{2,1,0:T(4,128)}, u32[]{:S(2)}) copy-start(s32[2,4,32]{2,1,0:T(4,128)} %mask_ref.1) | copy-start | bytes 3076
  1.9 3.7 %collective-permute-start = (f32[11,8,128]{2,1,0:T(8,128)S(1)}, f32[11,8,128]{2,1,0:T(8,128)S(1)}, u32[]{:S(2)}, u32[]{:S(2)}) collective-permute-start(f32[11,8,128]{2,1,0:T(8,128)S(1)} %get-tuple-element.29), channel_id=1, source_target_pairs={{0,1},{1,0},{2,3},{3,2},{4,5},{5,4},{6,7},{7,6},{8,9},{9,8},{10,11... | collective-permute-start | bytes 135176 | tf_op jit(solution)/shard_map/ppermute | solution.py:524
  2.4 4.5 %collective-permute-start.1 = (f32[11,8,128]{2,1,0:T(8,128)S(1)}, f32[11,8,128]{2,1,0:T(8,128)S(1)}, u32[]{:S(2)}, u32[]{:S(2)}) collective-permute-start(f32[11,8,128]{2,1,0:T(8,128)S(1)} %get-tuple-element.30), channel_id=1, source_target_pairs={{0,3},{1,2},{2,1},{3,0},{4,7},{5,6},{6,5},{7,4},{8,11},{9,10},{10,... | collective-permute-start | bytes 135176 | tf_op jit(solution)/shard_map/ppermute | solution.py:527
  8.0 14.1 %collective-permute-start.6 = (f32[19,8,384]{2,1,0:T(8,128)S(1)}, f32[19,8,384]{2,1,0:T(8,128)S(1)}, u32[]{:S(2)}, u32[]{:S(2)}) collective-permute-start(f32[19,8,384]{2,1,0:T(8,128)S(1)} %get-tuple-element.40), channel_id=1, source_target_pairs={{0,4},{4,8},{8,12},{1,5},{5,9},{9,13},{2,6},{6,10},{10,14},{3,7},{... | collective-permute-start | bytes 700424 | tf_op jit(solution)/shard_map/ppermute | solution.py:518
  11.5 10.6 %collective-permute-start.7 = (f32[19,8,384]{2,1,0:T(8,128)S(1)}, f32[19,8,384]{2,1,0:T(8,128)S(1)}, u32[]{:S(2)}, u32[]{:S(2)}) collective-permute-start(f32[19,8,384]{2,1,0:T(8,128)S(1)} %get-tuple-element.41), channel_id=1, source_target_pairs={{4,0},{8,4},{12,8},{5,1},{9,5},{13,9},{6,2},{10,6},{14,10},{7,3},{... | collective-permute-start | bytes 700424 | tf_op jit(solution)/shard_map/ppermute | solution.py:518
  12.8 2.1 %collective-permute-start.2 = (f32[2,8,128]{2,1,0:T(8,128)S(1)}, f32[2,8,128]{2,1,0:T(8,128)S(1)}, u32[]{:S(2)}, u32[]{:S(2)}) collective-permute-start(f32[2,8,128]{2,1,0:T(8,128)S(1)} %half.1.a_ref), channel_id=1, source_target_pairs={{0,1},{1,0},{2,3},{3,2},{4,5},{5,4},{6,7},{7,6},{8,9},{9,8},{10,11... | collective-permute-start | bytes 24584 | tf_op jit(solution)/shard_map/ppermute | solution.py:524
  15.0 8.9 %collective-permute-start.3 = (f32[2,8,128]{2,1,0:T(8,128)S(1)}, f32[2,8,128]{2,1,0:T(8,128)S(1)}, u32[]{:S(2)}, u32[]{:S(2)}) collective-permute-start(f32[2,8,128]{2,1,0:T(8,128)S(1)} %add.1.sums_ref), channel_id=1, source_target_pairs={{0,4},{4,8},{8,12},{12,0},{1,5},{5,9},{9,13},{13,1},{2,6},{6,10},{... | collective-permute-start | bytes 24584 | tf_op jit(solution)/shard_map/ppermute | solution.py:514
  17.5 6.4 %collective-permute-start.4 = (f32[2,8,128]{2,1,0:T(8,128)S(1)}, f32[2,8,128]{2,1,0:T(8,128)S(1)}, u32[]{:S(2)}, u32[]{:S(2)}) collective-permute-start(f32[2,8,128]{2,1,0:T(8,128)S(1)} %add.1.sums_ref), channel_id=1, source_target_pairs={{0,8},{4,12},{8,0},{12,4},{1,9},{5,13},{9,1},{13,5},{2,10},{6,14},... | collective-permute-start | bytes 24584 | tf_op jit(solution)/shard_map/ppermute | solution.py:514
  20.1 3.8 %collective-permute-start.5 = (f32[2,8,128]{2,1,0:T(8,128)S(1)}, f32[2,8,128]{2,1,0:T(8,128)S(1)}, u32[]{:S(2)}, u32[]{:S(2)}) collective-permute-start(f32[2,8,128]{2,1,0:T(8,128)S(1)} %add.1.sums_ref), channel_id=1, source_target_pairs={{0,12},{4,0},{8,4},{12,8},{1,13},{5,1},{9,5},{13,9},{2,14},{6,2},{... | collective-permute-start | bytes 24584 | tf_op jit(solution)/shard_map/ppermute | solution.py:514

commit v8 on v7

--- a/solution.py
+++ b/solution.py
@@ -475,9 +475,9 @@
     steps.run([OUT], full - 2 * OUT, 5, steps.combine(factor, keep))
 
     steps.run([OUT], full - 2 * OUT, 25, steps.prepare(4))
-    steps.run([OUT + 1], full - 2 * OUT - 2, 16, steps.corrections)
+    steps.run([OUT + 1], full - 2 * OUT - 2, 24, steps.corrections)
     steps.run([low - 8], rows + 8, 10, steps.distances(APART))
-    steps.run([low], rows, 8, steps.distances(LEVEL))
+    steps.run([low], rows, 16, steps.distances(LEVEL))
     steps.run([low - 8], 8, 8, steps.early(factor))
     steps.run([low], rows, 8, steps.combine(factor, finish))
     for t in range(cols // 128):

time: 31.9 us -> 31.7 us (level)
  no operation moved by 1% of the time
where the time goes in v8:
time: 31.7 us; the launch traced here: 31.5 us
  starting transfers between devices  14.6 us (46%)
  Pallas kernels  13.1 us (41%)
  local copies, waits for them, and re-layouts  1.64 us (5%)
  waiting for transfers between devices  1.35 us (4%)
  between operations  0.77 us (2%)
    pallas_call x1, Pallas kernels, on_device(): pl.pallas_call(functools.partial(smooth_kernel, len(far)), out_shape=[sha...  7.58 us
    ppermute x3, starting transfers between devices, ring(): return lax.ppermute(x, axis, [(i, (i + by) % size) for i in range(size)])  6.47 us
    ppermute x2, starting transfers between devices, line(): lax.ppermute(x, axis, [(i, i + by) for i in range(size) if 0 <= i + by <...  4.78 us
    ppermute x1, starting transfers between devices, on_device(): lax.ppermute(chip, 'gx', [(i, (i + (1 if i % 2 else -1)) % size) for i in...  2.61 us
    pallas_call x1, Pallas kernels, on_device(): pl.pallas_call(inner_kernel, out_shape=state, in_specs=[vm], out_specs=[v...  1.87 us
    pallas_call x1, Pallas kernels, on_device(): pl.pallas_call(outer_kernel, out_shape=state, in_specs=[vm] * 7, out_spec...  1.74 us
    unnamed x4, local copies, waits for them, and re-layouts  1.64 us
    ppermute x1, waiting for transfers between devices, on_device(): lax.ppermute(chip, 'gx', [(i, (i + (1 if i % 2 else -1)) % size) for i in...  1.33 us
  transfers between devices with their start and end apart: 8, of which 1 were waited for; matrix products, arithmetic and copies ran while one was open for 0% of the time, Pallas kernels for 13%

profile of v8, /device:TPU:0, one launch (start us, length us, event | category | flops | bytes accessed | tf_op | source)
XLA Modules:
  0.0 31.5 jit_solution(17772912475268264587)
XLA Ops:
  0.0 0.0 copy-start
  0.0 0.9 %copy-done = f32[8,32,256]{2,1,0:T(8,128)S(1)} copy-done((f32[8,32,256]{2,1,0:T(8,128)S(1)}, f32[8,32,256]{2,1,0:T(8,128)}, u32[]{:S(2)}) %copy-start) | copy-done | bytes 262168
  1.0 0.0 copy-start.1
  1.0 0.7 %copy-done.1 = s32[2,4,32]{2,1,0:T(4,128)S(1)} copy-done((s32[2,4,32]{2,1,0:T(4,128)S(1)}, s32[2,4,32]{2,1,0:T(4,128)}, u32[]{:S(2)}) %copy-start.1) | copy-done | bytes 1048
  1.6 0.3 pack.1
  1.9 0.5 %collective-permute-start = (f32[11,8,128]{2,1,0:T(8,128)S(1)}, f32[11,8,128]{2,1,0:T(8,128)S(1)}, u32[]{:S(2)}, u32[]{:S(2)}) collective-permute-start(f32[11,8,128]{2,1,0:T(8,128)S(1)} %get-tuple-element.29), channel_id=1, source_target_pairs={{0,1},{1,0},{2,3},{3,2},{4,5},{5,4},{6,7},{7,6},{8,9},{9,8},{10,11... | collective-permute-start | bytes 135176 | tf_op jit(solution)/shard_map/ppermute | solution.py:524
  2.4 2.6 %collective-permute-start.1 = (f32[11,8,128]{2,1,0:T(8,128)S(1)}, f32[11,8,128]{2,1,0:T(8,128)S(1)}, u32[]{:S(2)}, u32[]{:S(2)}) collective-permute-start(f32[11,8,128]{2,1,0:T(8,128)S(1)} %get-tuple-element.30), channel_id=1, source_target_pairs={{0,3},{1,2},{2,1},{3,0},{4,7},{5,6},{6,5},{7,4},{8,11},{9,10},{10,... | collective-permute-start | bytes 135176 | tf_op jit(solution)/shard_map/ppermute | solution.py:527
  5.0 0.6 %order.1.part_ref = f32[36,8,384]{2,1,0:T(8,128)S(1)} custom-call(f32[36,8,256]{2,1,0:T(8,128)S(1)} %get-tuple-element.32.own_ref), custom_call_target="tpu_custom_call" | custom-call | flops 5000000 | bytes 1000000 | tf_op jit(solution)/shard_map/order/pallas_call | solution.py:530
  5.6 0.0 collective-permute-done.core_ref
  5.6 1.3 %collective-permute-done.1.chip_ref = f32[11,8,128]{2,1,0:T(8,128)S(1)} collective-permute-done((f32[11,8,128]{2,1,0:T(8,128)S(1)}, f32[11,8,128]{2,1,0:T(8,128)S(1)}, u32[]{:S(2)}, u32[]{:S(2)}) %collective-permute-start.1) | collective-permute-done | bytes 45088 | tf_op jit(solution)/shard_map/ppermute | solution.py:527
  7.0 1.1 %widen.1 = (f32[36,8,384]{2,1,0:T(8,128)S(1)}, f32[19,8,384]{2,1,0:T(8,128)S(1)}, f32[19,8,384]{2,1,0:T(8,128)S(1)}) custom-call(f32[36,8,384]{2,1,0:T(8,128)S(1)} %order.1.part_ref, f32[11,8,128]{2,1,0:T(8,128)S(1)} %collective-permute-done.core_ref, f32[11,8,128]{2,1,0:T(8,128)S(1)} %collective-permute-done.1.chip_ref), custom_call_target="tpu_custom_call", output_to_operand_aliasing={{0}: (0, {})} | custom-call | tf_op jit(solution)/shard_map/widen/pallas_call | solution.py:548
  8.0 3.5 %collective-permute-start.6 = (f32[19,8,384]{2,1,0:T(8,128)S(1)}, f32[19,8,384]{2,1,0:T(8,128)S(1)}, u32[]{:S(2)}, u32[]{:S(2)}) collective-permute-start(f32[19,8,384]{2,1,0:T(8,128)S(1)} %get-tuple-element.40), channel_id=1, source_target_pairs={{0,4},{4,8},{8,12},{1,5},{5,9},{9,13},{2,6},{6,10},{10,14},{3,7},{... | collective-permute-start | bytes 700424 | tf_op jit(solution)/shard_map/ppermute | solution.py:518
  11.5 1.3 %collective-permute-start.7 = (f32[19,8,384]{2,1,0:T(8,128)S(1)}, f32[19,8,384]{2,1,0:T(8,128)S(1)}, u32[]{:S(2)}, u32[]{:S(2)}) collective-permute-start(f32[19,8,384]{2,1,0:T(8,128)S(1)} %get-tuple-element.41), channel_id=1, source_target_pairs={{4,0},{8,4},{12,8},{5,1},{9,5},{13,9},{6,2},{10,6},{14,10},{7,3},{... | collective-permute-start | bytes 700424 | tf_op jit(solution)/shard_map/ppermute | solution.py:518
  12.8 0.2 collective-permute-start.2
  13.1 1.9 %inner.1 = (f32[5,68,8,384]{3,2,1,0:T(8,128)S(1)}, f32[3,68,8,384]{3,2,1,0:T(8,128)S(1)}, f32[9,68,8,384]{3,2,1,0:T(8,128)S(1)}, f32[4,10,8,384]{3,2,1,0:T(8,128)S(1)}, f32[9,10,8,384]{3,2,1,0:T(8,128)S(1)}) custom-call(f32[36,8,384]{2,1,0:T(8,128)S(1)} %get-tuple-element.33.wide_ref), custom_call_target="tpu_custom_call" | custom-call | flops 20000000 | bytes 8000000 | tf_op jit(solution)/shard_map/inner/pallas_call | solution.py:570
  15.0 0.0 collective-permute-done.2.b_ref
  15.0 2.5 %collective-permute-start.3 = (f32[2,8,128]{2,1,0:T(8,128)S(1)}, f32[2,8,128]{2,1,0:T(8,128)S(1)}, u32[]{:S(2)}, u32[]{:S(2)}) collective-permute-start(f32[2,8,128]{2,1,0:T(8,128)S(1)} %add.1.sums_ref), channel_id=1, source_target_pairs={{0,4},{4,8},{8,12},{12,0},{1,5},{5,9},{9,13},{13,1},{2,6},{6,10},{... | collective-permute-start | bytes 24584 | tf_op jit(solution)/shard_map/ppermute | solution.py:514
  17.5 2.6 %collective-permute-start.4 = (f32[2,8,128]{2,1,0:T(8,128)S(1)}, f32[2,8,128]{2,1,0:T(8,128)S(1)}, u32[]{:S(2)}, u32[]{:S(2)}) collective-permute-start(f32[2,8,128]{2,1,0:T(8,128)S(1)} %add.1.sums_ref), channel_id=1, source_target_pairs={{0,8},{4,12},{8,0},{12,4},{1,9},{5,13},{9,1},{13,5},{2,10},{6,14},... | collective-permute-start | bytes 24584 | tf_op jit(solution)/shard_map/ppermute | solution.py:514
  20.1 1.3 %collective-permute-start.5 = (f32[2,8,128]{2,1,0:T(8,128)S(1)}, f32[2,8,128]{2,1,0:T(8,128)S(1)}, u32[]{:S(2)}, u32[]{:S(2)}) collective-permute-start(f32[2,8,128]{2,1,0:T(8,128)S(1)} %add.1.sums_ref), channel_id=1, source_target_pairs={{0,12},{4,0},{8,4},{12,8},{1,13},{5,1},{9,5},{13,9},{2,14},{6,2},{... | collective-permute-start | bytes 24584 | tf_op jit(solution)/shard_map/ppermute | solution.py:514
  22.1 0.0 collective-permute-done.6.above_ref
  22.1 0.0 collective-permute-done.7.below_ref
  22.1 1.7 %outer.1 = (f32[5,68,8,384]{3,2,1,0:T(8,128)S(1)}, f32[3,68,8,384]{3,2,1,0:T(8,128)S(1)}, f32[9,68,8,384]{3,2,1,0:T(8,128)S(1)}, f32[4,10,8,384]{3,2,1,0:T(8,128)S(1)}, f32[9,10,8,384]{3,2,1,0:T(8,128)S(1)}) custom-call(f32[19,8,384]{2,1,0:T(8,128)S(1)} %collective-permute-done.6.above, ...), custom_call_target="tpu_custom_call", output_to_operand_aliasing={{0}: (2, {}), {1}: (3, {}), {2}: (4, {}), {3}: (5, {}), {4}... | custom-call | flops 20000000 | bytes 8000000 | tf_op jit(solution)/shard_map/outer/pallas_call | solution.py:589
  23.9 0.0 collective-permute-done.3.refs_0_
  23.9 0.0 collective-permute-done.4.refs_1_
  23.9 0.0 collective-permute-done.5.refs_2_
  23.9 7.6 %smooth.1 = (f32[256,256]{1,0:T(8,128)}, f32[5,68,8,384]{3,2,1,0:T(8,128)S(1)}, f32[3,68,8,384]{3,2,1,0:T(8,128)S(1)}, f32[9,68,8,384]{3,2,1,0:T(8,128)S(1)}, f3...) custom-call(f32[2,8,128]{2,1,0:T(8,128)S(1)} %add.1.sums_ref, ...), custom_call_target="tpu_custom_call", output_to_operand_aliasing={{1}: (5, {}), {2}: (6, {}), {3}: (7, {}), {4}: (8, {}), {5}... | custom-call | tf_op jit(solution)/shard_map/smooth/pallas_call | solution.py:599
  (2 shorter events, 0.0 us)
Async XLA Ops:
  0.0 0.9 %copy-start = (f32[8,32,256]{2,1,0:T(8,128)S(1)}, f32[8,32,256]{2,1,0:T(8,128)}, u32[]{:S(2)}) copy-start(f32[8,32,256]{2,1,0:T(8,128)} %param.3) | copy-start | bytes 786436
  1.0 0.7 %copy-start.1 = (s32[2,4,32]{2,1,0:T(4,128)S(1)}, s32[2,4,32]{2,1,0:T(4,128)}, u32[]{:S(2)}) copy-start(s32[2,4,32]{2,1,0:T(4,128)} %mask_ref.1) | copy-start | bytes 3076
  1.9 3.7 %collective-permute-start = (f32[11,8,128]{2,1,0:T(8,128)S(1)}, f32[11,8,128]{2,1,0:T(8,128)S(1)}, u32[]{:S(2)}, u32[]{:S(2)}) collective-permute-start(f32[11,8,128]{2,1,0:T(8,128)S(1)} %get-tuple-element.29), channel_id=1, source_target_pairs={{0,1},{1,0},{2,3},{3,2},{4,5},{5,4},{6,7},{7,6},{8,9},{9,8},{10,11... | collective-permute-start | bytes 135176 | tf_op jit(solution)/shard_map/ppermute | solution.py:524
  2.4 4.5 %collective-permute-start.1 = (f32[11,8,128]{2,1,0:T(8,128)S(1)}, f32[11,8,128]{2,1,0:T(8,128)S(1)}, u32[]{:S(2)}, u32[]{:S(2)}) collective-permute-start(f32[11,8,128]{2,1,0:T(8,128)S(1)} %get-tuple-element.30), channel_id=1, source_target_pairs={{0,3},{1,2},{2,1},{3,0},{4,7},{5,6},{6,5},{7,4},{8,11},{9,10},{10,... | collective-permute-start | bytes 135176 | tf_op jit(solution)/shard_map/ppermute | solution.py:527
  8.0 14.1 %collective-permute-start.6 = (f32[19,8,384]{2,1,0:T(8,128)S(1)}, f32[19,8,384]{2,1,0:T(8,128)S(1)}, u32[]{:S(2)}, u32[]{:S(2)}) collective-permute-start(f32[19,8,384]{2,1,0:T(8,128)S(1)} %get-tuple-element.40), channel_id=1, source_target_pairs={{0,4},{4,8},{8,12},{1,5},{5,9},{9,13},{2,6},{6,10},{10,14},{3,7},{... | collective-permute-start | bytes 700424 | tf_op jit(solution)/shard_map/ppermute | solution.py:518
  11.5 10.6 %collective-permute-start.7 = (f32[19,8,384]{2,1,0:T(8,128)S(1)}, f32[19,8,384]{2,1,0:T(8,128)S(1)}, u32[]{:S(2)}, u32[]{:S(2)}) collective-permute-start(f32[19,8,384]{2,1,0:T(8,128)S(1)} %get-tuple-element.41), channel_id=1, source_target_pairs={{4,0},{8,4},{12,8},{5,1},{9,5},{13,9},{6,2},{10,6},{14,10},{7,3},{... | collective-permute-start | bytes 700424 | tf_op jit(solution)/shard_map/ppermute | solution.py:518
  12.8 2.1 %collective-permute-start.2 = (f32[2,8,128]{2,1,0:T(8,128)S(1)}, f32[2,8,128]{2,1,0:T(8,128)S(1)}, u32[]{:S(2)}, u32[]{:S(2)}) collective-permute-start(f32[2,8,128]{2,1,0:T(8,128)S(1)} %half.1.a_ref), channel_id=1, source_target_pairs={{0,1},{1,0},{2,3},{3,2},{4,5},{5,4},{6,7},{7,6},{8,9},{9,8},{10,11... | collective-permute-start | bytes 24584 | tf_op jit(solution)/shard_map/ppermute | solution.py:524
  15.0 8.9 %collective-permute-start.3 = (f32[2,8,128]{2,1,0:T(8,128)S(1)}, f32[2,8,128]{2,1,0:T(8,128)S(1)}, u32[]{:S(2)}, u32[]{:S(2)}) collective-permute-start(f32[2,8,128]{2,1,0:T(8,128)S(1)} %add.1.sums_ref), channel_id=1, source_target_pairs={{0,4},{4,8},{8,12},{12,0},{1,5},{5,9},{9,13},{13,1},{2,6},{6,10},{... | collective-permute-start | bytes 24584 | tf_op jit(solution)/shard_map/ppermute | solution.py:514
  17.5 6.4 %collective-permute-start.4 = (f32[2,8,128]{2,1,0:T(8,128)S(1)}, f32[2,8,128]{2,1,0:T(8,128)S(1)}, u32[]{:S(2)}, u32[]{:S(2)}) collective-permute-start(f32[2,8,128]{2,1,0:T(8,128)S(1)} %add.1.sums_ref), channel_id=1, source_target_pairs={{0,8},{4,12},{8,0},{12,4},{1,9},{5,13},{9,1},{13,5},{2,10},{6,14},... | collective-permute-start | bytes 24584 | tf_op jit(solution)/shard_map/ppermute | solution.py:514
  20.1 3.8 %collective-permute-start.5 = (f32[2,8,128]{2,1,0:T(8,128)S(1)}, f32[2,8,128]{2,1,0:T(8,128)S(1)}, u32[]{:S(2)}, u32[]{:S(2)}) collective-permute-start(f32[2,8,128]{2,1,0:T(8,128)S(1)} %add.1.sums_ref), channel_id=1, source_target_pairs={{0,12},{4,0},{8,4},{12,8},{1,13},{5,1},{9,5},{13,9},{2,14},{6,2},{... | collective-permute-start | bytes 24584 | tf_op jit(solution)/shard_map/ppermute | solution.py:514
